TPU v7x, 128 devices: a whole 4x4x4 slice. The times are simulated.
128 devices in a mesh: dp: 32 (over y_hi, x, z), seq: 4 (over y_lo, core).
Axes of the slice: x: 4, y: 4 (y_hi: 2, y_lo: 2; y = y_hi * 2 + y_lo), z: 4, core: 2. Of those that a mesh axis runs over, the one named last changes fastest.
Arguments:
- layer_in: bfloat16 [16384, 1024], P(('dp', 'seq')), may hold values from -6 to 6
- norm_one: bfloat16 [1024], P('dp'), may hold values from 0.099609375 to 1.8984375
- w_query: bfloat16 [1024, 1024], P('dp'), may hold values from -0.625 to 0.625
- key_weight: bfloat16 [1024, 512], P('dp'), may hold values from -0.625 to 0.625
- value_weight: bfloat16 [1024, 512], P('dp'), may hold values from -0.1875 to 0.1875
- w_output: bfloat16 [1024, 1024], P('dp'), may hold values from -4 to 4
- norm_two: bfloat16 [1024], P('dp'), may hold values from 0.099609375 to 1.8984375
- w_gate: bfloat16 [1024, 16, 512], P('dp'), may hold values from -0.1875 to 0.1875
- w_up: bfloat16 [1024, 16, 512], P('dp'), may hold values from -0.1875 to 0.1875
- w_down: bfloat16 [1024, 16, 512], P('dp'), may hold values from -1 to 1
- routes: int32 [16384, 8], P(('dp', 'seq')), may hold values from 0 to 15, all different within a row; in each aligned block of 128 rows (0 to 127, 128 to 255, ...) at most 72 rows name the same one
- route_gates: float32 [16384, 8], P(('dp', 'seq')), may hold values from 0.5 to 1.5
- cotangent: bfloat16 [16384, 1024], P(('dp', 'seq')), may hold values from -6 to 6
Outputs:
- layer_out: bfloat16 [16384, 1024], P(('dp', 'seq'))
- grad_input: bfloat16 [16384, 1024], P(('dp', 'seq'))
- grad_norm_one: float32 [1024], P('dp')
- grad_query_proj: float32 [1024, 1024], P('dp')
- grad_key_proj: float32 [1024, 512], P('dp')
- grad_value_proj: float32 [1024, 512], P('dp')
- grad_output_proj: float32 [1024, 1024], P('dp')
- grad_norm_two: float32 [1024], P('dp')
- grad_gate_proj: float32 [1024, 16, 512], P('dp')
- grad_up_proj: float32 [1024, 16, 512], P('dp')
- grad_down_proj: float32 [1024, 16, 512], P('dp')
- grad_gates: float32 [16384, 8], P(('dp', 'seq'))
Inputs may be any that keep to these rules, and one draw needn't show every extreme that they name: `routes`: each row names 8 different experts. In the 128 rows of one device no expert is named by more than 72 rows, a bound that some block reaches of some device in every draw.
All inputs are finite; a program needn't handle non-finite values.
Results may differ from a plain program's by a relative error of at most 0.03.
Values may be sent and summed in bfloat16 or wider, within the bound.
A program may use at most 256 MiB of HBM per device.

v0:
```python
import jax
import jax.numpy as jnp
from jax import lax
from jax.sharding import PartitionSpec as P

MODEL_WIDTH = 1024
QUERY_HEADS = 16
KEY_VALUE_HEADS = 8
HEAD_SIZE = 64
TOP = 8
EXPERTS = 16
BLOCK = 512


EPSILON = 1e-05
RESIDUAL = 0.22
ROPE_BASE = 10000.0
MASK_VALUE = -1e30


def angles(start, count, head_dim):
    freqs = ROPE_BASE ** (-jnp.arange(0, head_dim, 2).astype(jnp.float32) / head_dim)
    places = (start + jnp.arange(count, dtype=jnp.int32)).astype(jnp.float32)
    turns = places[:, None] * freqs[None, :]
    turns = jnp.concatenate([turns, turns], axis=-1)
    return (jnp.cos(turns)[:, None, :], jnp.sin(turns)[:, None, :])


def apply_rotary(value_matrix, cosine_table, sine_table):
    half_dim = value_matrix.shape[-1] // 2
    turned = jnp.concatenate([-value_matrix[..., half_dim:], value_matrix[..., :half_dim]], axis=-1)
    return value_matrix * cosine_table + turned * sine_table


def unrotate(value_matrix, cosine_table, sine_table):
    half_dim = value_matrix.shape[-1] // 2
    turned = jnp.concatenate([-value_matrix[..., half_dim:], value_matrix[..., :half_dim]], axis=-1)
    return value_matrix * cosine_table - turned * sine_table


def slot_tables(routes, experts, capacity, top_count):
    chosen = routes.reshape(-1)
    onehot = (chosen[:, None] == jnp.arange(experts, dtype=jnp.int32)[None, :]).astype(jnp.int32)
    ranks = jnp.sum(onehot * (jnp.cumsum(onehot, axis=0) - 1), axis=1)
    slots = chosen * capacity + ranks
    serial = jnp.arange(chosen.shape[0], dtype=jnp.int32)
    sources = jnp.zeros((experts * capacity,), jnp.int32).at[slots].set(serial)
    filled = jnp.zeros((experts * capacity,), jnp.float32).at[slots].set(1.0)
    return (slots, sources // top_count, sources, filled)


def masked_scores(query_block, key_rows, first_row):
    scores = (
        jnp.einsum("qkgd,skd->kgqs", query_block, key_rows, preferred_element_type=jnp.float32)
        / query_block.shape[-1]
    )
    row_places = first_row + jnp.arange(query_block.shape[0])
    causal = row_places[:, None] >= jnp.arange(key_rows.shape[0])[None, :]
    return jnp.where(causal, scores, MASK_VALUE)


def norm_back(grad_normed, value_matrix, factor, gain):
    scaled = grad_normed * gain
    mean_term = jnp.mean(scaled * value_matrix, axis=-1, keepdims=True)
    grad_values = factor * scaled - value_matrix * factor * factor * factor * mean_term
    grad_gain = jnp.sum(grad_normed * value_matrix * factor, axis=0)
    return (grad_values, grad_gain)


def shards(
    layer_in,
    norm_one,
    w_query,
    key_weight,
    value_weight,
    w_output,
    norm_two,
    w_gate,
    w_up,
    w_down,
    routes,
    route_gates,
    cotangent,
):
    sequence_count = lax.axis_size("seq")
    tokens_resident = layer_in.shape[0]
    sequence_length = tokens_resident * sequence_count
    key_value_resident = KEY_VALUE_HEADS // sequence_count
    group_width = QUERY_HEADS // KEY_VALUE_HEADS
    head_width = key_value_resident * group_width * HEAD_SIZE
    capacity = tokens_resident * TOP * 9 // (8 * EXPERTS)
    gathered = (
        lax.all_gather(norm_one, "dp", axis=0, tiled=True),
        lax.all_gather(w_query, "dp", axis=0, tiled=True),
        lax.all_gather(key_weight, "dp", axis=0, tiled=True),
        lax.all_gather(value_weight, "dp", axis=0, tiled=True),
        lax.all_gather(w_output, "dp", axis=0, tiled=True),
        lax.all_gather(norm_two, "dp", axis=0, tiled=True),
    )
    gain_first = gathered[0].astype(jnp.float32)
    query_w = gathered[1]
    key_w = gathered[2]
    value_w = gathered[3]
    output_w = gathered[4]
    gain_second = gathered[5].astype(jnp.float32)
    inputs = layer_in.astype(jnp.float32)
    factor_one = lax.rsqrt(jnp.mean(inputs * inputs, axis=-1, keepdims=True) + EPSILON)
    normed_input = (inputs * factor_one * gain_first).astype(jnp.bfloat16)
    cosine_table, sine_table = angles(
        lax.axis_index("seq") * tokens_resident, tokens_resident, HEAD_SIZE
    )
    query_pre = jnp.dot(normed_input, query_w, preferred_element_type=jnp.float32).reshape(
        tokens_resident, QUERY_HEADS, HEAD_SIZE
    )
    query_rot = (
        apply_rotary(query_pre, cosine_table, sine_table)
        .reshape(tokens_resident, QUERY_HEADS * HEAD_SIZE)
        .astype(jnp.bfloat16)
    )
    key_before_rotary = jnp.dot(normed_input, key_w, preferred_element_type=jnp.float32).reshape(
        tokens_resident, KEY_VALUE_HEADS, HEAD_SIZE
    )
    key_rotated = (
        apply_rotary(key_before_rotary, cosine_table, sine_table)
        .reshape(tokens_resident, KEY_VALUE_HEADS * HEAD_SIZE)
        .astype(jnp.bfloat16)
    )
    value_tok = jnp.dot(normed_input, value_w, preferred_element_type=jnp.float32).astype(
        jnp.bfloat16
    )
    query_heads, key_heads, value_heads = (
        lax.all_to_all(query_rot, "seq", split_axis=1, concat_axis=0, tiled=True),
        lax.all_to_all(key_rotated, "seq", split_axis=1, concat_axis=0, tiled=True),
        lax.all_to_all(value_tok, "seq", split_axis=1, concat_axis=0, tiled=True),
    )
    query_all = query_heads.reshape(sequence_length, key_value_resident, group_width, HEAD_SIZE)
    key_all = key_heads.reshape(sequence_length, key_value_resident, HEAD_SIZE)
    value_all = value_heads.reshape(sequence_length, key_value_resident, HEAD_SIZE)
    block_index = 0
    first_row = block_index * BLOCK
    scores = masked_scores(query_all, key_all, first_row)
    top_score = jnp.max(scores, axis=-1, keepdims=True)
    exponent = jnp.exp(scores - top_score)
    total_mass = jnp.sum(exponent, axis=-1, keepdims=True)
    probs = (exponent / total_mass).astype(jnp.bfloat16)
    log_sums = [top_score + jnp.log(total_mass)]
    attended = jnp.einsum("kgqs,skd->qkgd", probs, value_all, preferred_element_type=jnp.float32)
    attended_parts = attended.reshape(BLOCK, head_width).astype(jnp.bfloat16)
    attended_tok = lax.all_to_all(attended_parts, "seq", split_axis=0, concat_axis=1, tiled=True)
    branch = jnp.dot(attended_tok, output_w, preferred_element_type=jnp.float32)
    middle = inputs + RESIDUAL * branch
    factor_two = lax.rsqrt(jnp.mean(middle * middle, axis=-1, keepdims=True) + EPSILON)
    normed_two = (middle * factor_two * gain_second).astype(jnp.bfloat16)
    slots, owners, sources, filled = slot_tables(routes, EXPERTS, capacity, TOP)
    expert_inputs = normed_two[owners].reshape(EXPERTS, capacity, MODEL_WIDTH)
    expert_w = (
        lax.all_gather(w_gate, "dp", axis=0, tiled=True),
        lax.all_gather(w_up, "dp", axis=0, tiled=True),
        lax.all_gather(w_down, "dp", axis=0, tiled=True),
    )
    gate_pre = jnp.einsum(
        "ecd,def->ecf", expert_inputs, expert_w[0], preferred_element_type=jnp.float32
    )
    up_pre = jnp.einsum(
        "ecd,def->ecf", expert_inputs, expert_w[1], preferred_element_type=jnp.float32
    )
    active = (jax.nn.silu(gate_pre) * up_pre).astype(jnp.bfloat16)
    returned = jnp.einsum(
        "ecf,def->ecd", active, expert_w[2], preferred_element_type=jnp.float32
    ).reshape(EXPERTS * capacity, MODEL_WIDTH)
    picked = returned[slots].reshape(tokens_resident, TOP, MODEL_WIDTH)
    layer_out = (middle + RESIDUAL * jnp.sum(route_gates[:, :, None] * picked, axis=1)).astype(
        jnp.bfloat16
    )
    grad_out = cotangent.astype(jnp.float32)
    grad_gates = RESIDUAL * jnp.sum(grad_out[:, None, :] * picked, axis=-1)
    grad_pairs = (RESIDUAL * route_gates[:, :, None] * grad_out[:, None, :]).reshape(
        tokens_resident * TOP, MODEL_WIDTH
    )
    grad_back = (
        (grad_pairs[sources] * filled[:, None])
        .astype(jnp.bfloat16)
        .reshape(EXPERTS, capacity, MODEL_WIDTH)
    )
    grad_active = jnp.einsum(
        "ecd,def->ecf", grad_back, expert_w[2], preferred_element_type=jnp.float32
    )
    sigmoid_gate = jax.nn.sigmoid(gate_pre)
    grad_gate = (
        grad_active * up_pre * sigmoid_gate * (1.0 + gate_pre * (1.0 - sigmoid_gate))
    ).astype(jnp.bfloat16)
    grad_up = (grad_active * gate_pre * sigmoid_gate).astype(jnp.bfloat16)
    grad_rows = jnp.einsum(
        "ecf,def->ecd", grad_gate, expert_w[0], preferred_element_type=jnp.float32
    ) + jnp.einsum("ecf,def->ecd", grad_up, expert_w[1], preferred_element_type=jnp.float32)
    gate_term = jnp.einsum(
        "ecd,ecf->def", expert_inputs, grad_gate, preferred_element_type=jnp.float32
    )
    up_term = jnp.einsum("ecd,ecf->def", expert_inputs, grad_up, preferred_element_type=jnp.float32)
    down_term = jnp.einsum("ecd,ecf->def", grad_back, active, preferred_element_type=jnp.float32)
    expert_part = lax.psum_scatter(
        jnp.stack([gate_term, up_term, down_term], axis=1).astype(jnp.bfloat16),
        "dp",
        scatter_dimension=0,
        tiled=True,
    )
    grad_normed_two = jnp.sum(
        grad_rows.reshape(EXPERTS * capacity, MODEL_WIDTH)[slots].reshape(
            tokens_resident, TOP, MODEL_WIDTH
        ),
        axis=1,
    )
    grad_middle_norm, gain_two_term = norm_back(grad_normed_two, middle, factor_two, gain_second)
    grad_middle = grad_out + grad_middle_norm
    grad_branch = (RESIDUAL * grad_middle).astype(jnp.bfloat16)
    output_term = jnp.einsum(
        "th,td->hd", attended_tok, grad_branch, preferred_element_type=jnp.float32
    )
    grad_attended = jnp.einsum(
        "td,hd->th", grad_branch, output_w, preferred_element_type=jnp.float32
    ).astype(jnp.bfloat16)
    grad_heads = lax.all_to_all(grad_attended, "seq", split_axis=1, concat_axis=0, tiled=True)
    block_index = 0
    first_row = block_index * BLOCK
    scores = masked_scores(query_all, key_all, first_row)
    probs = jnp.exp(scores - log_sums[block_index])
    grad_block = grad_heads.reshape(BLOCK, key_value_resident, group_width, HEAD_SIZE)
    grad_probs = jnp.einsum(
        "qkgd,skd->kgqs", grad_block, value_all, preferred_element_type=jnp.float32
    )
    value_part = jnp.einsum(
        "kgqs,qkgd->skd", probs.astype(jnp.bfloat16), grad_block, preferred_element_type=jnp.float32
    )
    inner = jnp.sum(probs * grad_probs, axis=-1, keepdims=True)
    grad_scores = (probs * (grad_probs - inner)).astype(jnp.bfloat16)
    query_part = (
        jnp.einsum("kgqs,skd->qkgd", grad_scores, key_all, preferred_element_type=jnp.float32)
        / HEAD_SIZE
    )
    query_grad_parts = query_part.reshape(BLOCK, head_width).astype(jnp.bfloat16)
    key_part = (
        jnp.einsum("kgqs,qkgd->skd", grad_scores, query_all, preferred_element_type=jnp.float32)
        / HEAD_SIZE
    )
    grad_key_heads = key_part.reshape(sequence_length, key_value_resident * HEAD_SIZE).astype(
        jnp.bfloat16
    )
    grad_value_heads = value_part.reshape(sequence_length, key_value_resident * HEAD_SIZE).astype(
        jnp.bfloat16
    )
    grad_query_tok, grad_key_per_token, grad_value_tok = (
        lax.all_to_all(query_grad_parts, "seq", split_axis=0, concat_axis=1, tiled=True),
        lax.all_to_all(grad_key_heads, "seq", split_axis=0, concat_axis=1, tiled=True),
        lax.all_to_all(grad_value_heads, "seq", split_axis=0, concat_axis=1, tiled=True),
    )
    query_back = unrotate(
        grad_query_tok.astype(jnp.float32).reshape(tokens_resident, QUERY_HEADS, HEAD_SIZE),
        cosine_table,
        sine_table,
    )
    query_back = query_back.reshape(tokens_resident, QUERY_HEADS * HEAD_SIZE).astype(jnp.bfloat16)
    key_unturned = unrotate(
        grad_key_per_token.astype(jnp.float32).reshape(tokens_resident, KEY_VALUE_HEADS, HEAD_SIZE),
        cosine_table,
        sine_table,
    )
    key_unturned = key_unturned.reshape(tokens_resident, KEY_VALUE_HEADS * HEAD_SIZE).astype(
        jnp.bfloat16
    )
    query_term = jnp.einsum(
        "td,tf->df", normed_input, query_back, preferred_element_type=jnp.float32
    )
    key_term = jnp.einsum(
        "td,tf->df", normed_input, key_unturned, preferred_element_type=jnp.float32
    )
    value_term = jnp.einsum(
        "td,tf->df", normed_input, grad_value_tok, preferred_element_type=jnp.float32
    )
    grad_normed = (
        jnp.einsum("tf,df->td", query_back, query_w, preferred_element_type=jnp.float32)
        + jnp.einsum("tf,df->td", key_unturned, key_w, preferred_element_type=jnp.float32)
        + jnp.einsum("tf,df->td", grad_value_tok, value_w, preferred_element_type=jnp.float32)
    )
    grad_input_norm, gain_one_term = norm_back(grad_normed, inputs, factor_one, gain_first)
    grad_input = (grad_middle + grad_input_norm).astype(jnp.bfloat16)
    attn_parts = (
        lax.psum_scatter(
            gain_one_term.astype(jnp.bfloat16), "dp", scatter_dimension=0, tiled=True
        ).astype(jnp.float32),
        lax.psum_scatter(
            query_term.astype(jnp.bfloat16), "dp", scatter_dimension=0, tiled=True
        ).astype(jnp.float32),
        lax.psum_scatter(
            key_term.astype(jnp.bfloat16), "dp", scatter_dimension=0, tiled=True
        ).astype(jnp.float32),
        lax.psum_scatter(
            value_term.astype(jnp.bfloat16), "dp", scatter_dimension=0, tiled=True
        ).astype(jnp.float32),
        lax.psum_scatter(
            output_term.astype(jnp.bfloat16), "dp", scatter_dimension=0, tiled=True
        ).astype(jnp.float32),
        lax.psum_scatter(
            gain_two_term.astype(jnp.bfloat16), "dp", scatter_dimension=0, tiled=True
        ).astype(jnp.float32),
    )
    summed = (
        lax.psum(attn_parts[0].astype(jnp.bfloat16), "seq").astype(jnp.float32),
        lax.psum(attn_parts[1].astype(jnp.bfloat16), "seq").astype(jnp.float32),
        lax.psum(attn_parts[2].astype(jnp.bfloat16), "seq").astype(jnp.float32),
        lax.psum(attn_parts[3].astype(jnp.bfloat16), "seq").astype(jnp.float32),
        lax.psum(attn_parts[4].astype(jnp.bfloat16), "seq").astype(jnp.float32),
        lax.psum(attn_parts[5].astype(jnp.bfloat16), "seq").astype(jnp.float32),
        lax.psum(expert_part, "seq").astype(jnp.float32),
    )
    expert_grads = summed[6]
    return (
        layer_out,
        grad_input,
        summed[0],
        summed[1],
        summed[2],
        summed[3],
        summed[4],
        summed[5],
        expert_grads[:, 0],
        expert_grads[:, 1],
        expert_grads[:, 2],
        grad_gates,
    )


def solution(mesh):
    placed = (
        P(("dp", "seq"), None),
        P("dp"),
        P("dp", None),
        P("dp", None),
        P("dp", None),
        P("dp", None),
        P("dp"),
        P("dp", None, None),
        P("dp", None, None),
        P("dp", None, None),
        P(("dp", "seq"), None),
        P(("dp", "seq"), None),
        P(("dp", "seq"), None),
    )
    return jax.shard_map(
        shards,
        mesh=mesh,
        in_specs=placed,
        out_specs=(
            P(("dp", "seq"), None),
            P(("dp", "seq"), None),
            P("dp"),
            P("dp", None),
            P("dp", None),
            P("dp", None),
            P("dp", None),
            P("dp"),
            P("dp", None, None),
            P("dp", None, None),
            P("dp", None, None),
            P(("dp", "seq"), None),
        ),
        check_vma=False,
    )
```

profile of v0, /device:TPU:1, one launch (start us, length us, event | category | flops | bytes accessed | tf_op | source)
XLA Modules:
  0.0 2117.4 jit_solution(16170524200236689719)
XLA Ops:
  18.7 84.8 %all-reduce.5 = (bf16[1024]{0:T(1024)(128)(2,1)S(1)}, bf16[1024]{0:T(1024)(128)(2,1)S(1)}) all-reduce(bf16[1024]{0:T(1024)(128)(2,1)S(1)} %dynamic-update-slice, bf16[1024]{0:T(1024)(128)(2,1)S(1)} %dynamic-update-slice.1), channel_id=1, replica_groups=mesh['dp'=32,'seq'=4] {'dp'}, use_global_device_ids=true, to_apply=%add | all-reduce | flops 2048 | bytes 8192
  104.7 4.5 reduce-window.6
  110.0 4.3 scatter_custom_fusion
  114.3 4.3 scatter_custom_fusion.1
  118.9 2.3 bitcast_multiply_fusion.1
  123.9 18.0 all-to-all-start.1
  141.9 3.6 all-gather.8.cloned.1.call-done
  147.7 69.8 %all-gather.12.cloned.1.call-done = bf16[1024,1024]{1,0:T(8,128)(2,1)} async-done(((bf16[32,1024]{1,0:T(8,128)(2,1)}), bf16[1024,1024]{1,0:T(8,128)(2,1)}) %all-gather.12.cloned.1.call-update) | async-done | bytes 2097168 | tf_op jit(solution)/shard_map/all_gather | solution.py:94
  220.1 5.3 all-to-all-start
  226.3 2.8 all-to-all-done
  229.1 4.4 all-to-all-start.2
  233.5 8.8 gather_fusion.2
  247.8 3.8 all-to-all-start.3
  251.6 38.5 %all-gather.14.cloned.1.call-done = bf16[1024,1024]{1,0:T(8,128)(2,1)} async-done(((bf16[32,1024]{1,0:T(8,128)(2,1)}), bf16[1024,1024]{1,0:T(8,128)(2,1)}) %all-gather.14.cloned.1.call-update) | async-done | bytes 2097168 | tf_op jit(solution)/shard_map/all_gather | solution.py:97
  292.5 4.4 gather_fusion
  296.9 146.3 %all-gather.16.cloned.1.call-done = bf16[1024,16,512]{2,0,1:T(8,128)(2,1)} async-done(((bf16[32,16,512]{2,0,1:T(8,128)(2,1)}), bf16[1024,16,512]{2,0,1:T(8,128)(2,1)}) %all-gather.16.cloned.1.call-update) | async-done | bytes 16777232 | tf_op jit(solution)/shard_map/all_gather | solution.py:157
  443.2 10.1 fusion.75
  453.2 142.9 %all-gather.18.cloned.1.call-done = bf16[1024,16,512]{2,0,1:T(8,128)(2,1)} async-done(((bf16[32,16,512]{2,0,1:T(8,128)(2,1)}), bf16[1024,16,512]{2,0,1:T(8,128)(2,1)}) %all-gather.18.cloned.1.call-update) | async-done | bytes 16777232 | tf_op jit(solution)/shard_map/all_gather | solution.py:158
  596.2 10.1 fusion.76
  606.3 143.0 %all-gather.20.cloned.1.call-done = bf16[1024,16,512]{2,0,1:T(8,128)(2,1)} async-done(((bf16[32,16,512]{2,0,1:T(8,128)(2,1)}), bf16[1024,16,512]{2,0,1:T(8,128)(2,1)}) %all-gather.20.cloned.1.call-update) | async-done | bytes 16777232 | tf_op jit(solution)/shard_map/all_gather | solution.py:159
  749.3 13.7 multiply_convert_fusion.1
  763.0 13.4 fusion.78
  776.4 14.7 convolution_add_fusion
  791.1 8.8 gather_fusion.3
  800.0 3.2 bitcast_reduce_fusion
  804.7 13.4 fusion.77
  818.2 8.7 gather_fusion.1
  826.9 4.7 fusion.4
  834.1 4.5 all-to-all-start.4
  838.5 5.1 all-to-all-done.4
  844.0 3.3 fusion
  850.9 6.8 all_to_all.116
  859.5 3.7 fusion.24
  864.1 7.6 all_to_all.117
  874.0 3.0 convolution_convert_fusion
  876.9 9.6 convert_bitcast_fusion.1
  891.2 4.6 all-to-all-start.5
  895.8 9.6 convert_bitcast_fusion.2
  910.7 10.5 convert_bitcast_fusion
  921.2 33.8 %pad_maximum_fusion = bf16[1024,3,16,512]{0,3,2,1:T(8,128)(2,1)} fusion(bf16[1024,1,16,512]{0,3,2,1:T(8,128)(2,1)} %convert_bitcast_fusion, bf16[1024,1,16,512]{0,3,2,1:T(8,128)(2,1)} %convert_bitcast_fusion.1, bf16[1024,1,16,512]{0,3,2,1:T(8,128)(2,1)} %convert_bitcast_fusion.2), kind=kLoop, calls=%fused_computation.6 | loop fusion | flops 50331648 | bytes 100663296 | tf_op jit(solution)/shard_map/stack | solution.py:202
  955.1 62.4 %copy.107 = bf16[1024,3,16,512]{3,2,1,0:T(8,128)(2,1)} copy(bf16[1024,3,16,512]{0,3,2,1:T(8,128)(2,1)} %pad_maximum_fusion) | data formatting | bytes 100663296 | tf_op jit(solution)/shard_map/stack | solution.py:202
  1022.2 78.1 %all-reduce.4 = (bf16[1024]{0:T(1024)(128)(2,1)S(1)}, bf16[1024]{0:T(1024)(128)(2,1)S(1)}) all-reduce(bf16[1024]{0:T(1024)(128)(2,1)S(1)} %get-tuple-element.52, bf16[1024]{0:T(1024)(128)(2,1)S(1)} %copy-done.31), channel_id=2, replica_groups=mesh['dp'=32,'seq'=4] {'dp'}, use_global_device_ids=true, to_apply=%region_15.16.clone | all-reduce | flops 2048 | bytes 8192
  1101.5 99.4 %reduce-scatter.10.cloned.1.call-done = bf16[32,512]{1,0:T(8,128)(2,1)} async-done(((bf16[1024,512]{1,0:T(8,128)(2,1)}), bf16[32,512]{1,0:T(8,128)(2,1)}) %reduce-scatter.10.cloned.1.call-update) | async-done | bytes 32784 | tf_op jit(solution)/shard_map/reduce_scatter | solution.py:296
  1200.9 184.3 %reduce-scatter.12.cloned.1.call-done = bf16[32,1024]{1,0:T(8,128)(2,1)} async-done(((bf16[1024,1024]{1,0:T(8,128)(2,1)}), bf16[32,1024]{1,0:T(8,128)(2,1)}) %reduce-scatter.12.cloned.1.call-update) | async-done | bytes 65552 | tf_op jit(solution)/shard_map/reduce_scatter | solution.py:299
  1385.2 184.5 %reduce-scatter.6.cloned.1.call-done = bf16[32,1024]{1,0:T(8,128)(2,1)} async-done(((bf16[1024,1024]{1,0:T(8,128)(2,1)}), bf16[32,1024]{1,0:T(8,128)(2,1)}) %reduce-scatter.6.cloned.1.call-update) | async-done | bytes 65552 | tf_op jit(solution)/shard_map/reduce_scatter | solution.py:290
  1569.8 441.3 %reduce-scatter.14.cloned.1.call-done = bf16[32,3,16,512]{3,2,1,0:T(8,128)(2,1)} async-done(((bf16[1024,3,16,512]{3,2,1,0:T(8,128)(2,1)}), bf16[32,3,16,512]{3,2,1,0:T(8,128)(2,1)}) %reduce-scatter.14.cloned.1.call-update) | async-done | bytes 1572880 | tf_op jit(solution)/shard_map/reduce_scatter | solution.py:201
  2012.7 36.3 %all-reduce.11.cloned.1.call-done = (bf16[32]{0:T(256)(128)(2,1)}, bf16[32,512]{1,0:T(8,128)(2,1)}, bf16[32,512]{1,0:T(8,128)(2,1)}, bf16[32]{0:T(256)(128)(2,1)}) async-done(((bf16[32]{0:T(256)(128)(2,1)}, bf16[32,512]{1,0:T(8,128)(2,1)}, bf16[32,512]{1,0:T(8,128)(2,1)}, bf16[32]{0:T(256)(128)(2,1)}), (bf16[32]{0:T(256)(128)(2,1)}, bf16[32,512]{1,0:T(8,128)(2,1)}, bf16[32,512]{1,0:T(8,128)(2,1)}, ...) | async-done | bytes 65680 | tf_op jit(solution)/shard_map/psum | solution.py:307
  2054.1 49.7 %all-reduce.13.cloned.1.call-done = (bf16[32,1024]{1,0:T(8,128)(2,1)}, bf16[32,1024]{1,0:T(8,128)(2,1)}, bf16[32,3,16,512]{3,2,1,0:T(8,128)(2,1)}) async-done(((bf16[32,1024]{1,0:T(8,128)(2,1)}, bf16[32,1024]{1,0:T(8,128)(2,1)}, bf16[32,3,16,512]{3,2,1,0:T(8,128)(2,1)}), (bf16[32,1024]{1,0:T(8,128)(2,1)}, bf16[32,1024]{1,0:T(8,128)(2,1)}, bf16[32,3,16,512]{3,2,1,0:T(8,128)(2,1)})) %all-reduce.13.cloned.1.call-update) | async-done | bytes 1703952 | tf_op jit(solution)/shard_map/psum | solution.py:308
  (226 shorter events, 69.5 us)
Async XLA Ops:
  7.2 9.8 copy-start.33
  7.2 9.5 copy-start.30
  7.2 11.1 copy-start.34
  7.2 11.3 copy-start.35
  7.2 102.4 %copy-start.16 = (bf16[128,1024]{1,0:T(8,128)(2,1)S(1)}, bf16[128,1024]{1,0:T(8,128)(2,1)}, u32[]{:S(2)}) copy-start(bf16[128,1024]{1,0:T(8,128)(2,1)} %param.25) | copy-start | bytes 786436
  7.2 114.0 %all-gather.10.cloned.1.call-start = ((), (), s32[]{:S(2)}) async-start(), calls=%async_computation.14 | async-start | bytes 1081344 | tf_op jit(solution)/shard_map/all_gather | solution.py:95
  8.0 137.5 %all-gather.8.cloned.1.call-start = ((), (), s32[]{:S(2)}) async-start(), calls=%async_computation.13 | async-start | bytes 1081344 | tf_op jit(solution)/shard_map/all_gather | solution.py:96
  8.7 208.8 %all-gather.12.cloned.1.call-start = ((), (), s32[]{:S(2)}) async-start(), calls=%async_computation.15 | async-start | bytes 2162688 | tf_op jit(solution)/shard_map/all_gather | solution.py:94
  9.5 280.7 %all-gather.14.cloned.1.call-start = ((), (), s32[]{:S(2)}) async-start(), calls=%async_computation.16 | async-start | bytes 2162688 | tf_op jit(solution)/shard_map/all_gather | solution.py:97
  10.0 433.1 %all-gather.16.cloned.1.call-start = ((), (), s32[]{:S(2)}) async-start(), calls=%async_computation.17 | async-start | bytes 17301504 | tf_op jit(solution)/shard_map/all_gather | solution.py:157
  12.2 97.4 %copy-start.32 = (f32[128,8]{0,1:T(8,128)S(1)}, f32[128,8]{0,1:T(8,128)}, u32[]{:S(2)}) copy-start(f32[128,8]{0,1:T(8,128)} %param.24) | copy-start | bytes 12292
  12.2 106.6 %copy-start.2 = (bf16[128,1024]{1,0:T(8,128)(2,1)S(1)}, bf16[128,1024]{1,0:T(8,128)(2,1)}, u32[]{:S(2)}) copy-start(bf16[128,1024]{1,0:T(8,128)(2,1)} %param.13) | copy-start | bytes 786436
  12.2 583.9 %all-gather.18.cloned.1.call-start = ((), (), s32[]{:S(2)}) async-start(), calls=%async_computation.18 | async-start | bytes 17301504 | tf_op jit(solution)/shard_map/all_gather | solution.py:158
  14.5 734.8 %all-gather.20.cloned.1.call-start = ((), (), s32[]{:S(2)}) async-start(), calls=%async_computation.19 | async-start | bytes 17301504 | tf_op jit(solution)/shard_map/all_gather | solution.py:159
  103.8 754.0 %copy-start.22 = (f32[128,64]{0,1:T(8,128)}, f32[128,64]{0,1:T(8,128)S(1)}, u32[]{:S(2)}) copy-start(f32[128,64]{0,1:T(8,128)S(1)} %get-tuple-element.82) | copy-start | bytes 98308
  109.7 13.4 copy-start.11
  118.8 630.5 %copy-start.26 = (f32[16,72]{1,0:T(8,128)}, f32[16,72]{1,0:T(8,128)S(1)}, u32[]{:S(2)}) copy-start(f32[16,72]{1,0:T(8,128)S(1)} %mul.407) | copy-start | bytes 13828
  123.9 96.2 %all-to-all-start.1 = ((bf16[128,4,128]{2,0,1:T(8,128)(2,1)}), bf16[128,4,128]{2,0,1:T(8,128)(2,1)S(1)}, u32[]{:S(2)}, u32[]{:S(2)}) async-start(bf16[128,4,128]{2,0,1:T(8,128)(2,1)} %copy_bitcast_fusion.2), calls=%async_computation.1 | async-start | bytes 262144 | tf_op jit(solution)/shard_map/all_to_all | solution.py:133
  220.1 8.9 all-to-all-start
  229.1 13.8 all-to-all-start.2
  242.6 2.1 copy-start.24
  242.8 1.8 copy-start.23
  244.1 2.1 copy-start
  247.8 42.3 %all-to-all-start.3 = ((bf16[4,128,256]{1,2,0:T(8,128)(2,1)}), bf16[4,128,256]{1,2,0:T(8,128)(2,1)S(1)}, u32[]{:S(2)}, u32[]{:S(2)}) async-start(bf16[4,128,256]{1,2,0:T(8,128)(2,1)} %copy.88), calls=%async_computation.3 | async-start | bytes 524288 | tf_op jit(solution)/shard_map/all_to_all | solution.py:149
  290.1 2.3 copy-start.13
  826.9 4.7 copy-start.10
  826.9 4.7 copy-start.17
  826.9 5.6 copy-start.5
  831.5 7.0 copy-start.29
  834.1 9.6 all-to-all-start.4
  838.5 263.0 %reduce-scatter.8.cloned.1.call-start = ((), (), s32[]{:S(2)}) async-start(), calls=%async_computation.21 | async-start | bytes 1081344 | tf_op jit(solution)/shard_map/reduce_scatter | solution.py:293
  844.0 3.5 copy-start.1
  847.5 2.5 copy-start.19
  850.0 7.8 copy-start.21
  859.4 14.6 copy-start.7
  859.4 341.5 %reduce-scatter.10.cloned.1.call-start = ((), (), s32[]{:S(2)}) async-start(), calls=%async_computation.22 | async-start | bytes 1081344 | tf_op jit(solution)/shard_map/reduce_scatter | solution.py:296
  873.9 511.3 %reduce-scatter.12.cloned.1.call-start = ((), (), s32[]{:S(2)}) async-start(), calls=%async_computation.23 | async-start | bytes 2162688 | tf_op jit(solution)/shard_map/reduce_scatter | solution.py:299
  891.2 14.3 all-to-all-start.5
  895.8 673.9 %reduce-scatter.6.cloned.1.call-start = ((), (), s32[]{:S(2)}) async-start(), calls=%async_computation.20 | async-start | bytes 2162688 | tf_op jit(solution)/shard_map/reduce_scatter | solution.py:290
  905.5 5.2 copy-start.8
  905.5 5.2 copy-start.27
  910.6 1100.5 %reduce-scatter.14.cloned.1.call-start = ((), (), s32[]{:S(2)}) async-start(), calls=%async_computation.24 | async-start | bytes 51904512 | tf_op jit(solution)/shard_map/reduce_scatter | solution.py:201
  1017.5 4.1 copy-start.15
  1017.5 4.8 copy-start.31
  1017.5 1031.6 %all-reduce.11.cloned.1.call-start = ((), (), s32[]{:S(2)}) async-start(), calls=%async_computation.25 | async-start | bytes 133120 | tf_op jit(solution)/shard_map/psum | solution.py:307
  1019.0 2.6 copy-start.12
  1019.0 992.1 %copy-start.25 = (f32[128,8]{1,0:T(8,128)S(1)}, f32[128,8]{1,0:T(8,128)}, u32[]{:S(2)}) copy-start(f32[128,8]{1,0:T(8,128)} %get-tuple-element.48) | copy-start | bytes 12292
  1200.9 902.9 %all-reduce.13.cloned.1.call-start = ((), (), s32[]{:S(2)}) async-start(), calls=%async_computation.26 | async-start | bytes 3407872 | tf_op jit(solution)/shard_map/psum | solution.py:308
  (8 other events, 8.2 us)
Sparse Core Ops, SparseCore 0:
  11.1 67.9 all-gather.9
  82.0 63.4 all-gather.7
  148.6 68.9 all-gather.11
  220.5 69.5 all-gather.13
  293.8 149.3 all-gather.15
  446.8 149.2 all-gather.17
  600.0 149.2 all-gather.19
  859.5 158.2 reduce-scatter.7
  1020.9 179.9 reduce-scatter.9
  1203.1 182.0 reduce-scatter.11
  1387.7 181.9 reduce-scatter.5
  1575.4 435.6 reduce-scatter.13
  2014.6 34.4 all-reduce.10
  2051.7 52.1 all-reduce.12
where the time goes:
time: 2130 us; the launch traced here: 2120 us
  waiting for transfers between devices  1550 us (73%)
  blocking collectives  177 us (8%)
  matrix products  136 us (6%)
  local copies, waits for them, and re-layouts  128 us (6%)
  other arithmetic  67.7 us (3%)
  starting transfers between devices  41 us (2%)
    reduce_scatter x1, waiting for transfers between devices, shards(): lax.psum_scatter(jnp.stack([gate_term, up_term, down_term], axis=1).astyp...  441 us
    reduce_scatter x1, waiting for transfers between devices, shards(): lax.psum_scatter(query_term.astype(jnp.bfloat16), 'dp', scatter_dimension...  185 us
    reduce_scatter x1, waiting for transfers between devices, shards(): lax.psum_scatter(output_term.astype(jnp.bfloat16), 'dp', scatter_dimensio...  184 us
    unnamed x2, blocking collectives  163 us
    all_gather x1, waiting for transfers between devices, shards(): lax.all_gather(w_gate, 'dp', axis=0, tiled=True)  146 us
    all_gather x1, waiting for transfers between devices, shards(): lax.all_gather(w_down, 'dp', axis=0, tiled=True)  143 us
    all_gather x1, waiting for transfers between devices, shards(): lax.all_gather(w_up, 'dp', axis=0, tiled=True)  143 us
    reduce_scatter x1, waiting for transfers between devices, shards(): lax.psum_scatter(value_term.astype(jnp.bfloat16), 'dp', scatter_dimension...  99.4 us
  transfers between devices with their start and end apart: 20, of which 14 were waited for; matrix products, arithmetic and copies ran while one was open for 11% of the time, Pallas kernels for 0%

commit v1 on v0

v1 whole, which is shorter than its diff:
```python
import jax
import jax.numpy as jnp
from jax import lax
from jax.experimental import pallas as pl
from jax.experimental.pallas import tpu as pltpu
from jax.sharding import Mesh
from jax.sharding import PartitionSpec as P

MODEL_WIDTH = 1024
QUERY_HEADS = 16
KEY_VALUE_HEADS = 8
HEAD_SIZE = 64
TOP = 8
EXPERTS = 16
CAP = 72
SLOTS = EXPERTS * CAP
TOK = 128
SEQ_LEN = 512
FF = 512
EPSILON = 1e-05
RESIDUAL = 0.22
ROPE_BASE = 10000.0
MASK_VALUE = -1e30

BF16 = jnp.bfloat16
F32 = jnp.float32
AXES = ("yh", "x", "z", "seq")
BY_ID = pl.DeviceIdType.MESH


def place():
    return tuple(lax.axis_index(axis) for axis in AXES)


class Sender:
    def __init__(self, send, recv):
        self.send, self.recv, self.used, self.copies = send, recv, 0, []

    def start(self, source, target, device):
        copy = pltpu.make_async_remote_copy(
            src_ref=source,
            dst_ref=target,
            send_sem=self.send.at[self.used],
            recv_sem=self.recv.at[self.used],
            device_id=device,
            device_id_type=BY_ID,
        )
        copy.start()
        self.used += 1
        self.copies.append(copy)
        return copy

    def finish(self):
        for copy in self.copies:
            copy.wait_send()


def arrived(copies):
    for copy in copies:
        copy.wait_recv()


def greet(partners):
    barrier = pltpu.get_barrier_semaphore()
    for partner in partners:
        pl.semaphore_signal(barrier, inc=1, device_id=partner, device_id_type=BY_ID)
    pl.semaphore_wait(barrier, len(partners))


def remote_call(kernel, inputs, outputs, copies, local_copies, collective_id, name):
    return pl.pallas_call(
        kernel,
        out_shape=tuple(jax.ShapeDtypeStruct(shape, BF16) for shape in outputs),
        in_specs=[pl.BlockSpec(memory_space=pl.ANY)] * len(inputs),
        out_specs=tuple(pl.BlockSpec(memory_space=pl.ANY) for _ in outputs),
        scratch_shapes=[
            pltpu.SemaphoreType.DMA((copies,)),
            pltpu.SemaphoreType.DMA((copies,)),
            pltpu.SemaphoreType.DMA((local_copies,)),
        ],
        compiler_params=pltpu.CompilerParams(collective_id=collective_id, has_side_effects=True),
        name=name,
    )(*inputs)


def local_starts(pairs, sems):
    copies = []
    for index, (source, target) in enumerate(pairs):
        copy = pltpu.make_async_copy(source, target, sems.at[index])
        copy.start()
        copies.append(copy)
    return copies


def gather_kernel(
    heads, branch, tokens, experts, rows,
    heads_all, branch_all, tokens_all, experts_all, rows_all,
    send, recv, local,
):
    yh, x, z, seq = place()
    yl, core = seq // 2, seq % 2
    along_y = (1 - yh, x, z, seq)
    along_x = [(yh, (x + k) % 4, z, seq) for k in (1, 2, 3)]
    along_z = [(yh, x, (z + k) % 4, seq) for k in (1, 2, 3)]
    group = [
        (yh, x, (z + k // 4) % 4, (yl + (k // 2) % 2) % 2 * 2 + (core + k % 2) % 2)
        for k in range(1, 16)
    ]
    near = (yh, x, z, (1 - yl) * 2 + core)
    sibling = (yh, x, z, yl * 2 + 1 - core)
    expert = z * 4 + seq
    greet([along_y] + along_x + group)
    own = local_starts(
        [
            (heads, heads_all.at[yh, x, z]),
            (branch, branch_all.at[core, yh, x, z]),
            (tokens, tokens_all.at[yl, core]),
            (experts.at[z], experts_all.at[:, yh, x, z]),
            (rows.at[expert], rows_all.at[expert]),
        ],
        local,
    )
    sender = Sender(send, recv)
    first = [
        sender.start(heads, heads_all.at[yh, x, z], along_y),
        sender.start(branch, branch_all.at[core, yh, x, z], along_y),
    ]
    expert_first = [
        sender.start(experts.at[(z + k) % 4], experts_all.at[:, yh, x, z], along_z[k - 1])
        for k in (1, 2, 3)
    ]
    token_copies = [
        sender.start(tokens, tokens_all.at[yl, core], near),
        sender.start(tokens, tokens_all.at[yl, core], sibling),
    ]
    for copy in own:
        copy.wait()
    arrived(first)
    second = []
    for k in range(3):
        for source in (heads_all.at[:, x, z, 0], branch_all.at[core, :, x, z, 0]):
            second.append(sender.start(source, source, along_x[k]))
        for source in (heads_all.at[:, x, z, 1], branch_all.at[core, :, x, z, 1]):
            second.append(sender.start(source, source, along_z[k]))
    arrived(expert_first)
    mine = experts_all.at[:, yh, x]
    expert_second = [sender.start(mine, mine, along_y)]
    arrived(second)
    third = []
    for k in range(3):
        for source in (heads_all.at[:, :, z, 0], branch_all.at[core, :, :, z, 0]):
            third.append(sender.start(source, source, along_z[k]))
        for source in (heads_all.at[:, x, :, 1], branch_all.at[core, :, x, :, 1]):
            third.append(sender.start(source, source, along_x[k]))
    arrived(expert_second)
    mine = experts_all.at[:, :, x]
    expert_third = [sender.start(mine, mine, along_x[k]) for k in range(3)]
    row_copies = []
    for partner in group:
        other = partner[2] * 4 + partner[3]
        row_copies.append(sender.start(rows.at[other], rows_all.at[expert], partner))
    arrived(token_copies)
    far = tokens_all.at[1 - yl, core]
    last = [sender.start(far, far, sibling)]
    arrived(third)
    half = branch_all.at[core]
    last.append(sender.start(half, half, sibling))
    arrived(expert_third)
    arrived(row_copies)
    arrived(last)
    sender.finish()


def scatter_kernel(
    heads, branch, experts,
    heads_all, branch_all, experts_all,
    send, recv, local,
):
    yh, x, z, seq = place()
    dp = yh * 16 + x * 4 + z

    def branch_block(index):
        top = pl.multiple_of(index // 2 * 16, 16)
        left = pl.multiple_of(index % 2 * 512, 512)
        return branch.at[pl.ds(top, 16), pl.ds(left, 512)]

    others = [(dp + k) % 32 for k in range(1, 32)]
    partners = [(other // 16, other // 4 % 4, other % 4, seq) for other in others]
    greet(partners)
    own = local_starts(
        [
            (heads.at[dp], heads_all.at[dp]),
            (branch_block(dp), branch_all.at[dp]),
            (experts.at[:, dp], experts_all.at[dp]),
        ],
        local,
    )
    sender = Sender(send, recv)
    for other, partner in zip(others, partners):
        sender.start(experts.at[:, other], experts_all.at[dp], partner)
        sender.start(heads.at[other], heads_all.at[dp], partner)
        sender.start(branch_block(other), branch_all.at[dp], partner)
    for copy in own:
        copy.wait()
    arrived(sender.copies)
    sender.finish()


def share_kernel(
    heads, branch, experts,
    heads_all, branch_all, experts_all,
    send, recv, local, branch_sends, branch_recvs,
):
    yh, x, z, seq = place()
    yl, core = seq // 2, seq % 2
    dp = yh * 16 + x * 4 + z
    near = (yh, x, z, (1 - yl) * 2 + core)
    sibling = (yh, x, z, yl * 2 + 1 - core)
    owner = seq * 8 + dp // 4
    source_seq = dp // 8
    slot = dp % 4
    barrier = pltpu.get_barrier_semaphore()
    for partner in (near, sibling):
        pl.semaphore_signal(barrier, inc=1, device_id=partner, device_id_type=BY_ID)
    here = jnp.logical_and(owner == dp, True)
    for k in range(4):
        maker = dp % 8 * 4 + k
        foreign = jnp.logical_or(maker != dp, source_seq != seq)

        @pl.when(foreign)
        def _():
            pl.semaphore_signal(
                barrier,
                inc=1,
                device_id=(maker // 16, maker // 4 % 4, maker % 4, source_seq),
                device_id_type=BY_ID,
            )

    pl.semaphore_wait(barrier, 6 - here.astype(jnp.int32))
    own = local_starts(
        [(heads, heads_all.at[yl, core]), (experts, experts_all.at[yl, core])], local
    )
    sender = Sender(send, recv)
    first = []
    for partner in (near, sibling):
        first.append(sender.start(heads, heads_all.at[yl, core], partner))
        first.append(sender.start(experts, experts_all.at[yl, core], partner))
    place_of = branch_all.at[slot]

    def branch_copy(k):
        return pltpu.make_async_remote_copy(
            src_ref=branch,
            dst_ref=place_of,
            send_sem=branch_sends.at[k],
            recv_sem=branch_recvs.at[slot],
            device_id=(owner // 16, owner // 4 % 4, owner % 4, k),
            device_id_type=BY_ID,
        )

    for k in range(4):
        self_copy = jnp.logical_and(here, seq == k)

        @pl.when(jnp.logical_not(self_copy))
        def _():
            branch_copy(k).start()

        @pl.when(self_copy)
        def _():
            pltpu.make_async_copy(branch, place_of, branch_recvs.at[slot]).start()

    for copy in own:
        copy.wait()
    arrived(first[:2])
    last = []
    for buffer in (heads_all, experts_all):
        far = buffer.at[1 - yl, core]
        last.append(sender.start(far, far, sibling))
    arrived(first[2:])
    arrived(last)
    for k in range(4):
        pltpu.make_async_copy(branch, branch_all.at[k], branch_recvs.at[k]).wait()
        self_copy = jnp.logical_and(here, seq == k)

        @pl.when(jnp.logical_not(self_copy))
        def _():
            branch_copy(k).wait_send()

    sender.finish()


def angles(count, head_dim):
    freqs = ROPE_BASE ** (-jnp.arange(0, head_dim, 2).astype(F32) / head_dim)
    places = jnp.arange(count, dtype=jnp.int32).astype(F32)
    turns = places[:, None] * freqs[None, :]
    turns = jnp.concatenate([turns, turns], axis=-1)
    return (jnp.cos(turns)[:, None, :], jnp.sin(turns)[:, None, :])


def turned(values):
    half = values.shape[-1] // 2
    return jnp.concatenate([-values[..., half:], values[..., :half]], axis=-1)


def masked_scores(query_block, key_rows):
    scores = (
        jnp.einsum("qkgd,skd->kgqs", query_block, key_rows, preferred_element_type=F32)
        / query_block.shape[-1]
    )
    causal = jnp.arange(query_block.shape[0])[:, None] >= jnp.arange(key_rows.shape[0])[None, :]
    return jnp.where(causal, scores, MASK_VALUE)


def norm_back(grad_normed, values, factor, gain):
    scaled = grad_normed * gain
    mean_term = jnp.mean(scaled * values, axis=-1, keepdims=True)
    grad_values = factor * scaled - values * factor * factor * factor * mean_term
    grad_gain = jnp.sum(grad_normed * values * factor, axis=0)
    return (grad_values, grad_gain)


def slot_matrices(routes, route_gates):
    named = (routes[:, :, None] == jnp.arange(EXPERTS, dtype=jnp.int32)).astype(F32)
    uses = jnp.sum(named, axis=1)
    gates = jnp.sum(named * route_gates[:, :, None], axis=1)
    row = lax.broadcasted_iota(jnp.int32, (TOK, TOK), 0)
    column = lax.broadcasted_iota(jnp.int32, (TOK, TOK), 1)
    earlier = (row > column).astype(BF16)
    ranks = jnp.dot(earlier, uses.astype(BF16), preferred_element_type=F32)
    slot = jnp.arange(SLOTS, dtype=jnp.int32)
    spread = (jnp.arange(EXPERTS, dtype=jnp.int32)[:, None] == slot[None, :] // CAP).astype(F32)
    both = jnp.where(uses > 0.5, ranks, -1.0).astype(BF16)
    flat = jnp.dot(both, spread.astype(BF16), preferred_element_type=F32)
    hits = flat == (slot % CAP).astype(F32)[None, :]
    flat_gates = jnp.dot(gates, spread, precision=lax.Precision.HIGHEST)
    weights = jnp.where(hits, RESIDUAL * flat_gates, 0.0)
    return (named, spread, hits.astype(BF16), weights)


def shards(
    layer_in, norm_one, w_query, key_weight, value_weight, w_output, norm_two,
    w_gate, w_up, w_down, routes, route_gates, cotangent,
):
    seq = lax.axis_index("seq")
    core = seq % 2
    key_value_resident = KEY_VALUE_HEADS // 4
    group_width = QUERY_HEADS // KEY_VALUE_HEADS
    head_width = key_value_resident * group_width * HEAD_SIZE
    kv_width = key_value_resident * HEAD_SIZE

    gains = jnp.pad(jnp.stack([norm_one, norm_two], axis=1), ((0, 0), (0, 126)))
    heads_block = jnp.concatenate(
        [
            lax.dynamic_slice_in_dim(w_query, seq * head_width, head_width, 1),
            lax.dynamic_slice_in_dim(key_weight, seq * kv_width, kv_width, 1),
            lax.dynamic_slice_in_dim(value_weight, seq * kv_width, kv_width, 1),
            gains,
        ],
        axis=1,
    ).reshape(2, 16, 640)
    branch_block = lax.dynamic_slice_in_dim(w_output, core * 512, 512, 1).reshape(2, 16, 512)
    expert_block = jnp.stack(
        [
            lax.dynamic_index_in_dim(w.reshape(32, 4, 4, FF), seq, 2, keepdims=False)
            for w in (w_gate, w_up, w_down)
        ]
    ).transpose(2, 0, 1, 3)
    named, spread, hits, weights = slot_matrices(routes, route_gates)
    slot_weights = jnp.sum(weights, axis=0)
    grad_slots = (
        jnp.einsum("tj,td->jd", hits, cotangent, preferred_element_type=F32)
        * slot_weights[:, None]
    ).astype(BF16).reshape(EXPERTS, CAP, MODEL_WIDTH)

    heads_w, branch_w, tokens_all, expert_w, grad_returned = remote_call(
        gather_kernel,
        (heads_block, branch_block, layer_in, expert_block, grad_slots),
        (
            (2, 4, 4, 2, 16, 640),
            (2, 2, 4, 4, 2, 16, 512),
            (2, 2, TOK, MODEL_WIDTH),
            (3, 2, 4, 4, 32, FF),
            (EXPERTS, CAP, MODEL_WIDTH),
        ),
        52,
        5,
        1,
        "gather_all",
    )
    heads_w = heads_w.reshape(MODEL_WIDTH, 640)
    gain_first = heads_w[:, 512].astype(F32)
    gain_second = heads_w[:, 513].astype(F32)
    heads_w = heads_w[:, :512]
    branch_w = branch_w.reshape(2, MODEL_WIDTH, 512)
    expert_w = expert_w.reshape(3, MODEL_WIDTH, FF)
    grad_back = grad_returned.reshape(SLOTS, MODEL_WIDTH)

    sequence = tokens_all.reshape(SEQ_LEN, MODEL_WIDTH).astype(F32)
    factor_all = lax.rsqrt(jnp.mean(sequence * sequence, axis=-1, keepdims=True) + EPSILON)
    normed_all = (sequence * factor_all * gain_first).astype(BF16)
    cosine, sine = angles(SEQ_LEN, HEAD_SIZE)
    projected = jnp.dot(normed_all, heads_w, preferred_element_type=F32)
    query_pre = projected[:, :head_width].reshape(SEQ_LEN, -1, HEAD_SIZE)
    key_pre = projected[:, head_width : head_width + kv_width].reshape(SEQ_LEN, -1, HEAD_SIZE)
    query_all = (query_pre * cosine + turned(query_pre) * sine).astype(BF16)
    query_all = query_all.reshape(SEQ_LEN, key_value_resident, group_width, HEAD_SIZE)
    key_all = (key_pre * cosine + turned(key_pre) * sine).astype(BF16)
    value_all = projected[:, head_width + kv_width :].astype(BF16)
    value_all = value_all.reshape(SEQ_LEN, key_value_resident, HEAD_SIZE)
    scores = masked_scores(query_all, key_all)
    top_score = jnp.max(scores, axis=-1, keepdims=True)
    exponent = jnp.exp(scores - top_score)
    total_mass = jnp.sum(exponent, axis=-1, keepdims=True)
    probs = (exponent / total_mass).astype(BF16)
    log_sums = top_score + jnp.log(total_mass)
    attended = jnp.einsum("kgqs,skd->qkgd", probs, value_all, preferred_element_type=F32)
    attended = attended.reshape(SEQ_LEN, head_width).astype(BF16)
    attended_tok = lax.all_to_all(attended, "seq", split_axis=0, concat_axis=1, tiled=True)

    inputs = layer_in.astype(F32)
    branch = jnp.concatenate(
        [jnp.dot(attended_tok, branch_w[k], preferred_element_type=F32) for k in range(2)], axis=1
    )
    middle = inputs + RESIDUAL * branch
    factor_two = lax.rsqrt(jnp.mean(middle * middle, axis=-1, keepdims=True) + EPSILON)
    normed_two = (middle * factor_two * gain_second).astype(BF16)
    slot_rows = jnp.einsum("tj,td->jd", hits, normed_two, preferred_element_type=F32).astype(BF16)
    expert_rows = lax.all_to_all(
        slot_rows.reshape(EXPERTS, CAP, MODEL_WIDTH), ("z", "seq"), 0, 0, tiled=True
    ).reshape(SLOTS, MODEL_WIDTH)

    gate_pre = jnp.dot(expert_rows, expert_w[0], preferred_element_type=F32)
    up_pre = jnp.dot(expert_rows, expert_w[1], preferred_element_type=F32)
    sigmoid_gate = jax.nn.sigmoid(gate_pre)
    active = (gate_pre * sigmoid_gate * up_pre).astype(BF16)
    returned = jnp.einsum("cf,df->cd", active, expert_w[2], preferred_element_type=F32)
    grad_active = jnp.dot(grad_back, expert_w[2], preferred_element_type=F32)
    grad_gate = (
        grad_active * up_pre * sigmoid_gate * (1.0 + gate_pre * (1.0 - sigmoid_gate))
    ).astype(BF16)
    grad_up = (grad_active * gate_pre * sigmoid_gate).astype(BF16)
    grad_rows = (
        jnp.einsum("cf,df->cd", grad_gate, expert_w[0], preferred_element_type=F32)
        + jnp.einsum("cf,df->cd", grad_up, expert_w[1], preferred_element_type=F32)
    ).astype(BF16)
    grad_rows = lax.all_to_all(
        grad_rows.reshape(EXPERTS, CAP, MODEL_WIDTH), ("z", "seq"), 0, 0, tiled=True
    ).reshape(SLOTS, MODEL_WIDTH)
    returned = lax.all_to_all(
        returned.astype(BF16).reshape(EXPERTS, CAP, MODEL_WIDTH), ("z", "seq"), 0, 0, tiled=True
    ).reshape(SLOTS, MODEL_WIDTH)
    expert_grads = jnp.stack(
        [
            jnp.einsum("cd,cf->df", expert_rows, grad_gate, preferred_element_type=F32).astype(BF16),
            jnp.einsum("cd,cf->df", expert_rows, grad_up, preferred_element_type=F32).astype(BF16),
            jnp.einsum("cd,cf->df", grad_back, active, preferred_element_type=F32).astype(BF16),
        ]
    ).reshape(3, 32, 32, FF)

    grad_out = cotangent.astype(F32)
    layer_out = (
        middle + jnp.dot(weights.astype(BF16), returned, preferred_element_type=F32)
    ).astype(BF16)
    pair_dots = jnp.einsum("td,jd->tj", cotangent, returned, preferred_element_type=F32)
    expert_dots = jnp.einsum(
        "tj,ej->te", pair_dots * hits.astype(F32), spread, precision=lax.Precision.HIGHEST
    )
    grad_gates = RESIDUAL * jnp.sum(named * expert_dots[:, None, :], axis=-1)
    grad_normed_two = jnp.dot(hits, grad_rows, preferred_element_type=F32)
    grad_middle_norm, gain_two_term = norm_back(grad_normed_two, middle, factor_two, gain_second)
    grad_middle = grad_out + grad_middle_norm
    grad_branch = (RESIDUAL * grad_middle).astype(BF16)
    grad_branch_all = lax.all_gather(grad_branch, "seq", axis=0, tiled=True)
    branch_rows = lax.dynamic_slice_in_dim(branch_w, seq * head_width, head_width, 1)
    output_term = jnp.einsum(
        "th,td->hd", attended, grad_branch_all, preferred_element_type=F32
    ).astype(BF16)
    grad_heads = (
        jnp.einsum("td,hd->th", grad_branch_all[:, :512], branch_rows[0], preferred_element_type=F32)
        + jnp.einsum(
            "td,hd->th", grad_branch_all[:, 512:], branch_rows[1], preferred_element_type=F32
        )
    ).astype(BF16)

    scores = masked_scores(query_all, key_all)
    probs = jnp.exp(scores - log_sums)
    grad_block = grad_heads.reshape(SEQ_LEN, key_value_resident, group_width, HEAD_SIZE)
    grad_probs = jnp.einsum("qkgd,skd->kgqs", grad_block, value_all, preferred_element_type=F32)
    grad_value = jnp.einsum(
        "kgqs,qkgd->skd", probs.astype(BF16), grad_block, preferred_element_type=F32
    )
    inner = jnp.sum(probs * grad_probs, axis=-1, keepdims=True)
    grad_scores = (probs * (grad_probs - inner)).astype(BF16)
    grad_query = (
        jnp.einsum("kgqs,skd->qkgd", grad_scores, key_all, preferred_element_type=F32) / HEAD_SIZE
    ).reshape(SEQ_LEN, -1, HEAD_SIZE)
    grad_key = (
        jnp.einsum("kgqs,qkgd->skd", grad_scores, query_all, preferred_element_type=F32) / HEAD_SIZE
    )
    grad_query = grad_query.astype(BF16).astype(F32)
    grad_key = grad_key.astype(BF16).astype(F32)
    grad_projected = jnp.concatenate(
        [
            (grad_query * cosine - turned(grad_query) * sine).reshape(SEQ_LEN, -1).astype(BF16),
            (grad_key * cosine - turned(grad_key) * sine).reshape(SEQ_LEN, -1).astype(BF16),
            grad_value.reshape(SEQ_LEN, -1).astype(BF16),
        ],
        axis=1,
    )
    heads_term = jnp.einsum(
        "td,tf->df", normed_all, grad_projected, preferred_element_type=F32
    ).astype(BF16)
    grad_normed_parts = jnp.einsum(
        "tf,df->td", grad_projected, heads_w, preferred_element_type=F32
    ).astype(BF16)
    grad_normed_parts = lax.all_to_all(
        grad_normed_parts.reshape(4, TOK, MODEL_WIDTH), "seq", 0, 0, tiled=True
    )
    grad_normed = jnp.sum(grad_normed_parts.astype(F32), axis=0)
    factor_one = lax.rsqrt(jnp.mean(inputs * inputs, axis=-1, keepdims=True) + EPSILON)
    grad_input_norm, gain_one_term = norm_back(grad_normed, inputs, factor_one, gain_first)
    grad_input = (grad_middle + grad_input_norm).astype(BF16)

    gain_terms = jnp.pad(
        jnp.stack([gain_one_term, gain_two_term], axis=1).astype(BF16), ((0, 0), (0, 126))
    )
    heads_term = jnp.concatenate([heads_term, gain_terms], axis=1).reshape(32, 32, 640)
    heads_parts, branch_parts, expert_parts = remote_call(
        scatter_kernel,
        (heads_term, output_term, expert_grads),
        ((32, 32, 640), (32, 16, 512), (32, 3, 32, FF)),
        93,
        3,
        2,
        "scatter_all",
    )
    heads_sum = jnp.sum(heads_parts.astype(F32), axis=0).astype(BF16)
    branch_sum = jnp.sum(branch_parts.astype(F32), axis=0).astype(BF16)
    expert_sum = jnp.sum(expert_parts.astype(F32).reshape(8, 4, 3, 32, FF), axis=0).astype(BF16)
    heads_four, branch_four, expert_four = pl.pallas_call(
        share_kernel,
        out_shape=(
            jax.ShapeDtypeStruct((2, 2, 32, 640), BF16),
            jax.ShapeDtypeStruct((4, 16, 512), BF16),
            jax.ShapeDtypeStruct((2, 2, 4, 3, 32, FF), BF16),
        ),
        in_specs=[pl.BlockSpec(memory_space=pl.ANY)] * 3,
        out_specs=(pl.BlockSpec(memory_space=pl.ANY),) * 3,
        scratch_shapes=[
            pltpu.SemaphoreType.DMA((6,)),
            pltpu.SemaphoreType.DMA((6,)),
            pltpu.SemaphoreType.DMA((2,)),
            pltpu.SemaphoreType.DMA((4,)),
            pltpu.SemaphoreType.DMA((4,)),
        ],
        compiler_params=pltpu.CompilerParams(collective_id=3, has_side_effects=True),
        name="share_all",
    )(heads_sum, branch_sum, expert_sum)
    heads_four = heads_four.reshape(4, 32, 640).astype(F32)
    grad_query_proj = heads_four[:, :, :head_width].transpose(1, 0, 2).reshape(32, -1)
    grad_key_proj = heads_four[:, :, 256:384].transpose(1, 0, 2).reshape(32, -1)
    grad_value_proj = heads_four[:, :, 384:512].transpose(1, 0, 2).reshape(32, -1)
    gain_sums = jnp.sum(heads_four[:, :, 512:514], axis=0)
    grad_output_proj = (
        branch_four.reshape(2, 2, 16, 512).transpose(0, 2, 1, 3).reshape(32, MODEL_WIDTH).astype(F32)
    )
    expert_four = expert_four.reshape(4, 4, 3, 32, FF).transpose(2, 3, 1, 0, 4)
    expert_four = expert_four.reshape(3, 32, EXPERTS, FF).astype(F32)
    return (
        layer_out,
        grad_input,
        gain_sums[:, 0],
        grad_query_proj,
        grad_key_proj,
        grad_value_proj,
        grad_output_proj,
        gain_sums[:, 1],
        expert_four[0],
        expert_four[1],
        expert_four[2],
        grad_gates,
    )


def solution(mesh):
    dp = ("yh", "x", "z")
    cut = Mesh(mesh.devices.reshape(2, 4, 4, 4), AXES)
    tokens, rows, gain, experts = P(AXES, None), P(dp, None), P(dp), P(dp, None, None)
    return jax.shard_map(
        shards,
        mesh=cut,
        in_specs=(
            tokens, gain, rows, rows, rows, rows, gain, experts, experts, experts,
            tokens, tokens, tokens,
        ),
        out_specs=(
            tokens, tokens, gain, rows, rows, rows, rows, gain, experts, experts, experts, tokens,
        ),
        check_vma=False,
    )
```

time: 2130 us -> 447 us (0.21)
  the two profiles are of different devices: /device:TPU:1 before, /device:TPU:15 now
where the time goes in v1:
time: 447 us; the launch traced here: 438 us
  Pallas kernels  204 us (46%)
  waiting for transfers between devices  81.2 us (18%)
  matrix products  59.2 us (13%)
  starting transfers between devices  28.7 us (6%)
  local copies, waits for them, and re-layouts  26.6 us (6%)
  other arithmetic  23.8 us (5%)
  between operations  15.4 us (3%)
    pallas_call x2, Pallas kernels, remote_call(): pl.pallas_call(kernel, out_shape=tuple((jax.ShapeDtypeStruct(shape, BF16)...  156 us
    pallas_call x1, Pallas kernels, shards(): pl.pallas_call(share_kernel, out_shape=(jax.ShapeDtypeStruct((2, 2, 32, 6...  47.5 us
    all_to_all x1, waiting for transfers between devices, shards(): lax.all_to_all(slot_rows.reshape(EXPERTS, CAP, MODEL_WIDTH), ('z', 'seq')...  26.3 us
    all_to_all x1, waiting for transfers between devices, shards(): lax.all_to_all(grad_rows.reshape(EXPERTS, CAP, MODEL_WIDTH), ('z', 'seq')...  25 us
    all_to_all x1, waiting for transfers between devices, shards(): lax.all_to_all(returned.astype(BF16).reshape(EXPERTS, CAP, MODEL_WIDTH),...  19.9 us
  transfers between devices with their start and end apart: 6, of which 5 were waited for; matrix products, arithmetic and copies ran while one was open for 8% of the time, Pallas kernels for 0%

profile of v1, /device:TPU:15, one launch (start us, length us, event | category | flops | bytes accessed | tf_op | source)
XLA Modules:
  0.0 438.5 jit_solution(8267202655007003290)
XLA Ops:
  13.9 2.3 fusion.3
  18.3 78.6 %gather_all.1 = (bf16[2,4,4,2,16,640]{5,4,3,2,1,0:T(8,128)(2,1)}, bf16[2,2,4,4,2,16,512]{6,5,4,3,2,1,0:T(8,128)(2,1)}, bf16[2,2,128,1024]{3,2,1,0:T(8,128)(2,1)}...) custom-call(bf16[2,16,640]{2,1,0:T(8,128)(2,1)} %bitcast.248, bf16[2,16,512]{2,1,0:T(8,128)(2,1)} %bitcast.249, ...), custom_call_target="tpu_custom_call" | custom-call | tf_op jit(solution)/shard_map/gather_all/pallas_call | solution.py:71
  97.0 1.6 multiply_reduce_fusion
  98.6 1.3 slice_convert_fusion
  100.4 2.4 fusion.32
  107.8 5.0 %all-to-all-start = ((bf16[4,128,256]{1,2,0:T(8,128)(2,1)}), bf16[4,128,256]{1,2,0:T(8,128)(2,1)S(1)}, u32[]{:S(2)}, u32[]{:S(2)}) async-start(bf16[4,128,256]{1,2,0:T(8,128)(2,1)} %copy.118), calls=%async_computation | async-start | bytes 524288 | tf_op jit(solution)/shard_map/all_to_all | solution.py:417
  112.9 1.9 fusion.91
  114.8 2.1 all-to-all-done
  117.8 2.3 convolution_convert_fusion.1
  120.0 6.4 %all-to-all-start.1 = ((bf16[16,72,1024]{2,1,0:T(8,128)(2,1)}), bf16[16,72,1024]{2,1,0:T(8,128)(2,1)}, u32[]{:S(2)}, u32[]{:S(2)}) async-start(bf16[16,72,1024]{2,1,0:T(8,128)(2,1)} %bitcast.31), calls=%async_computation.1 | async-start | bytes 4718592 | tf_op jit(solution)/shard_map/all_to_all | solution.py:427
  126.5 3.1 fusion.90
  129.6 26.3 %all-to-all-done.1 = bf16[16,72,1024]{2,1,0:T(8,128)(2,1)} async-done(((bf16[16,72,1024]{2,1,0:T(8,128)(2,1)}), bf16[16,72,1024]{2,1,0:T(8,128)(2,1)}, u32[]{:S(2)}, u32[]{:S(2)}) %all-to-all-start.1) | async-done | bytes 2359328 | tf_op jit(solution)/shard_map/all_to_all | solution.py:427
  155.9 3.2 fusion.97
  159.1 3.2 fusion.96
  162.3 3.4 multiply_convert_fusion
  165.7 1.4 fusion.98
  167.2 2.9 fusion.4
  170.1 4.9 %all-to-all-start.3 = ((bf16[16,72,1024]{2,1,0:T(8,128)(2,1)}), bf16[16,72,1024]{2,1,0:T(8,128)(2,1)S(1)}, u32[]{:S(2)}, u32[]{:S(2)}) async-start(bf16[16,72,1024]{2,1,0:T(8,128)(2,1)} %bitcast.39), calls=%async_computation.3 | async-start | bytes 4718592 | tf_op jit(solution)/shard_map/all_to_all | solution.py:445
  175.0 4.4 %convolution_convert_fusion = bf16[1152,1024]{1,0:T(8,128)(2,1)} fusion(bf16[1152,512]{1,0:T(8,128)(2,1)} %get-tuple-element.46, bf16[1024,512]{1,0:T(8,128)(2,1)} %bitcast.231), kind=kOutput, calls=%fused_computation.11 | convolution fusion | flops 1209139200 | bytes 4587520 | tf_op jit(solution)/shard_map/cf,df->cd/dot_general | solution.py:435
  179.4 25.0 %all-to-all-done.3 = bf16[16,72,1024]{2,1,0:T(8,128)(2,1)S(1)} async-done(((bf16[16,72,1024]{2,1,0:T(8,128)(2,1)}), bf16[16,72,1024]{2,1,0:T(8,128)(2,1)S(1)}, u32[]{:S(2)}, u32[]{:S(2)}) %all-to-all-start.3) | async-done | bytes 2359328 | tf_op jit(solution)/shard_map/all_to_all | solution.py:445
  204.4 1.5 copy-done.4
  205.9 4.9 %all-to-all-start.2 = ((bf16[16,72,1024]{2,1,0:T(8,128)(2,1)}), bf16[16,72,1024]{2,1,0:T(8,128)(2,1)S(1)}, u32[]{:S(2)}, u32[]{:S(2)}) async-start(bf16[16,72,1024]{2,1,0:T(8,128)(2,1)} %bitcast.224), calls=%async_computation.2 | async-start | bytes 4718592 | tf_op jit(solution)/shard_map/all_to_all | solution.py:448
  211.1 4.7 %convolution_convert_fusion.2 = bf16[1024,512]{1,0:T(8,128)(2,1)} fusion(bf16[1152,1024]{1,0:T(8,128)(2,1)} %bitcast.267, bf16[1152,512]{1,0:T(8,128)(2,1)} %get-tuple-element.46), kind=kOutput, calls=%fused_computation.36 | convolution fusion | flops 1208483840 | bytes 4587520 | tf_op jit(solution)/shard_map/cd,cf->df/dot_general | solution.py:455
  217.7 3.6 convolution_convert_fusion.3
  221.3 3.3 convolution_convert_fusion.4
  224.7 2.0 pad_maximum_fusion.experts
  226.7 19.9 %all-to-all-done.2 = bf16[16,72,1024]{2,1,0:T(8,128)(2,1)S(1)} async-done(((bf16[16,72,1024]{2,1,0:T(8,128)(2,1)}), bf16[16,72,1024]{2,1,0:T(8,128)(2,1)S(1)}, u32[]{:S(2)}, u32[]{:S(2)}) %all-to-all-start.2) | async-done | bytes 2359328 | tf_op jit(solution)/shard_map/all_to_all | solution.py:448
  246.6 1.9 fusion.8
  248.9 1.2 fusion.18
  250.2 1.4 fusion.47
  251.6 1.4 fusion.15
  253.1 3.1 fusion.27
  257.5 1.2 fusion.2
  261.5 1.7 convolution_convert_fusion.6
  263.2 7.2 %all-to-all-start.4 = ((bf16[4,128,1024]{2,1,0:T(8,128)(2,1)}), bf16[4,128,1024]{2,1,0:T(8,128)(2,1)}, u32[]{:S(2)}, u32[]{:S(2)}) async-start(bf16[4,128,1024]{2,1,0:T(8,128)(2,1)} %bitcast.229), calls=%async_computation.4 | async-start | bytes 2097152 | tf_op jit(solution)/shard_map/all_to_all | solution.py:515
  271.0 1.2 convolution_convert_fusion.7.branch
  272.3 2.8 convolution_convert_fusion.5
  275.1 7.9 %all-to-all-done.4 = bf16[4,128,1024]{2,1,0:T(8,128)(2,1)} async-done(((bf16[4,128,1024]{2,1,0:T(8,128)(2,1)}), bf16[4,128,1024]{2,1,0:T(8,128)(2,1)}, u32[]{:S(2)}, u32[]{:S(2)}) %all-to-all-start.4) | async-done | bytes 1048608 | tf_op jit(solution)/shard_map/all_to_all | solution.py:515
  283.0 1.5 convert_reduce_fusion
  284.9 1.5 copy.123
  286.4 77.4 %scatter_all.1 = (bf16[32,32,640]{2,1,0:T(8,128)(2,1)}, bf16[32,16,512]{2,1,0:T(8,128)(2,1)}, bf16[32,3,32,512]{3,2,1,0:T(8,128)(2,1)}) custom-call(bf16[32,32,640]{2,1,0:T(8,128)(2,1)} %bitcast.209, bf16[256,1024]{1,0:T(8,128)(2,1)} %convolution_convert_fusion.7.branch, bf16[3,32,32,512]{3,2,1,0:T(8,128)(2,1)} %pad_maximum_fusion.experts), custom_call_target="tpu_custom_call" | custom-call | tf_op jit(solution)/shard_map/scatter_all/pallas_call | solution.py:71
  363.9 2.1 reduce_sum.181.heads
  366.0 1.7 reduce_sum.182.branch
  367.8 3.4 reduce.3.experts
  371.1 47.5 %share_all.1 = (bf16[2,2,32,640]{3,2,1,0:T(8,128)(2,1)}, bf16[4,16,512]{2,1,0:T(8,128)(2,1)}, bf16[2,2,4,3,32,512]{5,4,3,2,1,0:T(8,128)(2,1)}) custom-call(bf16[32,640]{1,0:T(8,128)(2,1)} %reduce_sum.181.heads, bf16[16,512]{1,0:T(8,128)(2,1)} %reduce_sum.182.branch, bf16[4,3,32,512]{3,2,1,0:T(8,128)(2,1)} %reduce.3.experts), custom_call_target="tpu_custom_call" | custom-call | tf_op jit(solution)/shard_map/share_all/pallas_call | solution.py:539
  425.8 1.3 squeeze.56
  427.9 1.3 squeeze.55
  429.9 1.3 squeeze.54
  (181 shorter events, 31.1 us)
Async XLA Ops:
  7.2 4.4 %copy-start = (bf16[32,1024]{1,0:T(8,128)(2,1)S(1)}, bf16[32,1024]{1,0:T(8,128)(2,1)}, u32[]{:S(2)}) copy-start(bf16[32,1024]{1,0:T(8,128)(2,1)} %param.18) | copy-start | bytes 196612
  7.2 2.6 copy-start.33
  7.2 2.8 copy-start.34
  9.4 2.2 copy-start.43
  9.4 2.2 copy-start.44
  10.0 3.9 copy-start.10
  12.7 105.1 %copy-start.13 = (pred[128,1152]{1,0:T(32,128)(4,1)}, pred[128,1152]{1,0:T(32,128)(4,1)S(1)}, u32[]{:S(2)}) copy-start(pred[128,1152]{1,0:T(32,128)(4,1)S(1)} %convolution_compare_fusion) | copy-start | bytes 442372
  97.0 3.1 copy-start.7
  100.4 2.5 copy-start.21
  102.8 2.8 copy-start.31
  103.4 1.6 copy-start.35
  104.1 0.9 copy-start.26
  105.0 1.9 copy-start.2
  107.8 9.1 %all-to-all-start = ((bf16[4,128,256]{1,2,0:T(8,128)(2,1)}), bf16[4,128,256]{1,2,0:T(8,128)(2,1)S(1)}, u32[]{:S(2)}, u32[]{:S(2)}) async-start(bf16[4,128,256]{1,2,0:T(8,128)(2,1)} %copy.118), calls=%async_computation | async-start | bytes 524288 | tf_op jit(solution)/shard_map/all_to_all | solution.py:417
  114.8 2.8 copy-start.8
  120.0 35.8 %all-to-all-start.1 = ((bf16[16,72,1024]{2,1,0:T(8,128)(2,1)}), bf16[16,72,1024]{2,1,0:T(8,128)(2,1)}, u32[]{:S(2)}, u32[]{:S(2)}) async-start(bf16[16,72,1024]{2,1,0:T(8,128)(2,1)} %bitcast.31), calls=%async_computation.1 | async-start | bytes 4718592 | tf_op jit(solution)/shard_map/all_to_all | solution.py:427
  129.6 32.7 %copy-start.28 = (bf16[1,2,4,4,32,512]{5,4,3,2,1,0:T(8,128)(2,1)}, bf16[1,2,4,4,32,512]{5,4,3,2,1,0:T(8,128)(2,1)S(1)}, u32[]{:S(2)}) copy-start(bf16[1,2,4,4,32,512]{5,4,3,2,1,0:T(8,128)(2,1)S(1)} %get-tuple-element.50) | copy-start | bytes 3145732
  155.9 3.2 copy-start.30
  159.0 3.2 copy-start.45
  165.7 1.4 copy-start.46
  165.7 1.4 copy-start.20
  170.1 34.4 %all-to-all-start.3 = ((bf16[16,72,1024]{2,1,0:T(8,128)(2,1)}), bf16[16,72,1024]{2,1,0:T(8,128)(2,1)S(1)}, u32[]{:S(2)}, u32[]{:S(2)}) async-start(bf16[16,72,1024]{2,1,0:T(8,128)(2,1)} %bitcast.39), calls=%async_computation.3 | async-start | bytes 4718592 | tf_op jit(solution)/shard_map/all_to_all | solution.py:445
  204.4 1.5 copy-start.4
  205.9 40.7 %all-to-all-start.2 = ((bf16[16,72,1024]{2,1,0:T(8,128)(2,1)}), bf16[16,72,1024]{2,1,0:T(8,128)(2,1)S(1)}, u32[]{:S(2)}, u32[]{:S(2)}) async-start(bf16[16,72,1024]{2,1,0:T(8,128)(2,1)} %bitcast.224), calls=%async_computation.2 | async-start | bytes 4718592 | tf_op jit(solution)/shard_map/all_to_all | solution.py:448
  210.8 39.3 %all-gather.2.cloned.1.call-start = ((), (), s32[]{:S(2)}) async-start(), calls=%async_computation.5 | async-start | bytes 1310720 | tf_op jit(solution)/shard_map/all_gather | solution.py:472
  211.1 4.7 %copy-start.5 = (bf16[16,72,1024]{2,1,0:T(8,128)(2,1)S(1)}, bf16[16,72,1024]{2,1,0:T(8,128)(2,1)}, u32[]{:S(2)}) copy-start(bf16[16,72,1024]{2,1,0:T(8,128)(2,1)} %copy-done.4) | copy-start | bytes 7077892
  211.1 4.7 %copy-start.14 = (pred[128,1152]{1,0:T(32,128)(4,1)S(1)}, pred[128,1152]{1,0:T(32,128)(4,1)}, u32[]{:S(2)}) copy-start(pred[128,1152]{1,0:T(32,128)(4,1)} %copy-done.13) | copy-start | bytes 442372
  215.8 0.9 copy-start.11
  217.7 3.6 copy-start.47
  221.3 3.3 copy-start.29
  246.6 2.3 copy-start.37
  253.1 3.5 copy-start.3
  253.1 3.4 copy-start.32
  256.5 4.3 copy-start.40
  257.5 1.2 copy-start.27
  259.6 1.0 copy-start.18
  260.1 1.3 copy-start.39
  260.8 2.4 copy-start.41
  261.5 9.6 %copy-start.6 = (bf16[512,1024]{1,0:T(8,128)(2,1)S(1)}, bf16[512,1024]{1,0:T(8,128)(2,1)}, u32[]{:S(2)}) copy-start(bf16[512,1024]{1,0:T(8,128)(2,1)} %all-gather.2.cloned.1.call-done) | copy-start | bytes 3145732
  261.5 9.6 %copy-start.24 = (bf16[2,64,2,512]{3,1,2,0:T(8,128)(2,1)S(1)}, bf16[2,64,2,512]{3,1,2,0:T(8,128)(2,1)}, u32[]{:S(2)}) copy-start(bf16[2,64,2,512]{3,1,2,0:T(8,128)(2,1)} %copy-done.23) | copy-start | bytes 786436
  263.2 9.1 %copy-start.22 = (bf16[512,1024]{1,0:T(8,128)(2,1)S(1)}, bf16[512,1024]{1,0:T(8,128)(2,1)}, u32[]{:S(2)}) copy-start(bf16[512,1024]{1,0:T(8,128)(2,1)} %copy-done.21) | copy-start | bytes 3145732
  263.2 19.8 %all-to-all-start.4 = ((bf16[4,128,1024]{2,1,0:T(8,128)(2,1)}), bf16[4,128,1024]{2,1,0:T(8,128)(2,1)}, u32[]{:S(2)}, u32[]{:S(2)}) async-start(bf16[4,128,1024]{2,1,0:T(8,128)(2,1)} %bitcast.229), calls=%async_computation.4 | async-start | bytes 2097152 | tf_op jit(solution)/shard_map/all_to_all | solution.py:515
  272.3 12.3 %copy-start.9 = (bf16[128,1024]{1,0:T(8,128)(2,1)S(1)}, bf16[128,1024]{1,0:T(8,128)(2,1)}, u32[]{:S(2)}) copy-start(bf16[128,1024]{1,0:T(8,128)(2,1)} %tokens.1) | copy-start | bytes 786436
  283.0 1.8 copy-start.25
  367.8 52.0 %copy-start.12 = (bf16[128,1024]{1,0:T(8,128)(2,1)S(1)}, bf16[128,1024]{1,0:T(8,128)(2,1)}, u32[]{:S(2)}) copy-start(bf16[128,1024]{1,0:T(8,128)(2,1)} %param.25) | copy-start | bytes 786436
  418.6 2.2 copy-start.42
  418.6 5.7 %copy-start.19 = (bf16[2,2,4,3,32,512]{5,4,3,2,1,0:T(8,128)(2,1)S(1)}, bf16[2,2,4,3,32,512]{5,4,3,2,1,0:T(8,128)(2,1)}, u32[]{:S(2)}) copy-start(bf16[2,2,4,3,32,512]{5,4,3,2,1,0:T(8,128)(2,1)} %get-tuple-element.33) | copy-start | bytes 4718596
  427.8 3.4 copy-start.1
  (6 other events, 4.7 us)
Sparse Core Ops, SparseCore 0:
  217.8 29.7 all-gather.1

commit v2 on v1

--- a/solution.py
+++ b/solution.py
@@ -92,9 +92,17 @@
     return copies
 
 
+def group_of(x, z, seq, yh):
+    yl, core = seq // 2, seq % 2
+    return [
+        (yh, x, (z + k // 4) % 4, (yl + (k // 2) % 2) % 2 * 2 + (core + k % 2) % 2)
+        for k in range(1, 16)
+    ]
+
+
 def gather_kernel(
     heads, branch, tokens, experts, rows,
-    heads_all, branch_all, tokens_all, experts_all, rows_all,
+    heads_all, branch_all, tokens_all, gate_all, rest_all, rows_all,
     send, recv, local,
 ):
     yh, x, z, seq = place()
@@ -102,113 +110,168 @@
     along_y = (1 - yh, x, z, seq)
     along_x = [(yh, (x + k) % 4, z, seq) for k in (1, 2, 3)]
     along_z = [(yh, x, (z + k) % 4, seq) for k in (1, 2, 3)]
-    group = [
-        (yh, x, (z + k // 4) % 4, (yl + (k // 2) % 2) % 2 * 2 + (core + k % 2) % 2)
-        for k in range(1, 16)
-    ]
     near = (yh, x, z, (1 - yl) * 2 + core)
     sibling = (yh, x, z, yl * 2 + 1 - core)
+    group = group_of(x, z, seq, yh)
     expert = z * 4 + seq
     greet([along_y] + along_x + group)
-    own = local_starts(
-        [
-            (heads, heads_all.at[yh, x, z]),
-            (branch, branch_all.at[core, yh, x, z]),
-            (tokens, tokens_all.at[yl, core]),
-            (experts.at[z], experts_all.at[:, yh, x, z]),
-            (rows.at[expert], rows_all.at[expert]),
-        ],
-        local,
-    )
     sender = Sender(send, recv)
     first = [
         sender.start(heads, heads_all.at[yh, x, z], along_y),
         sender.start(branch, branch_all.at[core, yh, x, z], along_y),
     ]
-    expert_first = [
-        sender.start(experts.at[(z + k) % 4], experts_all.at[:, yh, x, z], along_z[k - 1])
-        for k in (1, 2, 3)
-    ]
+    expert_first = []
+    for partner in along_z:
+        block = experts.at[partner[2]]
+        expert_first.append(sender.start(block.at[0], gate_all.at[yh, x, z], partner))
+        expert_first.append(
+            sender.start(block.at[pl.ds(1, 2)], rest_all.at[:, yh, z], partner)
+        )
     token_copies = [
         sender.start(tokens, tokens_all.at[yl, core], near),
         sender.start(tokens, tokens_all.at[yl, core], sibling),
     ]
-    for copy in own:
+    own = local_starts(
+        [
+            (heads, heads_all.at[yh, x, z]),
+            (branch, branch_all.at[core, yh, x, z]),
+            (experts.at[z, 0], gate_all.at[yh, x, z]),
+            (experts.at[z, pl.ds(1, 2)], rest_all.at[:, yh, z]),
+            (tokens, tokens_all.at[yl, core]),
+            (rows.at[expert], rows_all.at[expert]),
+        ],
+        local,
+    )
+    for copy in own[:2]:
         copy.wait()
     arrived(first)
     second = []
-    for k in range(3):
-        for source in (heads_all.at[:, x, z, 0], branch_all.at[core, :, x, z, 0]):
-            second.append(sender.start(source, source, along_x[k]))
-        for source in (heads_all.at[:, x, z, 1], branch_all.at[core, :, x, z, 1]):
-            second.append(sender.start(source, source, along_z[k]))
+    for partner in along_z:
+        for source in (heads_all.at[:, x, z], branch_all.at[core, :, x, z]):
+            second.append(sender.start(source, source, partner))
+    for copy in own[2:4]:
+        copy.wait()
     arrived(expert_first)
-    mine = experts_all.at[:, yh, x]
-    expert_second = [sender.start(mine, mine, along_y)]
+    mine, rest = gate_all.at[yh, x], rest_all.at[:, yh]
+    expert_second = [
+        sender.start(mine, mine, along_y),
+        sender.start(rest, rest, along_y),
+    ]
     arrived(second)
     third = []
-    for k in range(3):
-        for source in (heads_all.at[:, :, z, 0], branch_all.at[core, :, :, z, 0]):
-            third.append(sender.start(source, source, along_z[k]))
-        for source in (heads_all.at[:, x, :, 1], branch_all.at[core, :, x, :, 1]):
-            third.append(sender.start(source, source, along_x[k]))
-    arrived(expert_second)
-    mine = experts_all.at[:, :, x]
-    expert_third = [sender.start(mine, mine, along_x[k]) for k in range(3)]
+    for partner in along_x:
+        for source in (heads_all.at[:, x], branch_all.at[core, :, x]):
+            third.append(sender.start(source, source, partner))
     row_copies = []
     for partner in group:
         other = partner[2] * 4 + partner[3]
         row_copies.append(sender.start(rows.at[other], rows_all.at[expert], partner))
+    arrived(expert_second)
+    mine = gate_all.at[:, x]
+    expert_third = [sender.start(mine, mine, partner) for partner in along_x]
     arrived(token_copies)
     far = tokens_all.at[1 - yl, core]
     last = [sender.start(far, far, sibling)]
     arrived(third)
     half = branch_all.at[core]
     last.append(sender.start(half, half, sibling))
+    for copy in own[4:]:
+        copy.wait()
     arrived(expert_third)
     arrived(row_copies)
     arrived(last)
     sender.finish()
 
 
-def scatter_kernel(
-    heads, branch, experts,
-    heads_all, branch_all, experts_all,
-    send, recv, local,
-):
+def dispatch_kernel(rows, rest, rows_all, rest_all, send, recv, local):
     yh, x, z, seq = place()
-    dp = yh * 16 + x * 4 + z
-
-    def branch_block(index):
-        top = pl.multiple_of(index // 2 * 16, 16)
-        left = pl.multiple_of(index % 2 * 512, 512)
-        return branch.at[pl.ds(top, 16), pl.ds(left, 512)]
-
-    others = [(dp + k) % 32 for k in range(1, 32)]
-    partners = [(other // 16, other // 4 % 4, other % 4, seq) for other in others]
-    greet(partners)
+    along_x = [(yh, (x + k) % 4, z, seq) for k in (1, 2, 3)]
+    group = group_of(x, z, seq, yh)
+    expert = z * 4 + seq
+    greet(along_x + group)
+    sender = Sender(send, recv)
+    for partner in group:
+        other = partner[2] * 4 + partner[3]
+        sender.start(rows.at[other], rows_all.at[expert], partner)
+    for partner in along_x:
+        sender.start(rest, rest_all.at[:, :, x], partner)
     own = local_starts(
-        [
-            (heads.at[dp], heads_all.at[dp]),
-            (branch_block(dp), branch_all.at[dp]),
-            (experts.at[:, dp], experts_all.at[dp]),
-        ],
-        local,
-    )
-    sender = Sender(send, recv)
-    for other, partner in zip(others, partners):
-        sender.start(experts.at[:, other], experts_all.at[dp], partner)
-        sender.start(heads.at[other], heads_all.at[dp], partner)
-        sender.start(branch_block(other), branch_all.at[dp], partner)
+        [(rows.at[expert], rows_all.at[expert]), (rest, rest_all.at[:, :, x])], local
+    )
     for copy in own:
         copy.wait()
     arrived(sender.copies)
     sender.finish()
 
 
-def share_kernel(
+def trade_kernel(blocks, blocks_all, send, recv, local):
+    yh, x, z, seq = place()
+    partners = [(yh, x, z, (seq + k) % 4) for k in (1, 2, 3)]
+    greet(partners)
+    own = local_starts([(blocks.at[seq], blocks_all.at[seq])], local)
+    sender = Sender(send, recv)
+    for partner in partners:
+        sender.start(blocks.at[partner[3]], blocks_all.at[seq], partner)
+    own[0].wait()
+    arrived(sender.copies)
+    sender.finish()
+
+
+def spread_kernel(block, blocks_all, send, recv, local):
+    yh, x, z, seq = place()
+    yl, core = seq // 2, seq % 2
+    near = (yh, x, z, (1 - yl) * 2 + core)
+    sibling = (yh, x, z, yl * 2 + 1 - core)
+    greet([near, sibling])
+    sender = Sender(send, recv)
+    first = [
+        sender.start(block, blocks_all.at[yl, core], near),
+        sender.start(block, blocks_all.at[yl, core], sibling),
+    ]
+    own = local_starts([(block, blocks_all.at[yl, core])], local)
+    arrived(first[:1])
+    far = blocks_all.at[1 - yl, core]
+    last = sender.start(far, far, sibling)
+    arrived(first[1:])
+    own[0].wait()
+    arrived([last])
+    sender.finish()
+
+
+def gather_sums(parts):
+    total = parts[0].astype(F32)
+    for part in parts[1:]:
+        total = total + part.astype(F32)
+    return total
+
+
+def trade_sum_kernel(parts, total, arriving, paired, outgoing, incoming, send, recv):
+    yh, x, z, seq = place()
+    yl, core = seq // 2, seq % 2
+    near = (yh, x, z, (1 - yl) * 2 + core)
+    sibling = (yh, x, z, yl * 2 + 1 - core)
+    greet([near, sibling])
+    sender = Sender(send, recv)
+    first = [
+        sender.start(parts.at[1 - yl, 1 - core], arriving.at[0], sibling),
+        sender.start(parts.at[yl, 1 - core], arriving.at[1], sibling),
+    ]
+    arrived(first[:1])
+    outgoing[...] = gather_sums([parts[1 - yl, core], arriving[0]]).astype(BF16)
+    last = sender.start(outgoing, incoming, near)
+    arrived(first[1:])
+    paired[...] = gather_sums([parts[yl, core], arriving[1]])
+    arrived([last])
+    total[...] = paired[...] + incoming[...].astype(F32)
+    sender.finish()
+
+
+def finish_kernel(
     heads, branch, experts,
-    heads_all, branch_all, experts_all,
+    heads_four, branch_four, experts_four,
+    heads_x, branch_x, heads_out, branch_out,
+    heads_plane, branch_plane, experts_plane,
+    heads_sum, branch_sum, experts_sum,
     send, recv, local, branch_sends, branch_recvs,
 ):
     yh, x, z, seq = place()
@@ -216,13 +279,15 @@
     dp = yh * 16 + x * 4 + z
     near = (yh, x, z, (1 - yl) * 2 + core)
     sibling = (yh, x, z, yl * 2 + 1 - core)
+    along_x = [(yh, (x + k) % 4, z, seq) for k in (1, 2, 3)]
+    plane = [((yh + k // 4) % 2, x, (z + k % 4) % 4, seq) for k in range(1, 8)]
     owner = seq * 8 + dp // 4
     source_seq = dp // 8
     slot = dp % 4
+    here = owner == dp
     barrier = pltpu.get_barrier_semaphore()
-    for partner in (near, sibling):
+    for partner in [near, sibling] + along_x + plane:
         pl.semaphore_signal(barrier, inc=1, device_id=partner, device_id_type=BY_ID)
-    here = jnp.logical_and(owner == dp, True)
     for k in range(4):
         maker = dp % 8 * 4 + k
         foreign = jnp.logical_or(maker != dp, source_seq != seq)
@@ -236,20 +301,59 @@
                 device_id_type=BY_ID,
             )
 
-    pl.semaphore_wait(barrier, 6 - here.astype(jnp.int32))
-    own = local_starts(
-        [(heads, heads_all.at[yl, core]), (experts, experts_all.at[yl, core])], local
-    )
+    pl.semaphore_wait(barrier, 16 - here.astype(jnp.int32))
     sender = Sender(send, recv)
     first = []
+    for k, partner in enumerate(along_x):
+        first.append(sender.start(heads.at[:, partner[1]], heads_x.at[k], partner))
+        first.append(sender.start(branch.at[:, partner[1]], branch_x.at[k], partner))
+    across = []
+    for k, partner in enumerate(plane):
+        across.append(
+            sender.start(experts.at[partner[0], partner[2]], experts_plane.at[yh, z], partner)
+        )
+    arrived(first)
+    for y in range(2):
+        for j in range(4):
+            heads_out[y, j] = gather_sums(
+                [heads[y, x, j]] + [heads_x[k, y, j] for k in range(3)]
+            ).astype(BF16)
+        total = gather_sums([branch[y, x]] + [branch_x[k, y] for k in range(3)]).astype(BF16)
+        for j in range(4):
+            branch_out[y, j] = total[j // 2 * 16 : j // 2 * 16 + 16, j % 2 * 512 : j % 2 * 512 + 512]
+    second = []
+    for k, partner in enumerate(plane):
+        second.append(sender.start(heads_out.at[partner[0], partner[2]], heads_plane.at[k], partner))
+        second.append(
+            sender.start(branch_out.at[partner[0], partner[2]], branch_plane.at[k], partner)
+        )
+    arrived(across)
+    for j in range(4):
+        @pl.when(z == j)
+        def _():
+            experts_sum[j] = gather_sums([experts[yh, j], experts_plane[1 - yh, j]]).astype(BF16)
+
+        @pl.when(z != j)
+        def _():
+            experts_sum[j] = gather_sums([experts_plane[0, j], experts_plane[1, j]]).astype(BF16)
+
+    third = []
     for partner in (near, sibling):
-        first.append(sender.start(heads, heads_all.at[yl, core], partner))
-        first.append(sender.start(experts, experts_all.at[yl, core], partner))
-    place_of = branch_all.at[slot]
+        third.append(sender.start(experts_sum, experts_four.at[yl, core], partner))
+    own = local_starts([(experts_sum, experts_four.at[yl, core])], local)
+    arrived(second)
+    heads_sum[...] = gather_sums([heads_out[yh, z]] + [heads_plane[k] for k in range(7)]).astype(BF16)
+    branch_sum[...] = gather_sums(
+        [branch_out[yh, z]] + [branch_plane[k] for k in range(7)]
+    ).astype(BF16)
+    fourth = []
+    for partner in (near, sibling):
+        fourth.append(sender.start(heads_sum, heads_four.at[yl, core], partner))
+    place_of = branch_four.at[slot]
 
     def branch_copy(k):
         return pltpu.make_async_remote_copy(
-            src_ref=branch,
+            src_ref=branch_sum,
             dst_ref=place_of,
             send_sem=branch_sends.at[k],
             recv_sem=branch_recvs.at[slot],
@@ -266,19 +370,23 @@
 
         @pl.when(self_copy)
         def _():
-            pltpu.make_async_copy(branch, place_of, branch_recvs.at[slot]).start()
-
-    for copy in own:
-        copy.wait()
-    arrived(first[:2])
-    last = []
-    for buffer in (heads_all, experts_all):
-        far = buffer.at[1 - yl, core]
-        last.append(sender.start(far, far, sibling))
-    arrived(first[2:])
+            pltpu.make_async_copy(branch_sum, place_of, branch_recvs.at[slot]).start()
+
+    own_heads = pltpu.make_async_copy(heads_sum, heads_four.at[yl, core], local.at[1])
+    own_heads.start()
+    arrived(third[:1])
+    far = experts_four.at[1 - yl, core]
+    last = [sender.start(far, far, sibling)]
+    arrived(fourth[:1])
+    far = heads_four.at[1 - yl, core]
+    last.append(sender.start(far, far, sibling))
+    arrived(third[1:])
+    arrived(fourth[1:])
+    own[0].wait()
+    own_heads.wait()
     arrived(last)
     for k in range(4):
-        pltpu.make_async_copy(branch, branch_all.at[k], branch_recvs.at[k]).wait()
+        pltpu.make_async_copy(branch_sum, branch_four.at[k], branch_recvs.at[k]).wait()
         self_copy = jnp.logical_and(here, seq == k)
 
         @pl.when(jnp.logical_not(self_copy))
@@ -286,6 +394,52 @@
             branch_copy(k).wait_send()
 
     sender.finish()
+
+
+def unpack_kernel(heads, branch, experts, query, key, value, output, gate, up, down):
+    for s in range(4):
+        block = heads[s // 2, s % 2].astype(F32)
+        query[:, s * 256 : s * 256 + 256] = block[:, :256]
+        key[:, s * 128 : s * 128 + 128] = block[:, 256:384]
+        value[:, s * 128 : s * 128 + 128] = block[:, 384:512]
+        rows, columns = s // 2 * 16, s % 2 * 512
+        output[rows : rows + 16, columns : columns + 512] = branch[s].astype(F32)
+        for j in range(4):
+            block = experts[s // 2, s % 2, j].astype(F32)
+            for index, result in enumerate((gate, up, down)):
+                result[:, j * 4 + s, :] = block[:, index * 512 : index * 512 + 512]
+
+
+def expert_kernel(
+    rows, back, gate_w, up_w, down_w, grad_rows, returned, active, grad_gate, grad_up
+):
+    gate_pre = jnp.dot(rows[...], gate_w[...], preferred_element_type=F32)
+    up_pre = jnp.dot(rows[...], up_w[...], preferred_element_type=F32)
+    grad_active = jnp.dot(back[...], down_w[...], preferred_element_type=F32)
+    sigmoid_gate = jax.nn.sigmoid(gate_pre)
+    silu = gate_pre * sigmoid_gate
+    act = (silu * up_pre).astype(BF16)
+    slope = sigmoid_gate * (1.0 + gate_pre * (1.0 - sigmoid_gate))
+    by_gate = (grad_active * up_pre * slope).astype(BF16)
+    by_up = (grad_active * silu).astype(BF16)
+    active[...] = act
+    grad_gate[...] = by_gate
+    grad_up[...] = by_up
+    turned_dims = (((1,), (1,)), ((), ()))
+    grad_rows[...] = (
+        lax.dot_general(by_gate, gate_w[...], turned_dims, preferred_element_type=F32)
+        + lax.dot_general(by_up, up_w[...], turned_dims, preferred_element_type=F32)
+    ).astype(BF16)
+    returned[...] = lax.dot_general(
+        act, down_w[...], turned_dims, preferred_element_type=F32
+    ).astype(BF16)
+
+
+def expert_grad_kernel(rows, back, active, grad_gate, grad_up, result):
+    first_dims = (((0,), (0,)), ((), ()))
+    for index, (left, right) in enumerate(((rows, grad_gate), (rows, grad_up), (back, active))):
+        total = lax.dot_general(left[...], right[...], first_dims, preferred_element_type=F32)
+        result[:, 0, :, index * 512 : index * 512 + 512] = total.astype(BF16).reshape(4, TOK, 512)
 
 
 def angles(count, head_dim):
@@ -336,6 +490,11 @@
     return (named, spread, hits.astype(BF16), weights)
 
 
+def to_group(rows):
+    blocks = rows.reshape(EXPERTS, CAP, MODEL_WIDTH)
+    return lax.all_to_all(blocks, ("z", "seq"), 0, 0, tiled=True).reshape(SLOTS, MODEL_WIDTH)
+
+
 def shards(
     layer_in, norm_one, w_query, key_weight, value_weight, w_output, norm_two,
     w_gate, w_up, w_down, routes, route_gates, cotangent,
@@ -356,8 +515,8 @@
             gains,
         ],
         axis=1,
-    ).reshape(2, 16, 640)
-    branch_block = lax.dynamic_slice_in_dim(w_output, core * 512, 512, 1).reshape(2, 16, 512)
+    )
+    branch_block = lax.dynamic_slice_in_dim(w_output, core * 512, 512, 1)
     expert_block = jnp.stack(
         [
             lax.dynamic_index_in_dim(w.reshape(32, 4, 4, FF), seq, 2, keepdims=False)
@@ -371,18 +530,19 @@
         * slot_weights[:, None]
     ).astype(BF16).reshape(EXPERTS, CAP, MODEL_WIDTH)
 
-    heads_w, branch_w, tokens_all, expert_w, grad_returned = remote_call(
+    heads_w, branch_w, tokens_all, gate_w, rest_w, grad_back = remote_call(
         gather_kernel,
         (heads_block, branch_block, layer_in, expert_block, grad_slots),
         (
-            (2, 4, 4, 2, 16, 640),
-            (2, 2, 4, 4, 2, 16, 512),
+            (2, 4, 4, 32, 640),
+            (2, 2, 4, 4, 32, 512),
             (2, 2, TOK, MODEL_WIDTH),
-            (3, 2, 4, 4, 32, FF),
+            (2, 4, 4, 32, FF),
+            (2, 2, 4, 32, FF),
             (EXPERTS, CAP, MODEL_WIDTH),
         ),
-        52,
-        5,
+        48,
+        6,
         1,
         "gather_all",
     )
@@ -391,8 +551,8 @@
     gain_second = heads_w[:, 513].astype(F32)
     heads_w = heads_w[:, :512]
     branch_w = branch_w.reshape(2, MODEL_WIDTH, 512)
-    expert_w = expert_w.reshape(3, MODEL_WIDTH, FF)
-    grad_back = grad_returned.reshape(SLOTS, MODEL_WIDTH)
+    gate_w = gate_w.reshape(MODEL_WIDTH, FF)
+    grad_back = grad_back.reshape(SLOTS, MODEL_WIDTH)
 
     sequence = tokens_all.reshape(SEQ_LEN, MODEL_WIDTH).astype(F32)
     factor_all = lax.rsqrt(jnp.mean(sequence * sequence, axis=-1, keepdims=True) + EPSILON)
@@ -414,7 +574,10 @@
     log_sums = top_score + jnp.log(total_mass)
     attended = jnp.einsum("kgqs,skd->qkgd", probs, value_all, preferred_element_type=F32)
     attended = attended.reshape(SEQ_LEN, head_width).astype(BF16)
-    attended_tok = lax.all_to_all(attended, "seq", split_axis=0, concat_axis=1, tiled=True)
+    (attended_tok,) = remote_call(
+        trade_kernel, (attended.reshape(4, TOK, head_width),), ((4, TOK, head_width),), 3, 1, 4, "trade_heads"
+    )
+    attended_tok = attended_tok.transpose(1, 0, 2).reshape(TOK, MODEL_WIDTH)
 
     inputs = layer_in.astype(F32)
     branch = jnp.concatenate(
@@ -424,52 +587,62 @@
     factor_two = lax.rsqrt(jnp.mean(middle * middle, axis=-1, keepdims=True) + EPSILON)
     normed_two = (middle * factor_two * gain_second).astype(BF16)
     slot_rows = jnp.einsum("tj,td->jd", hits, normed_two, preferred_element_type=F32).astype(BF16)
-    expert_rows = lax.all_to_all(
-        slot_rows.reshape(EXPERTS, CAP, MODEL_WIDTH), ("z", "seq"), 0, 0, tiled=True
-    ).reshape(SLOTS, MODEL_WIDTH)
-
-    gate_pre = jnp.dot(expert_rows, expert_w[0], preferred_element_type=F32)
-    up_pre = jnp.dot(expert_rows, expert_w[1], preferred_element_type=F32)
-    sigmoid_gate = jax.nn.sigmoid(gate_pre)
-    active = (gate_pre * sigmoid_gate * up_pre).astype(BF16)
-    returned = jnp.einsum("cf,df->cd", active, expert_w[2], preferred_element_type=F32)
-    grad_active = jnp.dot(grad_back, expert_w[2], preferred_element_type=F32)
-    grad_gate = (
-        grad_active * up_pre * sigmoid_gate * (1.0 + gate_pre * (1.0 - sigmoid_gate))
-    ).astype(BF16)
-    grad_up = (grad_active * gate_pre * sigmoid_gate).astype(BF16)
-    grad_rows = (
-        jnp.einsum("cf,df->cd", grad_gate, expert_w[0], preferred_element_type=F32)
-        + jnp.einsum("cf,df->cd", grad_up, expert_w[1], preferred_element_type=F32)
-    ).astype(BF16)
-    grad_rows = lax.all_to_all(
-        grad_rows.reshape(EXPERTS, CAP, MODEL_WIDTH), ("z", "seq"), 0, 0, tiled=True
-    ).reshape(SLOTS, MODEL_WIDTH)
-    returned = lax.all_to_all(
-        returned.astype(BF16).reshape(EXPERTS, CAP, MODEL_WIDTH), ("z", "seq"), 0, 0, tiled=True
-    ).reshape(SLOTS, MODEL_WIDTH)
-    expert_grads = jnp.stack(
-        [
-            jnp.einsum("cd,cf->df", expert_rows, grad_gate, preferred_element_type=F32).astype(BF16),
-            jnp.einsum("cd,cf->df", expert_rows, grad_up, preferred_element_type=F32).astype(BF16),
-            jnp.einsum("cd,cf->df", grad_back, active, preferred_element_type=F32).astype(BF16),
-        ]
-    ).reshape(3, 32, 32, FF)
+    expert_rows, rest_w = remote_call(
+        dispatch_kernel,
+        (slot_rows.reshape(EXPERTS, CAP, MODEL_WIDTH), rest_w),
+        ((EXPERTS, CAP, MODEL_WIDTH), (2, 2, 4, 4, 32, FF)),
+        18,
+        2,
+        7,
+        "dispatch_rows",
+    )
+    expert_rows = expert_rows.reshape(SLOTS, MODEL_WIDTH)
+    up_w = rest_w[0].reshape(MODEL_WIDTH, FF)
+    down_w = rest_w[1].reshape(MODEL_WIDTH, FF)
+
+    step = SLOTS // 3
+    wide = pl.BlockSpec((step, MODEL_WIDTH), lambda i: (i, 0))
+    narrow = pl.BlockSpec((step, FF), lambda i: (i, 0))
+    weight = pl.BlockSpec((MODEL_WIDTH, FF), lambda i: (0, 0))
+    grad_rows, returned, active, grad_gate, grad_up = pl.pallas_call(
+        expert_kernel,
+        grid=(3,),
+        out_shape=(jax.ShapeDtypeStruct((SLOTS, MODEL_WIDTH), BF16),) * 2
+        + (jax.ShapeDtypeStruct((SLOTS, FF), BF16),) * 3,
+        in_specs=[wide, wide, weight, weight, weight],
+        out_specs=(wide, wide, narrow, narrow, narrow),
+        compiler_params=pltpu.CompilerParams(vmem_limit_bytes=48 * 2**20),
+        name="expert_rows",
+    )(expert_rows, grad_back, gate_w, up_w, down_w)
+    grad_rows = to_group(grad_rows)
+    half = pl.BlockSpec((SLOTS, 512), lambda i: (0, i))
+    whole = pl.BlockSpec((SLOTS, FF), lambda i: (0, 0))
+    expert_grads = pl.pallas_call(
+        expert_grad_kernel,
+        grid=(2,),
+        out_shape=jax.ShapeDtypeStruct((4, 2, TOK, 3 * FF), BF16),
+        in_specs=[half, half, whole, whole, whole],
+        out_specs=pl.BlockSpec((4, 1, TOK, 3 * FF), lambda i: (0, i, 0, 0)),
+        compiler_params=pltpu.CompilerParams(vmem_limit_bytes=48 * 2**20),
+        name="expert_grads",
+    )(expert_rows, grad_back, active, grad_gate, grad_up)
+    x_place = lax.axis_index("x")
+    x_parts = [lax.dynamic_index_in_dim(expert_grads, x_place, 0, keepdims=False)]
+    for k in (1, 2, 3):
+        block = lax.dynamic_index_in_dim(expert_grads, (x_place + k) % 4, 0, keepdims=False)
+        x_parts.append(lax.ppermute(block, "x", [(i, (i + k) % 4) for i in range(4)]))
 
     grad_out = cotangent.astype(F32)
-    layer_out = (
-        middle + jnp.dot(weights.astype(BF16), returned, preferred_element_type=F32)
-    ).astype(BF16)
-    pair_dots = jnp.einsum("td,jd->tj", cotangent, returned, preferred_element_type=F32)
-    expert_dots = jnp.einsum(
-        "tj,ej->te", pair_dots * hits.astype(F32), spread, precision=lax.Precision.HIGHEST
-    )
-    grad_gates = RESIDUAL * jnp.sum(named * expert_dots[:, None, :], axis=-1)
     grad_normed_two = jnp.dot(hits, grad_rows, preferred_element_type=F32)
     grad_middle_norm, gain_two_term = norm_back(grad_normed_two, middle, factor_two, gain_second)
     grad_middle = grad_out + grad_middle_norm
     grad_branch = (RESIDUAL * grad_middle).astype(BF16)
-    grad_branch_all = lax.all_gather(grad_branch, "seq", axis=0, tiled=True)
+    (grad_branch_all,) = remote_call(
+        spread_kernel, (grad_branch,), ((2, 2, TOK, MODEL_WIDTH),), 3, 1, 5, "spread_branch"
+    )
+    returned, grad_branch_all = lax.optimization_barrier((returned, grad_branch_all))
+    returned = to_group(returned)
+    grad_branch_all = grad_branch_all.reshape(SEQ_LEN, MODEL_WIDTH)
     branch_rows = lax.dynamic_slice_in_dim(branch_w, seq * head_width, head_width, 1)
     output_term = jnp.einsum(
         "th,td->hd", attended, grad_branch_all, preferred_element_type=F32
@@ -512,10 +685,32 @@
     grad_normed_parts = jnp.einsum(
         "tf,df->td", grad_projected, heads_w, preferred_element_type=F32
     ).astype(BF16)
-    grad_normed_parts = lax.all_to_all(
-        grad_normed_parts.reshape(4, TOK, MODEL_WIDTH), "seq", 0, 0, tiled=True
-    )
-    grad_normed = jnp.sum(grad_normed_parts.astype(F32), axis=0)
+    block = (TOK, MODEL_WIDTH)
+    grad_normed = pl.pallas_call(
+        trade_sum_kernel,
+        out_shape=jax.ShapeDtypeStruct(block, F32),
+        in_specs=[pl.BlockSpec(memory_space=pltpu.VMEM)],
+        out_specs=pl.BlockSpec(memory_space=pltpu.VMEM),
+        scratch_shapes=[
+            pltpu.VMEM((2,) + block, BF16),
+            pltpu.VMEM(block, F32),
+            pltpu.VMEM(block, BF16),
+            pltpu.VMEM(block, BF16),
+            pltpu.SemaphoreType.DMA((3,)),
+            pltpu.SemaphoreType.DMA((3,)),
+        ],
+        compiler_params=pltpu.CompilerParams(
+            collective_id=6, has_side_effects=True, vmem_limit_bytes=16 * 2**20
+        ),
+        name="trade_normed",
+    )(grad_normed_parts.reshape(2, 2, TOK, MODEL_WIDTH))
+    x_parts, heads_term, grad_normed, returned = lax.optimization_barrier(
+        (x_parts, heads_term, grad_normed, returned)
+    )
+    expert_grads = (
+        x_parts[0].astype(F32) + x_parts[1].astype(F32)
+        + x_parts[2].astype(F32) + x_parts[3].astype(F32)
+    ).astype(BF16)
     factor_one = lax.rsqrt(jnp.mean(inputs * inputs, axis=-1, keepdims=True) + EPSILON)
     grad_input_norm, gain_one_term = norm_back(grad_normed, inputs, factor_one, gain_first)
     grad_input = (grad_middle + grad_input_norm).astype(BF16)
@@ -524,59 +719,75 @@
         jnp.stack([gain_one_term, gain_two_term], axis=1).astype(BF16), ((0, 0), (0, 126))
     )
     heads_term = jnp.concatenate([heads_term, gain_terms], axis=1).reshape(32, 32, 640)
-    heads_parts, branch_parts, expert_parts = remote_call(
-        scatter_kernel,
-        (heads_term, output_term, expert_grads),
-        ((32, 32, 640), (32, 16, 512), (32, 3, 32, FF)),
-        93,
-        3,
-        2,
-        "scatter_all",
-    )
-    heads_sum = jnp.sum(heads_parts.astype(F32), axis=0).astype(BF16)
-    branch_sum = jnp.sum(branch_parts.astype(F32), axis=0).astype(BF16)
-    expert_sum = jnp.sum(expert_parts.astype(F32).reshape(8, 4, 3, 32, FF), axis=0).astype(BF16)
+    any_place, vmem = pl.BlockSpec(memory_space=pl.ANY), pl.BlockSpec(memory_space=pltpu.VMEM)
     heads_four, branch_four, expert_four = pl.pallas_call(
-        share_kernel,
+        finish_kernel,
         out_shape=(
             jax.ShapeDtypeStruct((2, 2, 32, 640), BF16),
             jax.ShapeDtypeStruct((4, 16, 512), BF16),
-            jax.ShapeDtypeStruct((2, 2, 4, 3, 32, FF), BF16),
+            jax.ShapeDtypeStruct((2, 2, 4, 32, 3 * FF), BF16),
         ),
-        in_specs=[pl.BlockSpec(memory_space=pl.ANY)] * 3,
-        out_specs=(pl.BlockSpec(memory_space=pl.ANY),) * 3,
+        in_specs=[vmem] * 3,
+        out_specs=(any_place,) * 3,
         scratch_shapes=[
-            pltpu.SemaphoreType.DMA((6,)),
-            pltpu.SemaphoreType.DMA((6,)),
+            pltpu.VMEM((3, 2, 4, 32, 640), BF16),
+            pltpu.VMEM((3, 2, 32, MODEL_WIDTH), BF16),
+            pltpu.VMEM((2, 4, 32, 640), BF16),
+            pltpu.VMEM((2, 4, 16, 512), BF16),
+            pltpu.VMEM((7, 32, 640), BF16),
+            pltpu.VMEM((7, 16, 512), BF16),
+            pltpu.VMEM((2, 4, 32, 3 * FF), BF16),
+            pltpu.VMEM((32, 640), BF16),
+            pltpu.VMEM((16, 512), BF16),
+            pltpu.VMEM((4, 32, 3 * FF), BF16),
+            pltpu.SemaphoreType.DMA((33,)),
+            pltpu.SemaphoreType.DMA((33,)),
             pltpu.SemaphoreType.DMA((2,)),
             pltpu.SemaphoreType.DMA((4,)),
             pltpu.SemaphoreType.DMA((4,)),
         ],
-        compiler_params=pltpu.CompilerParams(collective_id=3, has_side_effects=True),
-        name="share_all",
-    )(heads_sum, branch_sum, expert_sum)
-    heads_four = heads_four.reshape(4, 32, 640).astype(F32)
-    grad_query_proj = heads_four[:, :, :head_width].transpose(1, 0, 2).reshape(32, -1)
-    grad_key_proj = heads_four[:, :, 256:384].transpose(1, 0, 2).reshape(32, -1)
-    grad_value_proj = heads_four[:, :, 384:512].transpose(1, 0, 2).reshape(32, -1)
-    gain_sums = jnp.sum(heads_four[:, :, 512:514], axis=0)
-    grad_output_proj = (
-        branch_four.reshape(2, 2, 16, 512).transpose(0, 2, 1, 3).reshape(32, MODEL_WIDTH).astype(F32)
-    )
-    expert_four = expert_four.reshape(4, 4, 3, 32, FF).transpose(2, 3, 1, 0, 4)
-    expert_four = expert_four.reshape(3, 32, EXPERTS, FF).astype(F32)
+        compiler_params=pltpu.CompilerParams(
+            collective_id=2, has_side_effects=True, vmem_limit_bytes=32 * 2**20
+        ),
+        name="finish",
+    )(
+        heads_term.reshape(2, 4, 4, 32, 640),
+        output_term.reshape(2, 4, 32, MODEL_WIDTH),
+        expert_grads.reshape(2, 4, 32, 3 * FF),
+    )
+    layer_out = (
+        middle + jnp.dot(weights.astype(BF16), returned, preferred_element_type=F32)
+    ).astype(BF16)
+    pair_dots = jnp.einsum("td,jd->tj", cotangent, returned, preferred_element_type=F32)
+    expert_dots = jnp.einsum(
+        "tj,ej->te", pair_dots * hits.astype(F32), spread, precision=lax.Precision.HIGHEST
+    )
+    grad_gates = RESIDUAL * jnp.sum(named * expert_dots[:, None, :], axis=-1)
+    gain_sums = jnp.sum(heads_four[:, :, :, 512:514].astype(F32), axis=(0, 1))
+    projections = pl.pallas_call(
+        unpack_kernel,
+        out_shape=tuple(
+            jax.ShapeDtypeStruct(shape, F32)
+            for shape in ((32, 1024), (32, 512), (32, 512), (32, 1024)) + ((32, EXPERTS, FF),) * 3
+        ),
+        in_specs=[vmem] * 3,
+        out_specs=(vmem,) * 7,
+        compiler_params=pltpu.CompilerParams(vmem_limit_bytes=16 * 2**20),
+        name="unpack",
+    )(heads_four, branch_four, expert_four)
+    experts_out = projections[4:]
     return (
         layer_out,
         grad_input,
         gain_sums[:, 0],
-        grad_query_proj,
-        grad_key_proj,
-        grad_value_proj,
-        grad_output_proj,
+        projections[0],
+        projections[1],
+        projections[2],
+        projections[3],
         gain_sums[:, 1],
-        expert_four[0],
-        expert_four[1],
-        expert_four[2],
+        experts_out[0],
+        experts_out[1],
+        experts_out[2],
         grad_gates,
     )
 

time: 447 us -> 290 us (0.65)
  the two profiles are of different devices: /device:TPU:15 before, /device:TPU:1 now
where the time goes in v2:
time: 290 us; the launch traced here: 289 us
  Pallas kernels  196 us (68%)
  matrix products  28.1 us (10%)
  local copies, waits for them, and re-layouts  23.4 us (8%)
  other arithmetic  15.6 us (5%)
  waiting for transfers between devices  13.4 us (5%)
  starting transfers between devices  10.7 us (4%)
    pallas_call x4, Pallas kernels, remote_call(): pl.pallas_call(kernel, out_shape=tuple((jax.ShapeDtypeStruct(shape, BF16)...  109 us
    pallas_call x1, Pallas kernels, shards(): pl.pallas_call(finish_kernel, out_shape=(jax.ShapeDtypeStruct((2, 2, 32,...  44.1 us
    pallas_call x1, Pallas kernels, shards(): pl.pallas_call(trade_sum_kernel, out_shape=jax.ShapeDtypeStruct(block, F3...  22.7 us
    all_to_all x2, waiting for transfers between devices, to_group(): lax.all_to_all(blocks, ('z', 'seq'), 0, 0, tiled=True)  13.4 us
    pallas_call x1, Pallas kernels, shards(): pl.pallas_call(expert_kernel, grid=(3,), out_shape=(jax.ShapeDtypeStruct(...  10.9 us
    all_to_all x2, starting transfers between devices, to_group(): lax.all_to_all(blocks, ('z', 'seq'), 0, 0, tiled=True)  8.4 us
    unnamed x143, local copies, waits for them, and re-layouts  8.1 us
    pallas_call x1, Pallas kernels, shards(): pl.pallas_call(expert_grad_kernel, grid=(2,), out_shape=jax.ShapeDtypeStr...  7.02 us
  transfers between devices with their start and end apart: 5, of which 1 were waited for; matrix products, arithmetic and copies ran while one was open for 7% of the time, Pallas kernels for 14%

profile of v2, /device:TPU:1, one launch (start us, length us, event | category | flops | bytes accessed | tf_op | source)
XLA Modules:
  0.0 289.0 jit_solution(11919037192423852152)
XLA Ops:
  0.7 0.8 iota_compare_fusion.1
  2.3 1.2 reshape.293
  6.8 1.2 fusion.89
  8.0 2.2 fusion.3
  10.9 0.8 maximum_bitcast_fusion.experts
  12.3 58.6 %gather_all.1 = (bf16[2,4,4,32,640]{4,3,2,1,0:T(8,128)(2,1)}, bf16[2,2,4,4,32,512]{5,4,3,2,1,0:T(8,128)(2,1)}, bf16[2,2,128,1024]{3,2,1,0:T(8,128)(2,1)}, bf16[2...) custom-call(bf16[32,640]{1,0:T(8,128)(2,1)} %fusion.64.heads, ...), custom_call_target="tpu_custom_call" | custom-call | tf_op jit(solution)/shard_map/gather_all/pallas_call | solution.py:71
  71.0 1.6 multiply_reduce_fusion
  72.6 1.2 slice_convert_fusion
  74.3 2.4 fusion.33
  77.4 1.7 fusion.88
  79.4 0.9 fusion.90
  81.0 0.9 fusion.20
  83.1 0.9 copy.96.blocks
  84.0 8.2 %trade_heads.1 = bf16[4,128,256]{2,1,0:T(8,128)(2,1)} custom-call(bf16[4,128,256]{2,1,0:T(8,128)(2,1)} %copy.96.blocks), custom_call_target="tpu_custom_call" | custom-call | tf_op jit(solution)/shard_map/trade_heads/pallas_call | solution.py:71
  92.2 1.1 copy.97
  94.7 0.8 copy-done.9
  95.5 2.3 convolution_convert_fusion
  97.8 31.4 %dispatch_rows.1 = (bf16[16,72,1024]{2,1,0:T(8,128)(2,1)}, bf16[2,2,4,4,32,512]{5,4,3,2,1,0:T(8,128)(2,1)}) custom-call(bf16[16,72,1024]{2,1,0:T(8,128)(2,1)} %bitcast.175, bf16[2,2,4,32,512]{4,3,2,1,0:T(8,128)(2,1)} %get-tuple-element.47.rest), custom_call_target="tpu_custom_call" | custom-call | tf_op jit(solution)/shard_map/dispatch_rows/pallas_call | solution.py:71
  129.2 1.9 fusion.87
  131.1 10.9 %expert_rows.1 = (bf16[1152,1024]{1,0:T(8,128)(2,1)}, bf16[1152,1024]{1,0:T(8,128)(2,1)}, bf16[1152,512]{1,0:T(8,128)(2,1)S(1)}, bf16[1152,512]{1,0:T(8,128)(2,1)S(1)}, bf16[1152,512]{1,0:T(8,128)(2,1)}) custom-call(bf16[1152,1024]{1,0:T(8,128)(2,1)} %bitcast.160, bf16[1152,1024]{1,0:T(8,128)(2,1)} %bitcast.176, bf16[1024,512]{1,0:T(8,128)(2,1)S(1)} %bitcast.167, ...), custom_call_target="tpu_custom_call" | custom-call | tf_op jit(solution)/shard_map/expert_rows/pallas_call | solution.py:607
  142.1 1.0 copy-done.3
  143.1 4.5 %all-to-all-start = ((bf16[16,72,1024]{2,1,0:T(8,128)(2,1)}), bf16[16,72,1024]{2,1,0:T(8,128)(2,1)}, u32[]{:S(2)}, u32[]{:S(2)}) async-start(bf16[16,72,1024]{2,1,0:T(8,128)(2,1)} %bitcast.190), calls=%async_computation | async-start | bytes 4718592 | tf_op jit(solution)/shard_map/all_to_all | solution.py:495
  147.6 1.3 copy-done.4
  148.9 1.3 copy-done.5
  150.1 7.0 %expert_grads.1 = bf16[4,2,128,1536]{3,2,1,0:T(8,128)(2,1)} custom-call(bf16[1152,1024]{1,0:T(8,128)(2,1)S(1)} %bitcast.161, bf16[1152,1024]{1,0:T(8,128)(2,1)} %bitcast.177, bf16[1152,512]{1,0:T(8,128)(2,1)S(1)} %get-tuple-element.52.active, bf16[1152,512]{1,0:T(8,128)(2,1)S(1)} %copy-done.4, bf16[1152,512]{1,0:T(8,128)(2,1)S(1)} %copy-done.5), custom_call_target="tpu_custom_call" | custom-call | tf_op jit(solution)/shard_map/expert_grads/pallas_call | solution.py:620
  157.2 3.6 %dynamic-slice_bitcast_fusion = (bf16[2,128,1536]{2,1,0:T(8,128)(2,1)}, bf16[2,128,1536]{2,1,0:T(8,128)(2,1)}, bf16[2,128,1536]{2,1,0:T(8,128)(2,1)}, bf16[2,128,1536]{2,1,0:T(8,128)(2,1)}) fusion(bf16[4,2,128,1536]{3,2,1,0:T(8,128)(2,1)} %expert_grads.1, s32[]{:T(128)S(6)} %select_n.102, s32[]{:T(128)S(6)} %select_n.100, s32[]{:T(128)S(6)} %select_n.98, ...), kind=kLoop, calls=%fused_computation.59 | loop fusion | bytes 6291472 | tf_op jit(solution)/shard_map/jit(dynamic_index_in_dim)/squeeze | solution.py:632
  160.8 1.1 collective-permute-start.2
  164.3 13.4 %all-to-all-done = bf16[16,72,1024]{2,1,0:T(8,128)(2,1)} async-done(((bf16[16,72,1024]{2,1,0:T(8,128)(2,1)}), bf16[16,72,1024]{2,1,0:T(8,128)(2,1)}, u32[]{:S(2)}, u32[]{:S(2)}) %all-to-all-start) | async-done | bytes 2359328 | tf_op jit(solution)/shard_map/all_to_all | solution.py:495
  177.7 2.9 %multiply_reduce_fusion.1 = (bf16[1024]{0:T(1024)(128)(2,1)}, f32[128]{0:T(128)S(1)}, f32[128,1024]{1,0:T(8,128)S(1)}) fusion(f32[128,1024]{1,0:T(8,128)S(1)} %copy-done.10, f32[128]{0:T(128)S(1)} %copy-done.62, f32[1024]{0:T(1024)S(1)} %bitcast.211, pred[128,1152]{1,0:T(32,128)(4,1)S(1)} %copy-done.23, bf16[1152,1024]{1,0:T(8,128)(2,1)} %bitcast.42), kind=kOutput, calls=%fused_computation.85 | convolution fusion | flops 302775168 | bytes 3562496 | tf_op jit(solution)/shard_map/dot_general | solution.py:636
  180.6 0.8 copy-done.14
  181.4 0.9 multiply_convert_fusion.block
  182.3 10.5 %spread_branch.1 = bf16[2,2,128,1024]{3,2,1,0:T(8,128)(2,1)} custom-call(bf16[128,1024]{1,0:T(8,128)(2,1)} %multiply_convert_fusion.block), custom_call_target="tpu_custom_call" | custom-call | tf_op jit(solution)/shard_map/spread_branch/pallas_call | solution.py:71
  192.8 3.9 %all-to-all-start.1 = ((bf16[16,72,1024]{2,1,0:T(8,128)(2,1)}), bf16[16,72,1024]{2,1,0:T(8,128)(2,1)S(1)}, u32[]{:S(2)}, u32[]{:S(2)}) async-start(bf16[16,72,1024]{2,1,0:T(8,128)(2,1)} %bitcast.189), calls=%async_computation.1 | async-start | bytes 4718592 | tf_op jit(solution)/shard_map/all_to_all | solution.py:495
  196.8 1.3 fusion.46
  198.1 1.3 fusion.16
  199.4 3.3 %fusion = (f32[2,2,512]{2,1,0:T(2,128)S(1)}, f32[2,512,512,2]{2,1,3,0:T(8,128)S(1)}) fusion(f32[2,2,512,512]{2,3,1,0:T(8,128)} %copy-done.7, f32[2,2,512]{2,1,0:T(2,128)S(1)} %copy-done.45, bf16[512,2,64,1]{0,2,3,1:T(8,128)(2,1)S(1)} %bitcast.199, bf16[512,2,2,64]{0,3,2,1:T(8,128)(2,1)S(1)} %bitcast.185), kind=kOutput, calls=%fused_computation.3 | convolution fusion | flops 137361408 | bytes 8798208 | tf_op jit(solution)/shard_map/qkgd,skd->kgqs/dot_general | solution.py:660
  202.9 1.2 fusion.2
  205.6 0.7 fusion.27
  206.4 0.8 fusion.28
  207.8 0.8 convolution_convert_fusion.1
  208.5 22.7 %trade_normed.1 = f32[128,1024]{1,0:T(8,128)S(1)} custom-call(bf16[2,2,128,1024]{3,2,1,0:T(8,128)(2,1)S(1)} %bitcast.168), custom_call_target="tpu_custom_call" | custom-call | tf_op jit(solution)/shard_map/trade_normed/pallas_call | solution.py:689
  231.7 1.7 convolution_convert_fusion.2
  233.5 1.9 fusion.8
  235.5 1.2 fusion.19
  237.0 1.1 fusion.41
  239.6 2.0 add_convert_fusion
  241.6 44.1 %finish.1 = (bf16[2,2,32,640]{3,2,1,0:T(8,128)(2,1)S(1)}, bf16[4,16,512]{2,1,0:T(8,128)(2,1)S(1)}, bf16[2,2,4,32,1536]{4,3,2,1,0:T(8,128)(2,1)S(1)}) custom-call(bf16[2,4,4,32,640]{4,3,2,1,0:T(8,128)(2,1)S(1)} %bitcast.162, bf16[2,4,32,1024]{3,2,1,0:T(8,128)(2,1)S(1)} %bitcast.166, bf16[2,4,32,1536]{3,2,1,0:T(8,128)(2,1)S(1)} %bitcast.165), custom_call_target="tpu_custom_call" | custom-call | tf_op jit(solution)/shard_map/finish/pallas_call | solution.py:723
  286.4 2.5 unpack.1
  (198 shorter events, 17.4 us)
Async XLA Ops:
  0.6 5.0 %copy-start = (bf16[32,1024]{1,0:T(8,128)(2,1)S(1)}, bf16[32,1024]{1,0:T(8,128)(2,1)}, u32[]{:S(2)}) copy-start(bf16[32,1024]{1,0:T(8,128)(2,1)} %param.18) | copy-start | bytes 196612
  0.7 3.2 %copy-start.38 = (bf16[32,16,512]{2,1,0:T(8,128)(2,1)S(1)}, bf16[32,16,512]{2,1,0:T(8,128)(2,1)}, u32[]{:S(2)}) copy-start(bf16[32,16,512]{2,1,0:T(8,128)(2,1)} %param.21) | copy-start | bytes 1572868
  0.7 3.4 %copy-start.39 = (bf16[32,16,512]{2,1,0:T(8,128)(2,1)S(1)}, bf16[32,16,512]{2,1,0:T(8,128)(2,1)}, u32[]{:S(2)}) copy-start(bf16[32,16,512]{2,1,0:T(8,128)(2,1)} %param.22) | copy-start | bytes 1572868
  0.7 6.0 %copy-start.55 = (s32[1152]{0:T(1024)}, s32[1152]{0:T(1024)S(1)}, u32[]{:S(2)}) copy-start(s32[1152]{0:T(1024)S(1)} %get-tuple-element.118) | copy-start | bytes 13828
  3.5 2.2 copy-start.58
  3.5 2.2 copy-start.64
  4.0 3.9 %copy-start.19 = (bf16[128,1024]{1,0:T(8,128)(2,1)S(1)}, bf16[128,1024]{1,0:T(8,128)(2,1)}, u32[]{:S(2)}) copy-start(bf16[128,1024]{1,0:T(8,128)(2,1)} %param.25) | copy-start | bytes 786436
  6.8 87.9 %copy-start.22 = (pred[128,1152]{1,0:T(32,128)(4,1)}, pred[128,1152]{1,0:T(32,128)(4,1)S(1)}, u32[]{:S(2)}) copy-start(pred[128,1152]{1,0:T(32,128)(4,1)S(1)} %convolution_compare_fusion) | copy-start | bytes 442372
  71.0 3.0 %copy-start.16 = (bf16[2,2,128,1024]{3,2,1,0:T(8,128)(2,1)S(1)}, bf16[2,2,128,1024]{3,2,1,0:T(8,128)(2,1)}, u32[]{:S(2)}) copy-start(bf16[2,2,128,1024]{3,2,1,0:T(8,128)(2,1)} %get-tuple-element.44) | copy-start | bytes 3145732
  73.9 2.7 copy-start.49
  74.3 2.5 copy-start.29
  76.7 4.3 %copy-start.36 = (bf16[512,128]{0,1:T(8,128)(2,1)}, bf16[512,128]{0,1:T(8,128)(2,1)S(1)}, u32[]{:S(2)}) copy-start(bf16[512,128]{0,1:T(8,128)(2,1)S(1)} %slice.139) | copy-start | bytes 393220
  77.1 2.1 copy-start.24
  77.1 2.1 copy-start.26
  77.3 17.4 %copy-start.46 = (f32[1024,1]{0,1:T(1,128)}, f32[1024,1]{0,1:T(1,128)S(1)}, u32[]{:S(2)}) copy-start(f32[1024,1]{0,1:T(1,128)S(1)} %copy.119) | copy-start | bytes 12292
  77.4 2.0 copy-start.43
  80.3 2.0 copy-start.7
  80.3 2.0 copy-start.51
  83.1 10.9 %copy-start.17 = (bf16[128,1024]{1,0:T(8,128)(2,1)S(1)}, bf16[128,1024]{1,0:T(8,128)(2,1)}, u32[]{:S(2)}) copy-start(bf16[128,1024]{1,0:T(8,128)(2,1)} %tokens.1) | copy-start | bytes 786436
  94.7 34.5 %copy-start.61 = (f32[128]{0:T(128)}, f32[128]{0:T(128)S(1)}, u32[]{:S(2)}) copy-start(f32[128]{0:T(128)S(1)} %add_rsqrt_fusion.2) | copy-start | bytes 1540
  129.2 1.9 copy-start.6
  143.1 4.5 %copy-start.2 = (bf16[16,72,1024]{2,1,0:T(8,128)(2,1)S(1)}, bf16[16,72,1024]{2,1,0:T(8,128)(2,1)}, u32[]{:S(2)}) copy-start(bf16[16,72,1024]{2,1,0:T(8,128)(2,1)} %get-tuple-element.48) | copy-start | bytes 7077892
  143.1 34.6 %all-to-all-start = ((bf16[16,72,1024]{2,1,0:T(8,128)(2,1)}), bf16[16,72,1024]{2,1,0:T(8,128)(2,1)}, u32[]{:S(2)}, u32[]{:S(2)}) async-start(bf16[16,72,1024]{2,1,0:T(8,128)(2,1)} %bitcast.190), calls=%async_computation | async-start | bytes 4718592 | tf_op jit(solution)/shard_map/all_to_all | solution.py:495
  157.2 6.0 %copy-start.68 = (f32[128]{0:T(128)S(1)}, f32[128]{0:T(128)}, u32[]{:S(2)}) copy-start(f32[128]{0:T(128)} %get-tuple-element.100) | copy-start | bytes 1540
  157.2 6.5 %copy-start.52 = (f32[2,2,512]{2,1,0:T(2,128)S(1)}, f32[2,2,512]{2,1,0:T(2,128)}, u32[]{:S(2)}) copy-start(f32[2,2,512]{2,1,0:T(2,128)} %copy-done.51) | copy-start | bytes 24580
  157.2 6.5 %copy-start.54 = (f32[2,2,512]{2,1,0:T(2,128)S(1)}, f32[2,2,512]{2,1,0:T(2,128)}, u32[]{:S(2)}) copy-start(f32[2,2,512]{2,1,0:T(2,128)} %copy-done.53) | copy-start | bytes 24580
  157.2 20.5 %copy-start.10 = (f32[128,1024]{1,0:T(8,128)S(1)}, f32[128,1024]{1,0:T(8,128)}, u32[]{:S(2)}) copy-start(f32[128,1024]{1,0:T(8,128)} %copy-done.9) | copy-start | bytes 1572868
  157.2 20.5 %copy-start.23 = (pred[128,1152]{1,0:T(32,128)(4,1)S(1)}, pred[128,1152]{1,0:T(32,128)(4,1)}, u32[]{:S(2)}) copy-start(pred[128,1152]{1,0:T(32,128)(4,1)} %copy-done.22) | copy-start | bytes 442372
  157.2 20.5 %copy-start.47 = (f32[1024,1]{0,1:T(1,128)S(1)}, f32[1024,1]{0,1:T(1,128)}, u32[]{:S(2)}) copy-start(f32[1024,1]{0,1:T(1,128)} %copy-done.46) | copy-start | bytes 12292
  157.2 20.5 %copy-start.62 = (f32[128]{0:T(128)S(1)}, f32[128]{0:T(128)}, u32[]{:S(2)}) copy-start(f32[128]{0:T(128)} %copy-done.61) | copy-start | bytes 1540
  160.8 20.5 %copy-start.20 = (bf16[128,1024]{1,0:T(8,128)(2,1)S(1)}, bf16[128,1024]{1,0:T(8,128)(2,1)}, u32[]{:S(2)}) copy-start(bf16[128,1024]{1,0:T(8,128)(2,1)} %param.25) | copy-start | bytes 786436
  160.8 72.6 %collective-permute-start.2 = (bf16[2,128,1536]{2,1,0:T(8,128)(2,1)}, bf16[2,128,1536]{2,1,0:T(8,128)(2,1)}, u32[]{:S(2)}, u32[]{:S(2)}) collective-permute-start(bf16[2,128,1536]{2,1,0:T(8,128)(2,1)} %get-tuple-element.86), channel_id=1, source_target_pairs={{0,48},{16,0},{32,16},{48,32},{1,49},{17,1},{33,17},{49,33},{2,50}... | collective-permute-start | bytes 2359304 | tf_op jit(solution)/shard_map/ppermute | solution.py:633
  162.0 71.5 %collective-permute-start.1 = (bf16[2,128,1536]{2,1,0:T(8,128)(2,1)}, bf16[2,128,1536]{2,1,0:T(8,128)(2,1)}, u32[]{:S(2)}, u32[]{:S(2)}) collective-permute-start(bf16[2,128,1536]{2,1,0:T(8,128)(2,1)} %get-tuple-element.87), channel_id=1, source_target_pairs={{0,32},{16,48},{32,0},{48,16},{1,33},{17,49},{33,1},{49,17},{2,34}... | collective-permute-start | bytes 2359304 | tf_op jit(solution)/shard_map/ppermute | solution.py:633
  162.6 70.9 %collective-permute-start = (bf16[2,128,1536]{2,1,0:T(8,128)(2,1)}, bf16[2,128,1536]{2,1,0:T(8,128)(2,1)}, u32[]{:S(2)}, u32[]{:S(2)}) collective-permute-start(bf16[2,128,1536]{2,1,0:T(8,128)(2,1)} %get-tuple-element.88), channel_id=1, source_target_pairs={{0,16},{16,32},{32,48},{48,0},{1,17},{17,33},{33,49},{49,1},{2,18}... | collective-permute-start | bytes 2359304 | tf_op jit(solution)/shard_map/ppermute | solution.py:633
  180.6 12.2 %copy-start.66 = (f32[128]{0:T(128)}, f32[128]{0:T(128)S(1)}, u32[]{:S(2)}) copy-start(f32[128]{0:T(128)S(1)} %broadcast_multiply_fusion.3) | copy-start | bytes 1540
  192.8 4.0 %copy-start.12 = (bf16[2,2,128,1024]{3,2,1,0:T(8,128)(2,1)S(1)}, bf16[2,2,128,1024]{3,2,1,0:T(8,128)(2,1)}, u32[]{:S(2)}) copy-start(bf16[2,2,128,1024]{3,2,1,0:T(8,128)(2,1)} %spread_branch.1) | copy-start | bytes 3145732
  192.8 40.7 %all-to-all-start.1 = ((bf16[16,72,1024]{2,1,0:T(8,128)(2,1)}), bf16[16,72,1024]{2,1,0:T(8,128)(2,1)S(1)}, u32[]{:S(2)}, u32[]{:S(2)}) async-start(bf16[16,72,1024]{2,1,0:T(8,128)(2,1)} %bitcast.189), calls=%async_computation.1 | async-start | bytes 4718592 | tf_op jit(solution)/shard_map/all_to_all | solution.py:495
  196.7 2.7 copy-start.37
  196.7 2.7 copy-start.45
  199.4 3.5 %copy-start.8 = (f32[2,2,512,512]{2,3,1,0:T(8,128)S(1)}, f32[2,2,512,512]{2,3,1,0:T(8,128)}, u32[]{:S(2)}) copy-start(f32[2,2,512,512]{2,3,1,0:T(8,128)} %copy-done.7) | copy-start | bytes 12582916
  207.8 23.5 %copy-start.13 = (bf16[2,2,128,1024]{3,2,1,0:T(8,128)(2,1)S(1)}, bf16[2,2,128,1024]{3,2,1,0:T(8,128)(2,1)}, u32[]{:S(2)}) copy-start(bf16[2,2,128,1024]{3,2,1,0:T(8,128)(2,1)} %spread_branch.1) | copy-start | bytes 3145732
  207.8 23.5 %copy-start.32 = (bf16[2,64,2,512]{3,1,2,0:T(8,128)(2,1)S(1)}, bf16[2,64,2,512]{3,1,2,0:T(8,128)(2,1)}, u32[]{:S(2)}) copy-start(bf16[2,64,2,512]{3,1,2,0:T(8,128)(2,1)} %copy-done.31) | copy-start | bytes 786436
  208.5 23.2 %copy-start.30 = (bf16[512,1024]{1,0:T(8,128)(2,1)S(1)}, bf16[512,1024]{1,0:T(8,128)(2,1)}, u32[]{:S(2)}) copy-start(bf16[512,1024]{1,0:T(8,128)(2,1)} %copy-done.29) | copy-start | bytes 3145732
  233.5 2.0 copy-start.11
  233.5 2.0 copy-start.42
  236.8 2.4 copy-start.57
  236.8 2.6 copy-start.33
  239.6 49.4 %copy-start.1 = (bf16[32,1024]{1,0:T(8,128)(2,1)S(1)}, bf16[32,1024]{1,0:T(8,128)(2,1)}, u32[]{:S(2)}) copy-start(bf16[32,1024]{1,0:T(8,128)(2,1)} %param.18) | copy-start | bytes 196612
  (26 other events, 32.3 us)

commit v3 on v2

v3 whole, which is shorter than its diff:
```python
import jax
import jax.numpy as jnp
import numpy as np
from jax import lax
from jax.experimental import pallas as pl
from jax.experimental.pallas import tpu as pltpu
from jax.sharding import Mesh
from jax.sharding import PartitionSpec as P

MODEL_WIDTH = 1024
QUERY_HEADS = 16
KEY_VALUE_HEADS = 8
HEAD_SIZE = 64
TOP = 8
EXPERTS = 16
CAP = 72
SLOTS = EXPERTS * CAP
TOK = 128
SEQ_LEN = 512
FF = 512
EPSILON = 1e-05
RESIDUAL = 0.22
ROPE_BASE = 10000.0
MASK_VALUE = -1e30

PLACES = np.arange(SEQ_LEN, dtype=np.float32)
FREQUENCIES = (ROPE_BASE ** (-np.arange(0, HEAD_SIZE, 2) / HEAD_SIZE)).astype(np.float32)
TURNS = PLACES[:, None] * np.tile(FREQUENCIES, 4)[None, :]
COSINE = np.cos(TURNS).astype(np.float32)
SINE = np.where(np.arange(TOK) % HEAD_SIZE < 32, -np.sin(TURNS), np.sin(TURNS)).astype(np.float32)

BF16 = jnp.bfloat16
F32 = jnp.float32
AXES = ("yh", "x", "z", "seq")
BY_ID = pl.DeviceIdType.MESH


def place():
    return tuple(lax.axis_index(axis) for axis in AXES)


class Sender:
    def __init__(self, send, recv):
        self.send, self.recv, self.used, self.copies = send, recv, 0, []

    def start(self, source, target, device):
        copy = pltpu.make_async_remote_copy(
            src_ref=source,
            dst_ref=target,
            send_sem=self.send.at[self.used],
            recv_sem=self.recv.at[self.used],
            device_id=device,
            device_id_type=BY_ID,
        )
        copy.start()
        self.used += 1
        self.copies.append(copy)
        return copy

    def finish(self):
        for copy in self.copies:
            copy.wait_send()


def arrived(copies):
    for copy in copies:
        copy.wait_recv()


def greet(partners):
    barrier = pltpu.get_barrier_semaphore()
    for partner in partners:
        pl.semaphore_signal(barrier, inc=1, device_id=partner, device_id_type=BY_ID)
    pl.semaphore_wait(barrier, len(partners))


def remote_call(kernel, inputs, outputs, copies, local_copies, collective_id, name):
    return pl.pallas_call(
        kernel,
        out_shape=tuple(
            shape if isinstance(shape, jax.ShapeDtypeStruct) else jax.ShapeDtypeStruct(shape, BF16)
            for shape in outputs
        ),
        in_specs=[pl.BlockSpec(memory_space=pltpu.HBM)] * len(inputs),
        out_specs=tuple(pl.BlockSpec(memory_space=pltpu.HBM) for _ in outputs),
        scratch_shapes=[
            pltpu.SemaphoreType.DMA((copies,)),
            pltpu.SemaphoreType.DMA((copies,)),
            pltpu.SemaphoreType.DMA((local_copies,)),
        ],
        compiler_params=pltpu.CompilerParams(collective_id=collective_id, has_side_effects=True),
        name=name,
    )(*inputs)


def local_starts(pairs, sems):
    copies = []
    for index, (source, target) in enumerate(pairs):
        copy = pltpu.make_async_copy(source, target, sems.at[index])
        copy.start()
        copies.append(copy)
    return copies


def group_of(x, z, seq, yh):
    yl, core = seq // 2, seq % 2
    return [
        (yh, x, (z + k // 4) % 4, (yl + (k // 2) % 2) % 2 * 2 + (core + k % 2) % 2)
        for k in range(1, 16)
    ]


class Blocks:
    def __init__(self, sender, block, blocks_all):
        yh, x, z, seq = place()
        self.yl, self.core = seq // 2, seq % 2
        self.sender, self.z, self.blocks = sender, z, blocks_all
        self.near = (yh, x, z, (1 - self.yl) * 2 + self.core)
        self.sibling = (yh, x, z, self.yl * 2 + 1 - self.core)
        self.along_z = [(yh, x, (z + k) % 4, seq) for k in (1, 2, 3)]
        own = blocks_all.at[z, self.yl, self.core]
        self.to_near = sender.start(block, own, self.near)
        self.to_z = [sender.start(block, own, partner) for partner in self.along_z]
        self.to_sibling = [sender.start(block, own, self.sibling)]

    def again(self, ref, partner):
        return self.sender.start(ref, ref, partner)

    def forward(self):
        arrived([self.to_near])
        beside = self.blocks.at[self.z, 1 - self.yl, self.core]
        self.passed = [self.again(beside.at[pl.ds(0, 64)], partner) for partner in self.along_z]
        self.to_sibling.append(self.again(beside, self.sibling))
        for k, copy in enumerate(self.to_z):
            arrived([copy])
            block = self.blocks.at[(self.z + 3 - k) % 4, self.yl, self.core]
            self.passed.append(self.again(block.at[pl.ds(64, 64)], self.near))
            self.to_sibling.append(self.again(block, self.sibling))

    def finish(self):
        for k in range(3):
            arrived([self.passed[k], self.passed[k + 3]])
            block = self.blocks.at[(self.z + 3 - k) % 4, 1 - self.yl, self.core]
            self.to_sibling.append(self.again(block, self.sibling))
        arrived(self.to_sibling)


def gather_kernel(
    heads, branch, tokens, experts, rows, gates,
    heads_all, branch_all, tokens_all, experts_all, rows_all, gates_all,
    send, recv, local,
):
    yh, x, z, seq = place()
    yl, core = seq // 2, seq % 2
    along_y = (1 - yh, x, z, seq)
    along_x = [(yh, (x + k) % 4, z, seq) for k in (1, 2, 3)]
    along_z = [(yh, x, (z + k) % 4, seq) for k in (1, 2, 3)]
    near = (yh, x, z, (1 - yl) * 2 + core)
    sibling = (yh, x, z, yl * 2 + 1 - core)
    group = [
        (yh, x, (z + k // 4) % 4, (yl + (k // 2) % 2) % 2 * 2 + (core + k % 2) % 2)
        for k in range(1, 16)
    ]
    expert = z * 4 + seq
    greet([along_y] + along_x + group)
    sender = Sender(send, recv)
    first = [
        sender.start(heads, heads_all.at[yh, x, z], along_y),
        sender.start(branch, branch_all.at[core, yh, x, z], along_y),
    ]
    expert_first = [
        sender.start(experts.at[partner[2]], experts_all.at[:, yh, z], partner)
        for partner in along_z
    ]
    token_copies = [
        sender.start(tokens, tokens_all.at[yl, core], near),
        sender.start(tokens, tokens_all.at[yl, core], sibling),
    ]
    own = local_starts(
        [
            (heads, heads_all.at[yh, x, z]),
            (branch, branch_all.at[core, yh, x, z]),
            (experts.at[z], experts_all.at[:, yh, z]),
            (tokens, tokens_all.at[yl, core]),
            (rows, rows_all.at[z, yl, core]),
            (gates.at[expert], gates_all.at[expert]),
        ],
        local,
    )
    for copy in own[:2]:
        copy.wait()
    arrived(first)
    second = []
    for partner in along_z:
        for source in (heads_all.at[:, x, z], branch_all.at[core, :, x, z]):
            second.append(sender.start(source, source, partner))
    own[2].wait()
    arrived(expert_first)
    mine = experts_all.at[:, yh]
    expert_second = [sender.start(mine, mine, along_y)]
    arrived(second)
    third = []
    for partner in along_x:
        for source in (heads_all.at[:, x], branch_all.at[core, :, x]):
            third.append(sender.start(source, source, partner))
    blocks = Blocks(sender, rows, rows_all)
    gate_copies = [
        sender.start(gates.at[partner[2] * 4 + partner[3]], gates_all.at[expert], partner)
        for partner in group
    ]
    arrived(token_copies)
    far = tokens_all.at[1 - yl, core]
    last = [sender.start(far, far, sibling)]
    blocks.forward()
    for copy in own[3:]:
        copy.wait()
    blocks.finish()
    arrived(third)
    half = branch_all.at[core]
    last.append(sender.start(half, half, sibling))
    arrived(expert_second)
    arrived(gate_copies)
    arrived(last)
    sender.finish()


def by_rows(left, right):
    return lax.dot_general(left, right, (((0,), (0,)), ((), ())), preferred_element_type=F32)


def by_columns(left, right):
    return lax.dot_general(left, right, (((1,), (1,)), ((), ())), preferred_element_type=F32)


def half_turn(values):
    lane = lax.broadcasted_iota(jnp.int32, values.shape, 1)
    return jnp.where(lane % 64 < 32, pltpu.roll(values, 96, 1), pltpu.roll(values, 32, 1))


def causal_scores(query, key):
    row = lax.broadcasted_iota(jnp.int32, (SEQ_LEN, SEQ_LEN), 0)
    column = lax.broadcasted_iota(jnp.int32, (SEQ_LEN, SEQ_LEN), 1)
    return jnp.where(row >= column, by_columns(query, key) * (1.0 / HEAD_SIZE), MASK_VALUE)


def forward_kernel(
    tokens_in, heads_in, branch_in, cosine_in, sine_in, gates_in, out_in,
    normed_out, query_out, key_out, value_out, attended_out, sums_out, middle_out, picks_out,
    back_out, rows_all, gains,
    tokens, heads_w, branch_here, cosine, sine, gates, out_here,
    normed, query, key, value, attended, sums, middle, picks, back,
    traded, rows, send, recv, fetch, keep,
):
    yh, x, z, seq = place()
    yl, core = seq // 2, seq % 2
    along_z = [(yh, x, (z + k) % 4, seq) for k in (1, 2, 3)]
    beside = [(yh, x, z, (seq + k) % 4) for k in (1, 2, 3)]
    fetched = local_starts(
        [
            (heads_in, heads_w), (tokens_in, tokens), (cosine_in, cosine), (sine_in, sine),
            (branch_in, branch_here), (gates_in, gates), (out_in, out_here),
        ],
        fetch,
    )
    greet(along_z + beside)
    for copy in fetched[:4]:
        copy.wait()
    gains[...] = heads_w[:, 512:640].astype(F32).T[0:8]
    sequence = tokens[...].reshape(SEQ_LEN, MODEL_WIDTH).astype(F32)
    factor = lax.rsqrt(jnp.mean(sequence * sequence, axis=-1, keepdims=True) + EPSILON)
    normed[...] = (sequence * factor * gains[0:1]).astype(BF16)
    projected = jnp.dot(normed[...], heads_w[:, 0:512], preferred_element_type=F32)
    for k in range(2):
        part = projected[:, k * 128 : k * 128 + 128]
        query[:, k * 128 : k * 128 + 128] = (
            part * cosine[...] + half_turn(part) * sine[...]
        ).astype(BF16)
    part = projected[:, 256:384]
    key[...] = (part * cosine[...] + half_turn(part) * sine[...]).astype(BF16)
    value[...] = projected[:, 384:512].astype(BF16)
    lane = lax.broadcasted_iota(jnp.int32, (SEQ_LEN, TOK), 1)
    all_sums = jnp.zeros((SEQ_LEN, TOK), F32)
    for k in range(2):
        results = []
        key_head, value_head = key[:, k * 64 : k * 64 + 64], value[:, k * 64 : k * 64 + 64]
        for g in range(2):
            head = k * 2 + g
            scores = causal_scores(query[:, head * 64 : head * 64 + 64], key_head)
            top = jnp.max(scores, axis=-1, keepdims=True)
            exponent = jnp.exp(scores - top)
            total = jnp.sum(exponent, axis=-1, keepdims=True)
            probs = (exponent / total).astype(BF16)
            all_sums = jnp.where(lane == head, top + jnp.log(total), all_sums)
            results.append(jnp.dot(probs, value_head, preferred_element_type=F32))
        attended[:, k * 128 : k * 128 + 128] = jnp.concatenate(results, axis=1).astype(BF16)
    sums[...] = all_sums

    sender = Sender(send, recv)
    trades = []
    for partner in beside:
        start = pl.multiple_of(partner[3] * TOK, TOK)
        trades.append(sender.start(attended.at[pl.ds(start, TOK)], traded.at[seq], partner))
    traded[seq] = attended[pl.ds(pl.multiple_of(seq * TOK, TOK), TOK), :]
    kept = local_starts(
        [
            (normed, normed_out), (query, query_out), (key, key_out), (value, value_out),
            (attended, attended_out), (sums, sums_out),
        ],
        keep,
    )
    fetched[4].wait()
    arrived(trades)
    here = jnp.concatenate([traded[k] for k in range(4)], axis=1)
    branch = jnp.concatenate(
        [jnp.dot(here, branch_here[k], preferred_element_type=F32) for k in range(2)], axis=1
    )
    mid = tokens[seq].astype(F32) + RESIDUAL * branch
    middle[...] = mid
    factor = lax.rsqrt(jnp.mean(mid * mid, axis=-1, keepdims=True) + EPSILON)
    rows[...] = (mid * factor * gains[1:2]).astype(BF16)

    blocks = Blocks(sender, rows, rows_all)
    for index, (source, target) in enumerate(
        ((rows, rows_all.at[z, yl, core]), (middle, middle_out))
    ):
        kept.append(pltpu.make_async_copy(source, target, keep.at[6 + index]))
        kept[-1].start()
    for copy in fetched[5:]:
        copy.wait()
    row = lax.broadcasted_iota(jnp.int32, (TOK, TOK), 0)
    column = lax.broadcasted_iota(jnp.int32, (TOK, TOK), 1)
    earlier = jnp.where(row < column, 1.0, 0.0).astype(BF16)
    slot = lax.broadcasted_iota(jnp.int32, (CAP, TOK), 0).astype(F32)

    def two(index, carry):
        parts = []
        for j in range(2):
            gate = gates[index * 2 + j]
            named = jnp.where(gate > 0.0, 1.0, 0.0)
            ranks = jnp.dot(named.astype(BF16), earlier, preferred_element_type=F32)
            place_in = jnp.where(named > 0.5, ranks, -1.0)[0:1]
            hit = jnp.where(slot == place_in, 1.0, 0.0)
            pick = hit.astype(BF16)
            picks[index * 2 + j] = pick
            weight = jnp.sum(hit * gate[0:1], axis=1, keepdims=True)
            chosen = jnp.dot(pick, out_here[index * 2 + j], preferred_element_type=F32)
            parts.append(chosen * (RESIDUAL * weight))
        start = pl.multiple_of(index * (2 * CAP), 2 * CAP)
        back[pl.ds(start, 2 * CAP), :] = jnp.concatenate(parts, axis=0).astype(BF16)
        return carry

    lax.fori_loop(0, 4, two, 0)
    blocks.forward()
    lax.fori_loop(4, 8, two, 0)
    for index, (source, target) in enumerate(((picks, picks_out), (back, back_out))):
        kept.append(pltpu.make_async_copy(source, target, keep.at[8 + index]))
        kept[-1].start()
    blocks.finish()
    for copy in kept:
        copy.wait()
    sender.finish()


def backward_kernel(
    block, returned, branch_w,
    attended_in, query_in, key_in, value_in, sums_in, normed_in, heads_in, cosine_in, sine_in,
    grad_normed, heads_term, branch_total, returned_all,
    attended, query, key, value, sums, normed, heads_w, cosine, sine,
    branch_here, blocks_all, output_term, parts,
    arriving, paired, outgoing, incoming, branch_z, branch_out, branch_plane, send, recv, local,
):
    yh, x, z, seq = place()
    yl, core = seq // 2, seq % 2
    expert = z * 4 + seq
    near = (yh, x, z, (1 - yl) * 2 + core)
    sibling = (yh, x, z, yl * 2 + 1 - core)
    along_z = [(yh, x, (z + k) % 4, seq) for k in (1, 2, 3)]
    plane = [((yh + k // 4) % 2, (x + k % 4) % 4, z, seq) for k in range(1, 8)]
    group = [
        (yh, x, (z + k // 4) % 4, (yl + (k // 2) % 2) % 2 * 2 + (core + k % 2) % 2)
        for k in range(1, 16)
    ]
    rows = pl.ds(pl.multiple_of(seq * 256, 256), 256)
    fetched = local_starts(
        [
            (branch_w.at[:, rows], branch_here),
            (attended_in, attended), (query_in, query), (key_in, key), (value_in, value),
            (sums_in, sums), (normed_in, normed), (heads_in, heads_w),
            (cosine_in, cosine), (sine_in, sine),
            (returned.at[0, expert], returned_all.at[expert]),
        ],
        local,
    )
    greet(group + plane)
    sender = Sender(send, recv)
    first = [
        sender.start(block, blocks_all.at[yl, core], near),
        sender.start(block, blocks_all.at[yl, core], sibling),
    ]
    blocks_all[yl, core] = block[...]
    arrived(first[:1])
    far = blocks_all.at[1 - yl, core]
    last = sender.start(far, far, sibling)
    row_copies = [
        sender.start(returned.at[0, partner[2] * 4 + partner[3]], returned_all.at[expert], partner)
        for partner in group
    ]
    for copy in fetched[:10]:
        copy.wait()
    arrived(first[1:])
    arrived([last])
    branch_all = blocks_all[...].reshape(SEQ_LEN, MODEL_WIDTH)
    output_term[...] = by_rows(attended[...], branch_all).astype(BF16).reshape(8, 2, 16, MODEL_WIDTH)

    def branch_block(place_z):
        left = pl.multiple_of(place_z % 2 * 512, 512)
        return output_term.at[:, place_z // 2, :, pl.ds(left, 512)]

    around = [
        sender.start(branch_block(partner[2]), branch_z.at[k], partner)
        for k, partner in enumerate(along_z)
    ]
    grad_heads = (
        by_columns(branch_all[:, :512], branch_here[0])
        + by_columns(branch_all[:, 512:], branch_here[1])
    ).astype(BF16)
    lane = lax.broadcasted_iota(jnp.int32, (SEQ_LEN, TOK), 1)
    grad_queries, grad_keys, grad_values = [], [], []
    for k in range(2):
        key_head, value_head = key[:, k * 64 : k * 64 + 64], value[:, k * 64 : k * 64 + 64]
        grad_key, grad_value = 0.0, 0.0
        for g in range(2):
            head = k * 2 + g
            query_head = query[:, head * 64 : head * 64 + 64]
            grad_head = grad_heads[:, head * 64 : head * 64 + 64]
            log_sum = jnp.sum(jnp.where(lane == head, sums[...], 0.0), axis=-1, keepdims=True)
            probs = jnp.exp(causal_scores(query_head, key_head) - log_sum)
            grad_probs = by_columns(grad_head, value_head)
            inner = jnp.sum(probs * grad_probs, axis=-1, keepdims=True)
            grad_scores = (probs * (grad_probs - inner)).astype(BF16)
            grad_value += by_rows(probs.astype(BF16), grad_head)
            grad_key += by_rows(grad_scores, query_head)
            grad_queries.append(
                jnp.dot(grad_scores, key_head, preferred_element_type=F32) * (1.0 / HEAD_SIZE)
            )
        grad_keys.append(grad_key * (1.0 / HEAD_SIZE))
        grad_values.append(grad_value)

    def unturn(pair):
        values = jnp.concatenate(pair, axis=1).astype(BF16).astype(F32)
        return (values * cosine[...] - half_turn(values) * sine[...]).astype(BF16)

    projected = jnp.concatenate(
        [
            unturn(grad_queries[:2]),
            unturn(grad_queries[2:]),
            unturn(grad_keys),
            jnp.concatenate(grad_values, axis=1).astype(BF16),
        ],
        axis=1,
    )
    parts[...] = by_columns(projected, heads_w[:, 0:512]).astype(BF16).reshape(2, 2, TOK, MODEL_WIDTH)
    second = [
        sender.start(parts.at[1 - yl, 1 - core], arriving.at[0], sibling),
        sender.start(parts.at[yl, 1 - core], arriving.at[1], sibling),
    ]
    arrived(around)
    mine = branch_block(z)[...]
    branch_out[...] = gather_sums([mine] + [branch_z[k] for k in range(3)]).astype(BF16)
    across = [
        sender.start(branch_out.at[partner[0] * 4 + partner[1]], branch_plane.at[k], partner)
        for k, partner in enumerate(plane)
    ]
    arrived(second[:1])
    outgoing[...] = gather_sums([parts[1 - yl, core], arriving[0]]).astype(BF16)
    third = sender.start(outgoing, incoming, near)
    heads_term[...] = by_rows(normed[...], projected).astype(BF16)
    arrived(second[1:])
    paired[...] = gather_sums([parts[yl, core], arriving[1]])
    arrived(across)
    branch_total[...] = gather_sums(
        [branch_out[yh * 4 + x]] + [branch_plane[k] for k in range(7)]
    ).astype(BF16)
    arrived([third])
    grad_normed[...] = paired[...] + incoming[...].astype(F32)
    fetched[10].wait()
    arrived(row_copies)
    sender.finish()


def gather_sums(parts):
    total = parts[0].astype(F32)
    for part in parts[1:]:
        total = total + part.astype(F32)
    return total


def finish_kernel(
    heads, branch_sum, experts, rows,
    heads_four, branch_four, experts_four, rows_all,
    upper_in, lower_in, upper_out, lower_out, upper_plane, lower_plane, experts_plane,
    heads_sum, experts_sum,
    send, recv, local, branch_sends, branch_recvs,
):
    yh, x, z, seq = place()
    yl, core = seq // 2, seq % 2
    dp = yh * 16 + x * 4 + z
    near = (yh, x, z, (1 - yl) * 2 + core)
    sibling = (yh, x, z, yl * 2 + 1 - core)
    along_x = [(yh, (x + k) % 4, z, seq) for k in (1, 2, 3)]
    along_z = [(yh, x, (z + k) % 4, seq) for k in (1, 2, 3)]
    plane = [((yh + k // 4) % 2, x, (z + k % 4) % 4, seq) for k in range(1, 8)]
    group = [
        (yh, x, (z + k // 4) % 4, (yl + (k // 2) % 2) % 2 * 2 + (core + k % 2) % 2)
        for k in range(1, 16)
    ]
    expert = z * 4 + seq
    other_plane = [((yh + k // 4) % 2, (x + k % 4) % 4, z, seq) for k in range(1, 8)]
    owner = seq * 8 + dp // 4
    source_seq = dp // 8
    slot = dp % 4
    here = owner == dp
    barrier = pltpu.get_barrier_semaphore()
    for partner in group + along_x + plane[3:] + other_plane[4:]:
        pl.semaphore_signal(barrier, inc=1, device_id=partner, device_id_type=BY_ID)
    for k in range(4):
        maker = dp % 8 * 4 + k
        foreign = jnp.logical_or(maker != dp, source_seq != seq)

        @pl.when(foreign)
        def _():
            pl.semaphore_signal(
                barrier,
                inc=1,
                device_id=(maker // 16, maker // 4 % 4, maker % 4, source_seq),
                device_id_type=BY_ID,
            )

    pl.semaphore_wait(barrier, 29 - here.astype(jnp.int32))
    sender = Sender(send, recv)
    upper, lower = pl.ds(0, 16), pl.ds(16, 16)
    first = []
    for k in range(3):
        partner = along_x[k]
        first.append(sender.start(heads.at[:, partner[1], :, upper], upper_in.at[k], partner))
        partner = along_z[k]
        first.append(sender.start(heads.at[:, :, partner[2], lower], lower_in.at[k], partner))
    place_of = branch_four.at[slot]

    def branch_copy(k):
        return pltpu.make_async_remote_copy(
            src_ref=branch_sum,
            dst_ref=place_of,
            send_sem=branch_sends.at[k],
            recv_sem=branch_recvs.at[slot],
            device_id=(owner // 16, owner // 4 % 4, owner % 4, k),
            device_id_type=BY_ID,
        )

    for k in range(4):
        self_copy = jnp.logical_and(here, seq == k)

        @pl.when(jnp.logical_not(self_copy))
        def _():
            branch_copy(k).start()

        @pl.when(self_copy)
        def _():
            pltpu.make_async_copy(branch_sum, place_of, branch_recvs.at[slot]).start()

    across = [
        sender.start(experts.at[partner[0], partner[2]], experts_plane.at[yh, z], partner)
        for partner in plane
    ]
    row_copies = [
        sender.start(rows.at[1, partner[2] * 4 + partner[3]], rows_all.at[expert], partner)
        for partner in group
    ]
    own_rows = pltpu.make_async_copy(rows.at[1, expert], rows_all.at[expert], local.at[2])
    own_rows.start()
    arrived(first)
    for y in range(2):
        for j in range(4):
            upper_out[y, j] = gather_sums(
                [heads[y, x, j, 0:16]] + [upper_in[k, y, j] for k in range(3)]
            ).astype(BF16)
            lower_out[y, j] = gather_sums(
                [heads[y, j, z, 16:32]] + [lower_in[k, y, j] for k in range(3)]
            ).astype(BF16)
    second = []
    for k in range(7):
        partner = plane[k]
        second.append(sender.start(upper_out.at[partner[0], partner[2]], upper_plane.at[k], partner))
        partner = other_plane[k]
        second.append(sender.start(lower_out.at[partner[0], partner[1]], lower_plane.at[k], partner))
    arrived(across)
    for j in range(4):
        @pl.when(z == j)
        def _():
            experts_sum[j] = gather_sums([experts[yh, j], experts_plane[1 - yh, j]]).astype(BF16)

        @pl.when(z != j)
        def _():
            experts_sum[j] = gather_sums([experts_plane[0, j], experts_plane[1, j]]).astype(BF16)

    third = []
    for partner in (near, sibling):
        third.append(sender.start(experts_sum, experts_four.at[yl, core], partner))
    own = local_starts([(experts_sum, experts_four.at[yl, core])], local)
    arrived(second)
    heads_sum[0:16] = gather_sums(
        [upper_out[yh, z]] + [upper_plane[k] for k in range(7)]
    ).astype(BF16)
    heads_sum[16:32] = gather_sums(
        [lower_out[yh, x]] + [lower_plane[k] for k in range(7)]
    ).astype(BF16)
    fourth = []
    for partner in (near, sibling):
        fourth.append(sender.start(heads_sum, heads_four.at[yl, core], partner))
    own_heads = pltpu.make_async_copy(heads_sum, heads_four.at[yl, core], local.at[1])
    own_heads.start()
    arrived(third[:1])
    far = experts_four.at[1 - yl, core]
    last = [sender.start(far, far, sibling)]
    arrived(fourth[:1])
    far = heads_four.at[1 - yl, core]
    last.append(sender.start(far, far, sibling))
    arrived(third[1:])
    arrived(fourth[1:])
    own[0].wait()
    own_heads.wait()
    own_rows.wait()
    arrived(row_copies)
    arrived(last)
    for k in range(4):
        pltpu.make_async_copy(branch_sum, branch_four.at[k], branch_recvs.at[k]).wait()
        self_copy = jnp.logical_and(here, seq == k)

        @pl.when(jnp.logical_not(self_copy))
        def _():
            branch_copy(k).wait_send()

    sender.finish()


def unpack_kernel(heads, branch, experts, query, key, value, output, gate, up, down):
    for s in range(4):
        block = heads[s // 2, s % 2].astype(F32)
        query[:, s * 256 : s * 256 + 256] = block[:, :256]
        key[:, s * 128 : s * 128 + 128] = block[:, 256:384]
        value[:, s * 128 : s * 128 + 128] = block[:, 384:512]
        rows, columns = s // 2 * 16, s % 2 * 512
        output[rows : rows + 16, columns : columns + 512] = branch[s].astype(F32)
        for j in range(4):
            block = experts[s // 2, s % 2, j].astype(F32)
            for index, result in enumerate((gate, up, down)):
                result[:, j * 4 + s, :] = block[:, index * 512 : index * 512 + 512]


def expert_kernel(
    rows_all, picks_in, back_in, own_w, first_w, second_w, third_w,
    grad_rows, returned_out, expert_grads_out,
    picks, back, returned, expert_grads,
    rows_here, weights, outgoing, chosen, active, by_gate, by_up, send, recv, local,
):
    yh, x, z, seq = place()
    expert = z * 4 + seq
    turns = (2, 1, 3, 0)
    offsets = [(turn, k) for turn in turns for k in range(4) if turn + k > 0]
    partners = [(yh, x, (z + turn) % 4, (seq + k) % 4) for turn, k in offsets]
    fetches = local_starts(
        [
            (part, weights.at[:, :, (x + 4 - k) % 4])
            for k, part in enumerate((own_w, first_w, second_w, third_w))
        ]
        + [(rows_all.at[(z + turn) % 4], rows_here.at[turn]) for turn in turns]
        + [(picks_in, picks), (back_in, back)],
        local,
    )
    greet(partners)
    sender = Sender(send, recv)
    for copy in fetches[:4] + fetches[8:]:
        copy.wait()
    gate_w, up_w, down_w = (weights[k].reshape(MODEL_WIDTH, FF) for k in range(3))
    for index, turn in enumerate(turns):
        fetches[4 + index].wait()
        first = (z + turn) % 4 * 4
        rows = jnp.concatenate(
            [
                jnp.dot(picks[first + j], rows_here[turn, j], preferred_element_type=F32)
                for j in range(4)
            ],
            axis=0,
        ).astype(BF16)
        span = pl.ds(index * 288, 288)
        chosen[span, :] = rows
        gate_pre = jnp.dot(rows, gate_w, preferred_element_type=F32)
        up_pre = jnp.dot(rows, up_w, preferred_element_type=F32)
        back_rows = back[pl.ds(pl.multiple_of(first * CAP, 288), 288), :]
        grad_active = jnp.dot(back_rows, down_w, preferred_element_type=F32)
        sigmoid_gate = jax.nn.sigmoid(gate_pre)
        silu = gate_pre * sigmoid_gate
        slope = sigmoid_gate * (1.0 + gate_pre * (1.0 - sigmoid_gate))
        grad_gate = (grad_active * up_pre * slope).astype(BF16)
        grad_up = (grad_active * silu).astype(BF16)
        by_gate[span, :] = grad_gate
        by_up[span, :] = grad_up
        active[span, :] = (silu * up_pre).astype(BF16)
        result = by_columns(grad_gate, gate_w) + by_columns(grad_up, up_w)
        for j in range(4):
            outgoing[first + j] = result[j * CAP : j * CAP + CAP].astype(BF16)
        for partner, offset in zip(partners, offsets):
            if offset[0] == turn:
                block = partner[2] * 4 + partner[3]
                sender.start(outgoing.at[block], grad_rows.at[expert], partner)
    kept = [pltpu.make_async_copy(outgoing.at[expert], grad_rows.at[expert], local.at[10])]
    kept[0].start()
    for index, turn in enumerate(turns):
        first = (z + turn) % 4 * 4
        result = by_columns(active[pl.ds(index * 288, 288), :], down_w)
        for j in range(4):
            piece = result[j * CAP : j * CAP + CAP].astype(BF16)
            returned[0, first + j], returned[1, first + j] = piece[:, :512], piece[:, 512:]
    kept.append(pltpu.make_async_copy(returned, returned_out, local.at[11]))
    kept[-1].start()
    for part in range(2):
        columns = pl.ds(part * 512, 512)
        for index, right in enumerate((by_gate, by_up)):
            total = by_rows(chosen[:, columns], right[...]).astype(BF16)
            expert_grads[:, part, :, index * 512 : index * 512 + 512] = total.reshape(4, TOK, 512)
        total = 0.0
        for index, turn in enumerate(turns):
            start = pl.multiple_of((z + turn) % 4 * 288, 288)
            total += by_rows(
                back[pl.ds(start, 288), columns], active[pl.ds(index * 288, 288), :]
            )
        expert_grads[:, part, :, 1024:1536] = total.astype(BF16).reshape(4, TOK, 512)
    kept.append(pltpu.make_async_copy(expert_grads, expert_grads_out, local.at[12]))
    kept[-1].start()
    for copy in kept:
        copy.wait()
    arrived(sender.copies)
    sender.finish()


def norm_back(grad_normed, values, factor, gain):
    scaled = grad_normed * gain
    mean_term = jnp.mean(scaled * values, axis=-1, keepdims=True)
    grad_values = factor * scaled - values * factor * factor * factor * mean_term
    grad_gain = jnp.sum(grad_normed * values * factor, axis=0)
    return (grad_values, grad_gain)


def slot_matrices(routes, route_gates):
    named = (routes[:, :, None] == jnp.arange(EXPERTS, dtype=jnp.int32)).astype(F32)
    uses = jnp.sum(named, axis=1)
    gates = jnp.sum(named * route_gates[:, :, None], axis=1)
    row = lax.broadcasted_iota(jnp.int32, (TOK, TOK), 0)
    column = lax.broadcasted_iota(jnp.int32, (TOK, TOK), 1)
    earlier = (row > column).astype(BF16)
    ranks = jnp.dot(earlier, uses.astype(BF16), preferred_element_type=F32)
    slot = jnp.arange(SLOTS, dtype=jnp.int32)
    spread = (jnp.arange(EXPERTS, dtype=jnp.int32)[:, None] == slot[None, :] // CAP).astype(F32)
    both = jnp.where(uses > 0.5, ranks, -1.0).astype(BF16)
    flat = jnp.dot(both, spread.astype(BF16), preferred_element_type=F32)
    hits = flat == (slot % CAP).astype(F32)[None, :]
    flat_gates = jnp.dot(gates, spread, precision=lax.Precision.HIGHEST)
    weights = jnp.where(hits, RESIDUAL * flat_gates, 0.0)
    return (named, spread, hits.astype(BF16), weights)


def shards(
    layer_in, norm_one, w_query, key_weight, value_weight, w_output, norm_two,
    w_gate, w_up, w_down, routes, route_gates, cotangent,
):
    seq = lax.axis_index("seq")
    core = seq % 2
    key_value_resident = KEY_VALUE_HEADS // 4
    group_width = QUERY_HEADS // KEY_VALUE_HEADS
    head_width = key_value_resident * group_width * HEAD_SIZE
    kv_width = key_value_resident * HEAD_SIZE

    gains = jnp.pad(jnp.stack([norm_one, norm_two], axis=1), ((0, 0), (0, 126)))
    heads_block = jnp.concatenate(
        [
            lax.dynamic_slice_in_dim(w_query, seq * head_width, head_width, 1),
            lax.dynamic_slice_in_dim(key_weight, seq * kv_width, kv_width, 1),
            lax.dynamic_slice_in_dim(value_weight, seq * kv_width, kv_width, 1),
            gains,
        ],
        axis=1,
    )
    branch_block = lax.dynamic_slice_in_dim(w_output, core * 512, 512, 1)
    expert_block = jnp.stack(
        [
            lax.dynamic_index_in_dim(w.reshape(32, 4, 4, FF), seq, 2, keepdims=False)
            for w in (w_gate, w_up, w_down)
        ]
    ).transpose(2, 0, 1, 3)
    named = (routes[:, :, None] == jnp.arange(EXPERTS, dtype=jnp.int32)).astype(F32)
    gates_sent = jnp.sum(named * route_gates[:, :, None], axis=1).T
    gates_sent = jnp.broadcast_to(gates_sent[:, None, :], (EXPERTS, 8, TOK))

    heads_w, branch_w, tokens_all, weights_here, out_rows, gates_all = remote_call(
        gather_kernel,
        (heads_block, branch_block, layer_in, expert_block, cotangent, gates_sent),
        (
            (2, 4, 4, 32, 640),
            (2, 2, 4, 4, 32, 512),
            (2, 2, TOK, MODEL_WIDTH),
            (3, 2, 4, 32, FF),
            (4, 2, 2, TOK, MODEL_WIDTH),
            jax.ShapeDtypeStruct((EXPERTS, 8, TOK), F32),
        ),
        55,
        6,
        1,
        "gather_all",
    )
    heads_w = heads_w.reshape(MODEL_WIDTH, 640)
    branch_w = branch_w.reshape(2, MODEL_WIDTH, 512)
    weights_here = weights_here.reshape(3, 2, TOK, FF)
    expert_w = [weights_here]
    for k in (1, 2, 3):
        expert_w.append(lax.ppermute(weights_here, "x", [(i, (i + k) % 4) for i in range(4)]))

    cosine, sine = jnp.asarray(COSINE), jnp.asarray(SINE)
    hbm, vmem = pl.BlockSpec(memory_space=pltpu.HBM), pl.BlockSpec(memory_space=pltpu.VMEM)
    block = (TOK, MODEL_WIDTH)

    def arrays(*entries):
        return tuple(jax.ShapeDtypeStruct(shape, kind) for shape, kind in entries)

    def buffers(*entries):
        return [pltpu.VMEM(shape, kind) for shape, kind in entries]

    kept_arrays = (
        ((SEQ_LEN, MODEL_WIDTH), BF16),
        ((SEQ_LEN, head_width), BF16),
        ((SEQ_LEN, kv_width), BF16),
        ((SEQ_LEN, kv_width), BF16),
        ((SEQ_LEN, head_width), BF16),
        ((SEQ_LEN, TOK), F32),
        (block, F32),
        ((EXPERTS, CAP, TOK), BF16),
        ((SLOTS, MODEL_WIDTH), BF16),
    )
    table = ((SEQ_LEN, TOK), F32)
    heads_array = ((MODEL_WIDTH, 640), BF16)
    (
        normed_all, query_all, key_all, value_all, attended, sums, middle, picks, grad_back,
        rows_all, gains,
    ) = pl.pallas_call(
        forward_kernel,
        out_shape=arrays(*kept_arrays, ((4, 2, 2) + block, BF16), ((8, MODEL_WIDTH), F32)),
        in_specs=[hbm] * 7,
        out_specs=(hbm,) * 10 + (vmem,),
        scratch_shapes=buffers(
            ((4,) + block, BF16),
            heads_array,
            ((2, MODEL_WIDTH, 512), BF16),
            table,
            table,
            ((EXPERTS, 8, TOK), F32),
            ((EXPERTS,) + block, BF16),
            *kept_arrays,
            ((4, TOK, head_width), BF16),
            (block, BF16),
        )
        + [
            pltpu.SemaphoreType.DMA((21,)),
            pltpu.SemaphoreType.DMA((21,)),
            pltpu.SemaphoreType.DMA((7,)),
            pltpu.SemaphoreType.DMA((10,)),
        ],
        compiler_params=pltpu.CompilerParams(
            collective_id=7, has_side_effects=True, vmem_limit_bytes=60 * 2**20
        ),
        name="forward",
    )(
        tokens_all.reshape((4,) + block),
        heads_w,
        branch_w,
        cosine,
        sine,
        gates_all,
        out_rows.reshape((EXPERTS,) + block),
    )
    gain_first, gain_second = gains[0], gains[1]
    inputs = layer_in.astype(F32)
    factor_two = lax.rsqrt(jnp.mean(middle * middle, axis=-1, keepdims=True) + EPSILON)

    returned_array = ((2, EXPERTS, CAP, 512), BF16)
    grads_array = ((4, 2, TOK, 3 * FF), BF16)
    grad_rows, returned, expert_grads = pl.pallas_call(
        expert_kernel,
        out_shape=arrays(((EXPERTS, CAP, MODEL_WIDTH), BF16), returned_array, grads_array),
        in_specs=[hbm] * 7,
        out_specs=(hbm,) * 3,
        scratch_shapes=buffers(
            ((EXPERTS, CAP, TOK), BF16), ((SLOTS, MODEL_WIDTH), BF16), returned_array, grads_array
        )
        + [
            pltpu.VMEM((4, 4) + block, BF16),
            pltpu.VMEM((3, 2, 4, TOK, FF), BF16),
            pltpu.VMEM((EXPERTS, CAP, MODEL_WIDTH), BF16),
            pltpu.VMEM((SLOTS, MODEL_WIDTH), BF16),
            pltpu.VMEM((SLOTS, FF), BF16),
            pltpu.VMEM((SLOTS, FF), BF16),
            pltpu.VMEM((SLOTS, FF), BF16),
            pltpu.SemaphoreType.DMA((15,)),
            pltpu.SemaphoreType.DMA((15,)),
            pltpu.SemaphoreType.DMA((13,)),
        ],
        compiler_params=pltpu.CompilerParams(
            collective_id=5, has_side_effects=True, vmem_limit_bytes=60 * 2**20
        ),
        name="experts",
    )(rows_all.reshape((4, 4) + block), picks, grad_back, *expert_w)
    grad_rows = grad_rows.reshape(SLOTS, MODEL_WIDTH)
    late_routes, late_gates, grad_rows = lax.optimization_barrier((routes, route_gates, grad_rows))
    named, spread, hits, weights = slot_matrices(late_routes, late_gates)
    x_place = lax.axis_index("x")
    x_parts = [lax.dynamic_index_in_dim(expert_grads, x_place, 0, keepdims=False)]
    for k in (1, 2, 3):
        piece = lax.dynamic_index_in_dim(expert_grads, (x_place + k) % 4, 0, keepdims=False)
        x_parts.append(lax.ppermute(piece, "x", [(i, (i + k) % 4) for i in range(4)]))

    grad_out = cotangent.astype(F32)
    grad_normed_two = jnp.dot(hits, grad_rows, preferred_element_type=F32)
    grad_middle_norm, gain_two_term = norm_back(grad_normed_two, middle, factor_two, gain_second)
    grad_middle = grad_out + grad_middle_norm
    grad_branch = (RESIDUAL * grad_middle).astype(BF16)
    grad_normed, heads_term, branch_total, returned_left = pl.pallas_call(
        backward_kernel,
        out_shape=arrays(
            (block, F32),
            ((MODEL_WIDTH, 512), BF16),
            ((16, 512), BF16),
            ((EXPERTS, CAP, 512), BF16),
        ),
        in_specs=[vmem] + [hbm] * 11,
        out_specs=(vmem, vmem, vmem, hbm),
        scratch_shapes=buffers(
            ((SEQ_LEN, head_width), BF16),
            ((SEQ_LEN, head_width), BF16),
            ((SEQ_LEN, kv_width), BF16),
            ((SEQ_LEN, kv_width), BF16),
            table,
            ((SEQ_LEN, MODEL_WIDTH), BF16),
            heads_array,
            table,
            table,
        )
        + [
            pltpu.VMEM((2, 256, 512), BF16),
            pltpu.VMEM((2, 2) + block, BF16),
            pltpu.VMEM((8, 2, 16, MODEL_WIDTH), BF16),
            pltpu.VMEM((2, 2) + block, BF16),
            pltpu.VMEM((2,) + block, BF16),
            pltpu.VMEM(block, F32),
            pltpu.VMEM(block, BF16),
            pltpu.VMEM(block, BF16),
            pltpu.VMEM((3, 8, 16, 512), BF16),
            pltpu.VMEM((8, 16, 512), BF16),
            pltpu.VMEM((7, 16, 512), BF16),
            pltpu.SemaphoreType.DMA((31,)),
            pltpu.SemaphoreType.DMA((31,)),
            pltpu.SemaphoreType.DMA((11,)),
        ],
        compiler_params=pltpu.CompilerParams(
            collective_id=6, has_side_effects=True, vmem_limit_bytes=60 * 2**20
        ),
        name="backward",
    )(
        grad_branch,
        returned,
        branch_w,
        attended,
        query_all,
        key_all,
        value_all,
        sums,
        normed_all,
        heads_w,
        cosine,
        sine,
    )
    x_parts, heads_term, grad_normed = lax.optimization_barrier((x_parts, heads_term, grad_normed))
    expert_grads = (
        x_parts[0].astype(F32) + x_parts[1].astype(F32)
        + x_parts[2].astype(F32) + x_parts[3].astype(F32)
    ).astype(BF16)
    factor_one = lax.rsqrt(jnp.mean(inputs * inputs, axis=-1, keepdims=True) + EPSILON)
    grad_input_norm, gain_one_term = norm_back(grad_normed, inputs, factor_one, gain_first)
    grad_input = (grad_middle + grad_input_norm).astype(BF16)

    gain_terms = jnp.pad(
        jnp.stack([gain_one_term, gain_two_term], axis=1).astype(BF16), ((0, 0), (0, 126))
    )
    heads_term = jnp.concatenate([heads_term, gain_terms], axis=1).reshape(32, 32, 640)
    heads_four, branch_four, expert_four, returned_right = pl.pallas_call(
        finish_kernel,
        out_shape=(
            jax.ShapeDtypeStruct((2, 2, 32, 640), BF16),
            jax.ShapeDtypeStruct((4, 16, 512), BF16),
            jax.ShapeDtypeStruct((2, 2, 4, 32, 3 * FF), BF16),
            jax.ShapeDtypeStruct((EXPERTS, CAP, 512), BF16),
        ),
        in_specs=[vmem] * 3 + [hbm],
        out_specs=(hbm,) * 4,
        scratch_shapes=[
            pltpu.VMEM((3, 2, 4, 16, 640), BF16),
            pltpu.VMEM((3, 2, 4, 16, 640), BF16),
            pltpu.VMEM((2, 4, 16, 640), BF16),
            pltpu.VMEM((2, 4, 16, 640), BF16),
            pltpu.VMEM((7, 16, 640), BF16),
            pltpu.VMEM((7, 16, 640), BF16),
            pltpu.VMEM((2, 4, 32, 3 * FF), BF16),
            pltpu.VMEM((32, 640), BF16),
            pltpu.VMEM((4, 32, 3 * FF), BF16),
            pltpu.SemaphoreType.DMA((48,)),
            pltpu.SemaphoreType.DMA((48,)),
            pltpu.SemaphoreType.DMA((3,)),
            pltpu.SemaphoreType.DMA((4,)),
            pltpu.SemaphoreType.DMA((4,)),
        ],
        compiler_params=pltpu.CompilerParams(
            collective_id=2, has_side_effects=True, vmem_limit_bytes=60 * 2**20
        ),
        name="finish",
    )(
        heads_term.reshape(2, 4, 4, 32, 640),
        branch_total,
        expert_grads.reshape(2, 4, 32, 3 * FF),
        returned,
    )
    halves = [half.reshape(SLOTS, 512) for half in (returned_left, returned_right)]
    mixed = [
        jnp.dot(weights.astype(BF16), half, preferred_element_type=F32) for half in halves
    ]
    layer_out = (middle + jnp.concatenate(mixed, axis=1)).astype(BF16)
    pair_dots = sum(
        jnp.einsum("td,jd->tj", cotangent[:, k * 512 : k * 512 + 512], half, preferred_element_type=F32)
        for k, half in enumerate(halves)
    )
    expert_dots = jnp.einsum(
        "tj,ej->te", pair_dots * hits.astype(F32), spread, precision=lax.Precision.HIGHEST
    )
    grad_gates = RESIDUAL * jnp.sum(named * expert_dots[:, None, :], axis=-1)
    gain_sums = jnp.sum(heads_four[:, :, :, 512:514].astype(F32), axis=(0, 1))
    projections = pl.pallas_call(
        unpack_kernel,
        out_shape=tuple(
            jax.ShapeDtypeStruct(shape, F32)
            for shape in ((32, 1024), (32, 512), (32, 512), (32, 1024)) + ((32, EXPERTS, FF),) * 3
        ),
        in_specs=[vmem] * 3,
        out_specs=(vmem,) * 7,
        compiler_params=pltpu.CompilerParams(vmem_limit_bytes=16 * 2**20),
        name="unpack",
    )(heads_four, branch_four, expert_four)
    experts_out = projections[4:]
    return (
        layer_out,
        grad_input,
        gain_sums[:, 0],
        projections[0],
        projections[1],
        projections[2],
        projections[3],
        gain_sums[:, 1],
        experts_out[0],
        experts_out[1],
        experts_out[2],
        grad_gates,
    )


def solution(mesh):
    dp = ("yh", "x", "z")
    cut = Mesh(mesh.devices.reshape(2, 4, 4, 4), AXES)
    tokens, rows, gain, experts = P(AXES, None), P(dp, None), P(dp), P(dp, None, None)
    return jax.shard_map(
        shards,
        mesh=cut,
        in_specs=(
            tokens, gain, rows, rows, rows, rows, gain, experts, experts, experts,
            tokens, tokens, tokens,
        ),
        out_specs=(
            tokens, tokens, gain, rows, rows, rows, rows, gain, experts, experts, experts, tokens,
        ),
        check_vma=False,
    )
```

time: 290 us -> 261 us (0.900)
  Pallas kernels: 196 us -> 218 us
  matrix products: 28.1 us -> 8.09 us
  waiting for transfers between devices: 13.4 us -> 0.02 us
  local copies, waits for them, and re-layouts: 23.4 us -> 13.7 us
  starting transfers between devices: 10.7 us -> 7.18 us
  other arithmetic: 15.6 us -> 12.2 us
    pallas_call x7 -> x4, Pallas kernels: 149 us -> 170 us  [the longest x1 52.6 us: remote_call(): pl.pallas_call(kernel, out_shape=tuple((shape if isinstance(shape, jax.Sh...]
    dot_general x18 -> x4, matrix products: 23.2 us -> 4.4 us  [the longest x2 3.72 us: shards(): jnp.einsum('td,jd->tj', cotangent[:, k * 512:k * 512 + 512], half, prefer...]
    all_to_all x2 -> x0, waiting for transfers between devices: 13.4 us -> none  [to_group(): lax.all_to_all(blocks, ('z', 'seq'), 0, 0, tiled=True)]
    all_to_all x2 -> x0, starting transfers between devices: 8.4 us -> none  [to_group(): lax.all_to_all(blocks, ('z', 'seq'), 0, 0, tiled=True)]
    unnamed x143 -> x59, local copies, waits for them, and re-layouts: 8.1 us -> 1.72 us
    ppermute x3 -> x6, starting transfers between devices: 2.29 us -> 7.18 us  [the longest x3 4.05 us: shards(): lax.ppermute(piece, 'x', [(i, (i + k) % 4) for i in range(4)])]
    convert_element_type x8 -> x0, other arithmetic: 3.12 us -> none  [the longest x1 1.19 us: shards(): grad_scores = (probs * (grad_probs - inner)).astype(BF16)]
  transfers between devices with their start and end apart: 5 -> 6, of which waited for: 1 -> 0; matrix products, arithmetic and copies ran while one was open for 7% -> 3% of each run, Pallas kernels for 14% -> 32%
where the time goes in v3:
time: 261 us; the launch traced here: 260 us
  Pallas kernels  218 us (84%)
  local copies, waits for them, and re-layouts  13.7 us (5%)
  other arithmetic  12.2 us (5%)
  matrix products  8.09 us (3%)
  starting transfers between devices  7.18 us (3%)
    pallas_call x1, Pallas kernels, remote_call(): pl.pallas_call(kernel, out_shape=tuple((shape if isinstance(shape, jax.Sh...  52.6 us
    pallas_call x1, Pallas kernels, shards(): pl.pallas_call(finish_kernel, out_shape=(jax.ShapeDtypeStruct((2, 2, 32,...  45.4 us
    pallas_call x1, Pallas kernels, shards(): pl.pallas_call(backward_kernel, out_shape=arrays((block, F32), ((MODEL_WI...  41.4 us
    pallas_call x1, Pallas kernels, shards(): pl.pallas_call(forward_kernel, out_shape=arrays(*kept_arrays, ((4, 2, 2)...  40.5 us
    pallas_call x1, Pallas kernels, shards(): pl.pallas_call(expert_kernel, out_shape=arrays(((EXPERTS, CAP, MODEL_WIDT...  35.2 us
  transfers between devices with their start and end apart: 6, of which 0 were waited for; matrix products, arithmetic and copies ran while one was open for 3% of the time, Pallas kernels for 32%

profile of v3, /device:TPU:1, one launch (start us, length us, event | category | flops | bytes accessed | tf_op | source)
XLA Modules:
  0.0 260.2 jit_solution(5800230812593374990)
XLA Ops:
  0.7 0.7 pad_maximum_fusion.1
  1.4 0.1 copy.73
  1.5 1.2 reshape.127
  2.7 1.2 reshape.128
  3.9 0.6 constant_dynamic-slice_fusion
  4.6 0.1 copy.89
  4.7 0.1 reshape.126
  4.8 0.3 constant_dynamic-slice_fusion.2
  5.2 0.6 constant_dynamic-slice_fusion.3.branch
  5.8 0.7 constant_dynamic-slice_fusion.6
  6.6 0.7 constant_dynamic-slice_fusion.4
  7.3 0.8 maximum_bitcast_fusion.experts
  8.1 0.6 fusion.23.heads
  8.7 0.6 broadcast_in_dim.8.gates
  9.3 52.6 %gather_all.1 = (bf16[2,4,4,32,640]{4,3,2,1,0:T(8,128)(2,1)}, bf16[2,2,4,4,32,512]{5,4,3,2,1,0:T(8,128)(2,1)}, bf16[2,2,128,1024]{3,2,1,0:T(8,128)(2,1)}, bf16[3...) custom-call(bf16[32,640]{1,0:T(8,128)(2,1)} %fusion.23.heads, ...), custom_call_target="tpu_custom_call" | custom-call | tf_op jit(solution)/shard_map/gather_all/pallas_call | solution.py:78
  62.0 1.1 collective-permute-start.1
  63.1 2.0 collective-permute-start.2
  65.1 0.1 fusion.9
  65.2 40.5 %forward.1 = (bf16[512,1024]{1,0:T(8,128)(2,1)}, bf16[512,256]{1,0:T(8,128)(2,1)}, bf16[512,128]{1,0:T(8,128)(2,1)}, bf16[512,128]{1,0:T(8,128)(2,1)}, bf16[512,...) custom-call(bf16[4,128,1024]{2,1,0:T(8,128)(2,1)} %bitcast.62, ...), custom_call_target="tpu_custom_call" | custom-call | tf_op jit(solution)/shard_map/forward/pallas_call | solution.py:853
  105.7 1.2 multiply_reduce_fusion.2
  107.0 0.8 fusion.42
  107.9 0.8 copy-done.10
  108.7 0.3 copy-done.11
  109.0 0.3 copy-done.12
  109.2 35.2 %experts.1 = (bf16[16,72,1024]{2,1,0:T(8,128)(2,1)}, bf16[2,16,72,512]{3,2,1,0:T(8,128)(2,1)}, bf16[4,2,128,1536]{3,2,1,0:T(8,128)(2,1)}) custom-call(bf16[4,4,128,1024]{3,2,1,0:T(8,128)(2,1)} %bitcast.59, bf16[16,72,128]{2,1,0:T(8,128)(2,1)} %get-tuple-element.63.picks_in, bf16[1152,1024]{1,0:T(8,128)(2,1)} %get-tuple-element.64.back_in, ...), custom_call_target="tpu_custom_call" | custom-call | tf_op jit(solution)/shard_map/experts/pallas_call | solution.py:895
  144.5 3.4 %dynamic-slice_bitcast_fusion = (bf16[2,128,1536]{2,1,0:T(8,128)(2,1)}, bf16[2,128,1536]{2,1,0:T(8,128)(2,1)}, bf16[2,128,1536]{2,1,0:T(8,128)(2,1)}, bf16[2,128,1536]{2,1,0:T(8,128)(2,1)S(1)}) fusion(bf16[4,2,128,1536]{3,2,1,0:T(8,128)(2,1)} %get-tuple-element.79, s32[]{:T(128)S(6)} %select_n.95, s32[]{:T(128)S(6)} %select_n.93, s32[]{:T(128)S(6)} %select_n.91, ...), kind=kLoop, calls=%fused_computation.17 | loop fusion | bytes 6291472 | tf_op jit(solution)/shard_map/jit(dynamic_index_in_dim)/squeeze | solution.py:926
  147.9 0.4 collective-permute-start.3
  148.3 1.6 collective-permute-start.4
  149.9 2.1 collective-permute-start.5
  151.9 0.4 convolution_compare_fusion
  152.4 2.4 multiply_reduce_fusion.1
  154.9 0.9 multiply_convert_fusion.block
  155.8 41.4 %backward.1 = (f32[128,1024]{1,0:T(8,128)}, bf16[1024,512]{1,0:T(8,128)(2,1)}, bf16[16,512]{1,0:T(8,128)(2,1)}, bf16[16,72,512]{2,1,0:T(8,128)(2,1)}) custom-call(bf16[128,1024]{1,0:T(8,128)(2,1)} %multiply_convert_fusion.block, bf16[2,16,72,512]{3,2,1,0:T(8,128)(2,1)} %get-tuple-element.71.returned.rows, bf16[2,1024,512]{2,1,0:T(8,128)(2,1)} %bitcast.50, ...), custom_call_target="tpu_custom_call" | custom-call | tf_op jit(solution)/shard_map/backward/pallas_call | solution.py:934
  197.3 1.8 fusion.19
  199.2 0.7 fusion.16
  199.9 0.9 copy.77
  200.8 2.5 fusion.5
  203.3 2.9 %add_convert_fusion = bf16[2,128,1536]{2,1,0:T(8,128)(2,1)} fusion(bf16[2,128,1536]{2,1,0:T(8,128)(2,1)} %collective-permute-done.5, bf16[2,128,1536]{2,1,0:T(8,128)(2,1)} %collective-permute-done.4, bf16[2,128,1536]{2,1,0:T(8,128)(2,1)} %collective-permute-done.3, bf16[2,128,1536]{2,1,0:T(8,128)(2,1)S(1)} %get-tuple-element.85), kind=kLoop, calls=%fused_computation.9 | loop fusion | flops 3145728 | bytes 3932160 | tf_op jit(solution)/shard_map/convert_element_type | solution.py:993
  206.1 45.4 %finish.1 = (bf16[2,2,32,640]{3,2,1,0:T(8,128)(2,1)}, bf16[4,16,512]{2,1,0:T(8,128)(2,1)}, bf16[2,2,4,32,1536]{4,3,2,1,0:T(8,128)(2,1)}, bf16[16,72,512]{2,1,0:T(8,128)(2,1)}) custom-call(bf16[2,4,4,32,640]{4,3,2,1,0:T(8,128)(2,1)} %bitcast.51, bf16[16,512]{1,0:T(8,128)(2,1)} %get-tuple-element.84.branch_sum, bf16[2,4,32,1536]{3,2,1,0:T(8,128)(2,1)} %bitcast.60, ...), custom_call_target="tpu_custom_call" | custom-call | tf_op jit(solution)/shard_map/finish/pallas_call | solution.py:1002
  251.6 1.9 fusion.3
  253.5 0.4 fusion.22
  254.0 0.5 fusion.4
  254.5 0.3 fusion.43
  254.9 0.3 fusion.44
  255.3 0.6 broadcast_multiply_fusion
  255.9 0.7 slice_reduce_fusion
  256.6 2.5 unpack.1
  259.1 1.1 fusion.15
  (74 shorter events, 0.5 us)
Async XLA Ops:
  0.6 4.6 %copy-start = (bf16[32,1024]{1,0:T(8,128)(2,1)S(1)}, bf16[32,1024]{1,0:T(8,128)(2,1)}, u32[]{:S(2)}) copy-start(bf16[32,1024]{1,0:T(8,128)(2,1)} %param.20) | copy-start | bytes 196612
  2.7 2.0 copy-start.15
  4.5 2.1 copy-start.16
  4.5 2.1 copy-start.19
  4.8 60.3 %copy-start.7 = (bf16[128,1024]{1,0:T(8,128)(2,1)S(1)}, bf16[128,1024]{1,0:T(8,128)(2,1)}, u32[]{:S(2)}) copy-start(bf16[128,1024]{1,0:T(8,128)(2,1)} %tokens.1) | copy-start | bytes 786436
  61.9 45.9 %collective-permute-start = (bf16[3,2,128,512]{3,2,1,0:T(8,128)(2,1)}, bf16[3,2,128,512]{3,2,1,0:T(8,128)(2,1)S(1)}, u32[]{:S(2)}, u32[]{:S(2)}) collective-permute-start(bf16[3,2,128,512]{3,2,1,0:T(8,128)(2,1)} %bitcast.63), channel_id=1, source_target_pairs={{0,16},{16,32},{32,48},{48,0},{1,17},{17,33},{33,49},{49,1},{2,18}... | collective-permute-start | bytes 2359304 | tf_op jit(solution)/shard_map/ppermute | solution.py:825
  62.0 45.9 %collective-permute-start.1 = (bf16[3,2,128,512]{3,2,1,0:T(8,128)(2,1)}, bf16[3,2,128,512]{3,2,1,0:T(8,128)(2,1)S(1)}, u32[]{:S(2)}, u32[]{:S(2)}) collective-permute-start(bf16[3,2,128,512]{3,2,1,0:T(8,128)(2,1)} %bitcast.64), channel_id=1, source_target_pairs={{0,32},{16,48},{32,0},{48,16},{1,33},{17,49},{33,1},{49,17},{2,34}... | collective-permute-start | bytes 2359304 | tf_op jit(solution)/shard_map/ppermute | solution.py:825
  63.1 44.8 %collective-permute-start.2 = (bf16[3,2,128,512]{3,2,1,0:T(8,128)(2,1)}, bf16[3,2,128,512]{3,2,1,0:T(8,128)(2,1)S(1)}, u32[]{:S(2)}, u32[]{:S(2)}) collective-permute-start(bf16[3,2,128,512]{3,2,1,0:T(8,128)(2,1)} %bitcast.65), channel_id=1, source_target_pairs={{0,48},{16,0},{32,16},{48,32},{1,49},{17,1},{33,17},{49,33},{2,50}... | collective-permute-start | bytes 2359304 | tf_op jit(solution)/shard_map/ppermute | solution.py:825
  106.9 45.0 %copy-start.17 = (s32[1152]{0:T(1024)}, s32[1152]{0:T(1024)S(1)}, u32[]{:S(2)}) copy-start(s32[1152]{0:T(1024)S(1)} %get-tuple-element.121) | copy-start | bytes 13828
  107.0 47.9 %copy-start.21 = (f32[128]{0:T(128)}, f32[128]{0:T(128)S(1)}, u32[]{:S(2)}) copy-start(f32[128]{0:T(128)S(1)} %add_rsqrt_fusion.1) | copy-start | bytes 1540
  107.0 92.2 %copy-start.23 = (f32[128]{0:T(128)}, f32[128]{0:T(128)S(1)}, u32[]{:S(2)}) copy-start(f32[128]{0:T(128)S(1)} %add_rsqrt_fusion) | copy-start | bytes 1540
  107.8 0.9 copy-start.10
  107.9 1.1 copy-start.11
  107.9 1.4 copy-start.12
  144.5 7.9 %copy-start.4 = (f32[128,1024]{1,0:T(8,128)S(1)}, f32[128,1024]{1,0:T(8,128)}, u32[]{:S(2)}) copy-start(f32[128,1024]{1,0:T(8,128)} %get-tuple-element.61) | copy-start | bytes 1572868
  147.9 51.2 %collective-permute-start.3 = (bf16[2,128,1536]{2,1,0:T(8,128)(2,1)}, bf16[2,128,1536]{2,1,0:T(8,128)(2,1)}, u32[]{:S(2)}, u32[]{:S(2)}) collective-permute-start(bf16[2,128,1536]{2,1,0:T(8,128)(2,1)} %get-tuple-element.110), channel_id=1, source_target_pairs={{0,16},{16,32},{32,48},{48,0},{1,17},{17,33},{33,49},{49,1},{2,18}... | collective-permute-start | bytes 2359304 | tf_op jit(solution)/shard_map/ppermute | solution.py:927
  148.3 50.9 %collective-permute-start.4 = (bf16[2,128,1536]{2,1,0:T(8,128)(2,1)}, bf16[2,128,1536]{2,1,0:T(8,128)(2,1)}, u32[]{:S(2)}, u32[]{:S(2)}) collective-permute-start(bf16[2,128,1536]{2,1,0:T(8,128)(2,1)} %get-tuple-element.109), channel_id=1, source_target_pairs={{0,32},{16,48},{32,0},{48,16},{1,33},{17,49},{33,1},{49,17},{2,34}... | collective-permute-start | bytes 2359304 | tf_op jit(solution)/shard_map/ppermute | solution.py:927
  149.9 49.3 %collective-permute-start.5 = (bf16[2,128,1536]{2,1,0:T(8,128)(2,1)}, bf16[2,128,1536]{2,1,0:T(8,128)(2,1)}, u32[]{:S(2)}, u32[]{:S(2)}) collective-permute-start(bf16[2,128,1536]{2,1,0:T(8,128)(2,1)} %get-tuple-element.108), channel_id=1, source_target_pairs={{0,48},{16,0},{32,16},{48,32},{1,49},{17,1},{33,17},{49,33},{2,50}... | collective-permute-start | bytes 2359304 | tf_op jit(solution)/shard_map/ppermute | solution.py:927
  152.4 2.4 copy-start.13
  152.4 2.5 copy-start.8
  154.8 1.0 copy-start.25
  197.3 1.9 copy-start.9
  206.1 45.5 %copy-start.14 = (pred[128,1152]{1,0:T(32,128)(4,1)S(1)}, pred[128,1152]{1,0:T(32,128)(4,1)}, u32[]{:S(2)}) copy-start(pred[128,1152]{1,0:T(32,128)(4,1)} %copy-done.13) | copy-start | bytes 442372
  251.6 1.9 copy-start.18
  251.6 2.3 copy-start.20
  251.6 2.9 %copy-start.6 = (bf16[16,72,512]{2,1,0:T(8,128)(2,1)S(1)}, bf16[16,72,512]{2,1,0:T(8,128)(2,1)}, u32[]{:S(2)}) copy-start(bf16[16,72,512]{2,1,0:T(8,128)(2,1)} %get-tuple-element.78) | copy-start | bytes 3538948
  253.5 1.4 copy-start.5
  254.5 0.8 copy-start.27
  254.5 1.4 copy-start.2
  254.5 2.1 copy-start.1
  254.5 2.1 copy-start.3
  254.9 4.2 %copy-start.22 = (f32[128]{0:T(128)S(1)}, f32[128]{0:T(128)}, u32[]{:S(2)}) copy-start(f32[128]{0:T(128)} %copy-done.21) | copy-start | bytes 1540
  254.9 4.2 %copy-start.24 = (f32[128]{0:T(128)S(1)}, f32[128]{0:T(128)}, u32[]{:S(2)}) copy-start(f32[128]{0:T(128)} %copy-done.23) | copy-start | bytes 1540
  254.9 4.2 %copy-start.26 = (f32[128]{0:T(128)S(1)}, f32[128]{0:T(128)}, u32[]{:S(2)}) copy-start(f32[128]{0:T(128)} %copy-done.25) | copy-start | bytes 1540

commit v4 on v3

v4 whole, which is shorter than its diff:
```python
import jax
import jax.numpy as jnp
import numpy as np
from jax import lax
from jax.experimental import pallas as pl
from jax.experimental.pallas import tpu as pltpu
from jax.sharding import Mesh
from jax.sharding import PartitionSpec as P

MODEL_WIDTH = 1024
QUERY_HEADS = 16
KEY_VALUE_HEADS = 8
HEAD_SIZE = 64
TOP = 8
EXPERTS = 16
CAP = 72
SLOTS = EXPERTS * CAP
TOK = 128
SEQ_LEN = 512
FF = 512
EPSILON = 1e-05
RESIDUAL = 0.22
ROPE_BASE = 10000.0
MASK_VALUE = -1e30

PLACES = np.arange(SEQ_LEN, dtype=np.float32)
FREQUENCIES = (ROPE_BASE ** (-np.arange(0, HEAD_SIZE, 2) / HEAD_SIZE)).astype(np.float32)
TURNS = PLACES[:, None] * np.tile(FREQUENCIES, 4)[None, :]
COSINE = np.cos(TURNS).astype(np.float32)
SINE = np.where(np.arange(TOK) % HEAD_SIZE < 32, -np.sin(TURNS), np.sin(TURNS)).astype(np.float32)

BF16 = jnp.bfloat16
F32 = jnp.float32
AXES = ("yh", "x", "z", "seq")
BY_ID = pl.DeviceIdType.MESH


def place():
    return tuple(lax.axis_index(axis) for axis in AXES)


class Sender:
    def __init__(self, send, recv):
        self.send, self.recv, self.used, self.copies = send, recv, 0, []

    def start(self, source, target, device):
        copy = pltpu.make_async_remote_copy(
            src_ref=source,
            dst_ref=target,
            send_sem=self.send.at[self.used],
            recv_sem=self.recv.at[self.used],
            device_id=device,
            device_id_type=BY_ID,
        )
        copy.start()
        self.used += 1
        self.copies.append(copy)
        return copy

    def finish(self):
        for copy in self.copies:
            copy.wait_send()


def arrived(copies):
    for copy in copies:
        copy.wait_recv()


def greet(partners):
    barrier = pltpu.get_barrier_semaphore()
    for partner in partners:
        pl.semaphore_signal(barrier, inc=1, device_id=partner, device_id_type=BY_ID)
    pl.semaphore_wait(barrier, len(partners))


def remote_call(kernel, inputs, outputs, scratch, copies, local_copies, collective_id, name):
    return pl.pallas_call(
        kernel,
        out_shape=tuple(
            shape if isinstance(shape, jax.ShapeDtypeStruct) else jax.ShapeDtypeStruct(shape, BF16)
            for shape in outputs
        ),
        in_specs=[pl.BlockSpec(memory_space=pltpu.HBM)] * len(inputs),
        out_specs=tuple(pl.BlockSpec(memory_space=pltpu.HBM) for _ in outputs),
        scratch_shapes=scratch
        + [
            pltpu.SemaphoreType.DMA((copies,)),
            pltpu.SemaphoreType.DMA((copies,)),
            pltpu.SemaphoreType.DMA((local_copies,)),
        ],
        compiler_params=pltpu.CompilerParams(collective_id=collective_id, has_side_effects=True),
        name=name,
    )(*inputs)


def local_starts(pairs, sems):
    copies = []
    for index, (source, target) in enumerate(pairs):
        copy = pltpu.make_async_copy(source, target, sems.at[index])
        copy.start()
        copies.append(copy)
    return copies


def group_of(x, z, seq, yh):
    yl, core = seq // 2, seq % 2
    return [
        (yh, x, (z + k // 4) % 4, (yl + (k // 2) % 2) % 2 * 2 + (core + k % 2) % 2)
        for k in range(1, 16)
    ]


class Blocks:
    def __init__(self, sender, block, blocks_all):
        yh, x, z, seq = place()
        self.yl, self.core = seq // 2, seq % 2
        self.sender, self.z, self.blocks = sender, z, blocks_all
        self.near = (yh, x, z, (1 - self.yl) * 2 + self.core)
        self.sibling = (yh, x, z, self.yl * 2 + 1 - self.core)
        self.along_z = [(yh, x, (z + k) % 4, seq) for k in (1, 2, 3)]
        own = blocks_all.at[z, self.yl, self.core]
        self.to_near = sender.start(block, own, self.near)
        self.to_z = [sender.start(block, own, partner) for partner in self.along_z]
        self.to_sibling = [sender.start(block, own, self.sibling)]

    def again(self, ref, partner):
        return self.sender.start(ref, ref, partner)

    def forward(self):
        arrived([self.to_near])
        beside = self.blocks.at[self.z, 1 - self.yl, self.core]
        self.passed = [self.again(beside.at[pl.ds(0, 64)], partner) for partner in self.along_z]
        self.to_sibling.append(self.again(beside, self.sibling))
        for k, copy in enumerate(self.to_z):
            arrived([copy])
            block = self.blocks.at[(self.z + 3 - k) % 4, self.yl, self.core]
            self.passed.append(self.again(block.at[pl.ds(64, 64)], self.near))
            self.to_sibling.append(self.again(block, self.sibling))

    def finish(self):
        for k in range(3):
            arrived([self.passed[k], self.passed[k + 3]])
            block = self.blocks.at[(self.z + 3 - k) % 4, 1 - self.yl, self.core]
            self.to_sibling.append(self.again(block, self.sibling))
        arrived(self.to_sibling)


def gather_kernel(
    w_query, key_weight, value_weight, w_output, gains, tokens, w_gate, w_up, w_down, gates,
    heads_all, branch_all, tokens_all, experts_all, gates_all,
    heads, weights, experts, send, recv, local,
):
    yh, x, z, seq = place()
    yl, core = seq // 2, seq % 2
    along_y = (1 - yh, x, z, seq)
    along_x = [(yh, (x + k) % 4, z, seq) for k in (1, 2, 3)]
    along_z = [(yh, x, (z + k) % 4, seq) for k in (1, 2, 3)]
    near = (yh, x, z, (1 - yl) * 2 + core)
    sibling = (yh, x, z, yl * 2 + 1 - core)
    group = [
        (yh, x, (z + k // 4) % 4, (yl + (k // 2) % 2) % 2 * 2 + (core + k % 2) % 2)
        for k in range(1, 16)
    ]
    expert = z * 4 + seq
    wide = pl.ds(pl.multiple_of(seq * 256, 256), 256)
    narrow = pl.ds(pl.multiple_of(seq * 128, 128), 128)
    branch = w_output.at[:, pl.ds(pl.multiple_of(core * 512, 512), 512)]
    built = local_starts(
        [
            (w_query.at[:, wide], heads.at[:, pl.ds(0, 256)]),
            (key_weight.at[:, narrow], heads.at[:, pl.ds(256, 128)]),
            (value_weight.at[:, narrow], heads.at[:, pl.ds(384, 128)]),
            (gains, heads.at[:, pl.ds(512, 128)]),
            (w_gate, weights.at[0]),
            (w_up, weights.at[1]),
            (w_down, weights.at[2]),
        ],
        local,
    )
    greet([along_y] + along_x + group)
    sender = Sender(send, recv)
    for copy in built[:4]:
        copy.wait()
    first = [
        sender.start(heads, heads_all.at[yh, x, z], along_y),
        sender.start(branch, branch_all.at[core, yh, x, z], along_y),
    ]
    token_copies = [
        sender.start(tokens, tokens_all.at[yl, core], near),
        sender.start(tokens, tokens_all.at[yl, core], sibling),
    ]
    own = []
    for source, target in (
        (heads, heads_all.at[yh, x, z]),
        (branch, branch_all.at[core, yh, x, z]),
        (tokens, tokens_all.at[yl, core]),
        (gates.at[expert], gates_all.at[expert]),
    ):
        own.append(pltpu.make_async_copy(source, target, local.at[7 + len(own)]))
        own[-1].start()
    for copy in built[4:]:
        copy.wait()
    row = lax.broadcasted_iota(jnp.int32, (TOK, 512), 0)
    column = lax.broadcasted_iota(jnp.int32, (TOK, 512), 1)
    same = jnp.logical_and(column // 16 == row % 32, column % 16 == row // 32 * 4 + seq)
    picker = jnp.where(same, 1.0, 0.0).astype(BF16)
    for k in range(3):
        picked = jnp.dot(picker, weights[k], preferred_element_type=F32).astype(BF16)
        experts[:, k] = picked.reshape(4, 32, FF)
    expert_first = [
        sender.start(experts.at[partner[2]], experts_all.at[:, yh, z], partner)
        for partner in along_z
    ]
    own.append(pltpu.make_async_copy(experts.at[z], experts_all.at[:, yh, z], local.at[11]))
    own[-1].start()
    for copy in own[:2]:
        copy.wait()
    arrived(first)
    second = []
    for k in range(3):
        source = heads_all.at[:, x, z]
        second.append(sender.start(source, source, along_z[k]))
        source = branch_all.at[core, :, x, z]
        second.append(sender.start(source, source, along_x[k]))
    own[4].wait()
    arrived(expert_first)
    mine = experts_all.at[:, yh]
    expert_second = [sender.start(mine, mine, along_y)]
    arrived(second)
    third = []
    for k in range(3):
        source = heads_all.at[:, x]
        third.append(sender.start(source, source, along_x[k]))
        source = branch_all.at[core, :, :, z]
        third.append(sender.start(source, source, along_z[k]))
    gate_copies = [
        sender.start(gates.at[partner[2] * 4 + partner[3]], gates_all.at[expert], partner)
        for partner in group
    ]
    arrived(token_copies)
    far = tokens_all.at[1 - yl, core]
    last = [sender.start(far, far, sibling)]
    for copy in own[2:4]:
        copy.wait()
    arrived(third)
    half = branch_all.at[core]
    last.append(sender.start(half, half, sibling))
    arrived(expert_second)
    arrived(gate_copies)
    arrived(last)
    sender.finish()


def by_rows(left, right):
    return lax.dot_general(left, right, (((0,), (0,)), ((), ())), preferred_element_type=F32)


def by_columns(left, right):
    return lax.dot_general(left, right, (((1,), (1,)), ((), ())), preferred_element_type=F32)


def half_turn(values):
    lane = lax.broadcasted_iota(jnp.int32, values.shape, 1)
    return jnp.where(lane % 64 < 32, pltpu.roll(values, 96, 1), pltpu.roll(values, 32, 1))


def causal_scores(query, key):
    row = lax.broadcasted_iota(jnp.int32, (SEQ_LEN, SEQ_LEN), 0)
    column = lax.broadcasted_iota(jnp.int32, (SEQ_LEN, SEQ_LEN), 1)
    return jnp.where(row >= column, by_columns(query, key) * (1.0 / HEAD_SIZE), MASK_VALUE)


def forward_kernel(
    tokens_in, heads_in, branch_in, cosine_in, sine_in, gates_in, out_in, weights_in, own_gates,
    normed_out, query_out, key_out, value_out, attended_out, sums_out, middle_out, picks_out,
    back_out, hits_out, shares_out, rows_all, weights_all, gains,
    tokens, heads_w, branch_here, cosine, sine, gates, out_here,
    normed, query, key, value, attended, sums, middle, picks, back, hits, shares,
    traded, rows, send, recv, fetch, keep,
):
    yh, x, z, seq = place()
    yl, core = seq // 2, seq % 2
    along_z = [(yh, x, (z + k) % 4, seq) for k in (1, 2, 3)]
    beside = [(yh, x, z, (seq + k) % 4) for k in (1, 2, 3)]
    fetched = local_starts(
        [
            (heads_in, heads_w), (tokens_in, tokens), (cosine_in, cosine), (sine_in, sine),
            (branch_in, branch_here), (gates_in, gates), (out_in, out_here.at[z, yl, core]),
        ],
        fetch,
    )
    along_x = [(yh, (x + k) % 4, z, seq) for k in (1, 2, 3)]
    greet(along_z + beside + along_x)
    sender = Sender(send, recv)
    out_blocks = Blocks(sender, out_in, out_here)
    weights = [
        sender.start(weights_in, weights_all.at[:, :, x], partner) for partner in along_x
    ]
    for copy in fetched[:4]:
        copy.wait()
    gains[...] = heads_w[:, 512:640].astype(F32).T[0:8]
    sequence = tokens[...].reshape(SEQ_LEN, MODEL_WIDTH).astype(F32)
    factor = lax.rsqrt(jnp.mean(sequence * sequence, axis=-1, keepdims=True) + EPSILON)
    normed[...] = (sequence * factor * gains[0:1]).astype(BF16)
    projected = jnp.dot(normed[...], heads_w[:, 0:512], preferred_element_type=F32)
    for k in range(2):
        part = projected[:, k * 128 : k * 128 + 128]
        query[:, k * 128 : k * 128 + 128] = (
            part * cosine[...] + half_turn(part) * sine[...]
        ).astype(BF16)
    part = projected[:, 256:384]
    key[...] = (part * cosine[...] + half_turn(part) * sine[...]).astype(BF16)
    value[...] = projected[:, 384:512].astype(BF16)
    lane = lax.broadcasted_iota(jnp.int32, (SEQ_LEN, TOK), 1)
    all_sums = jnp.zeros((SEQ_LEN, TOK), F32)
    for k in range(2):
        results = []
        key_head, value_head = key[:, k * 64 : k * 64 + 64], value[:, k * 64 : k * 64 + 64]
        for g in range(2):
            head = k * 2 + g
            scores = causal_scores(query[:, head * 64 : head * 64 + 64], key_head)
            top = jnp.max(scores, axis=-1, keepdims=True)
            exponent = jnp.exp(scores - top)
            total = jnp.sum(exponent, axis=-1, keepdims=True)
            probs = (exponent / total).astype(BF16)
            all_sums = jnp.where(lane == head, top + jnp.log(total), all_sums)
            results.append(jnp.dot(probs, value_head, preferred_element_type=F32))
        attended[:, k * 128 : k * 128 + 128] = jnp.concatenate(results, axis=1).astype(BF16)
    sums[...] = all_sums

    trades = []
    for partner in beside:
        start = pl.multiple_of(partner[3] * TOK, TOK)
        trades.append(sender.start(attended.at[pl.ds(start, TOK)], traded.at[seq], partner))
    traded[seq] = attended[pl.ds(pl.multiple_of(seq * TOK, TOK), TOK), :]
    out_blocks.forward()
    kept = local_starts(
        [
            (normed, normed_out), (query, query_out), (key, key_out), (value, value_out),
            (attended, attended_out), (sums, sums_out),
        ],
        keep,
    )
    fetched[4].wait()
    arrived(trades)
    here = jnp.concatenate([traded[k] for k in range(4)], axis=1)
    branch = jnp.concatenate(
        [jnp.dot(here, branch_here[k], preferred_element_type=F32) for k in range(2)], axis=1
    )
    mid = tokens[seq].astype(F32) + RESIDUAL * branch
    middle[...] = mid
    factor = lax.rsqrt(jnp.mean(mid * mid, axis=-1, keepdims=True) + EPSILON)
    rows[...] = (mid * factor * gains[1:2]).astype(BF16)

    blocks = Blocks(sender, rows, rows_all)
    for index, (source, target) in enumerate(
        ((rows, rows_all.at[z, yl, core]), (middle, middle_out))
    ):
        kept.append(pltpu.make_async_copy(source, target, keep.at[6 + index]))
        kept[-1].start()
    for copy in fetched[5:]:
        copy.wait()
    out_blocks.finish()
    row = lax.broadcasted_iota(jnp.int32, (TOK, TOK), 0)
    column = lax.broadcasted_iota(jnp.int32, (TOK, TOK), 1)
    earlier = jnp.where(row < column, 1.0, 0.0).astype(BF16)
    slot = lax.broadcasted_iota(jnp.int32, (CAP, TOK), 0).astype(F32)

    def two(index, carry):
        parts = []
        for j in range(2):
            gate = gates[index * 2 + j]
            named = jnp.where(gate > 0.0, 1.0, 0.0)
            ranks = jnp.dot(named.astype(BF16), earlier, preferred_element_type=F32)
            place_in = jnp.where(named > 0.5, ranks, -1.0)[0:1]
            hit = jnp.where(slot == place_in, 1.0, 0.0)
            pick = hit.astype(BF16)
            picks[index * 2 + j] = pick
            weight = jnp.sum(hit * gate[0:1], axis=1, keepdims=True)
            chosen = jnp.dot(
                pick, out_here[index // 2, index % 2, j], preferred_element_type=F32
            )
            parts.append(chosen * (RESIDUAL * weight))
        start = pl.multiple_of(index * (2 * CAP), 2 * CAP)
        back[pl.ds(start, 2 * CAP), :] = jnp.concatenate(parts, axis=0).astype(BF16)
        return carry

    lax.fori_loop(0, 4, two, 0)
    blocks.forward()
    lax.fori_loop(4, 8, two, 0)
    gate = own_gates[:, 0, :]
    named = jnp.where(gate > 0.0, 1.0, 0.0)
    ranks = jnp.dot(named.astype(BF16), earlier, preferred_element_type=F32)
    places = jnp.where(named > 0.5, ranks, -1.0).T
    gate_columns = gate.T * RESIDUAL
    lane = lax.broadcasted_iota(jnp.int32, (TOK, CAP), 1).astype(F32)
    for e in range(EXPERTS):
        hit = jnp.where(lane == places[:, e : e + 1], 1.0, 0.0)
        hits[e] = hit.astype(BF16)
        shares[e] = (hit * gate_columns[:, e : e + 1]).astype(BF16)
    for index, (source, target) in enumerate(
        ((picks, picks_out), (back, back_out), (hits, hits_out), (shares, shares_out))
    ):
        kept.append(pltpu.make_async_copy(source, target, keep.at[8 + index]))
        kept[-1].start()
    blocks.finish()
    for copy in kept:
        copy.wait()
    arrived(weights)
    sender.finish()


def backward_kernel(
    returned, branch_w,
    attended_in, query_in, key_in, value_in, sums_in, normed_in, heads_in, cosine_in, sine_in,
    experts_in, gate_in, rows_in, hits_in, shares_in, middle_in, out_in, tokens_in, gain_rows,
    layer_out, grad_input, pair_dots, heads_four, branch_four, experts_four,
    attended, query, key, value, sums, normed, heads_w, cosine, sine,
    gate_x, rows, hits, shares, middle, out_tokens, own_tokens, returned_all, block, grad_middle,
    experts_own, experts_x, branch_here, blocks_all, output_term, parts,
    arriving, paired, outgoing, incoming, branch_z, branch_out, branch_plane,
    heads, upper_in, lower_in, upper_out, lower_out, upper_plane, lower_plane,
    gains, gains_in, gains_out, gains_plane,
    experts, experts_plane, heads_sum, branch_sum, experts_sum,
    send, recv, local, branch_sends, branch_recvs,
):
    yh, x, z, seq = place()
    yl, core = seq // 2, seq % 2
    dp = yh * 16 + x * 4 + z
    expert = z * 4 + seq
    near = (yh, x, z, (1 - yl) * 2 + core)
    sibling = (yh, x, z, yl * 2 + 1 - core)
    along_x = [(yh, (x + k) % 4, z, seq) for k in (1, 2, 3)]
    along_z = [(yh, x, (z + k) % 4, seq) for k in (1, 2, 3)]
    plane = [((yh + k // 4) % 2, (x + k % 4) % 4, z, seq) for k in range(1, 8)]
    plane_z = [((yh + k // 4) % 2, x, (z + k % 4) % 4, seq) for k in range(1, 8)]
    group = [
        (yh, x, (z + k // 4) % 4, (yl + (k // 2) % 2) % 2 * 2 + (core + k % 2) % 2)
        for k in range(1, 16)
    ]
    owner = seq * 8 + dp // 4
    source_seq = dp // 8
    slot = dp % 4
    here = owner == dp
    span = pl.ds(pl.multiple_of(seq * 256, 256), 256)
    fetched = local_starts(
        [
            (rows_in, rows), (hits_in, hits), (middle_in, middle), (out_in, out_tokens),
            (branch_w.at[:, span], branch_here),
            (attended_in, attended), (query_in, query), (key_in, key), (value_in, value),
            (sums_in, sums), (normed_in, normed), (heads_in, heads_w),
            (cosine_in, cosine), (sine_in, sine),
            (returned.at[expert], returned_all.at[expert]),
            (experts_in.at[:, x], experts_own), (gate_in, gate_x), (shares_in, shares),
            (tokens_in, own_tokens),
        ],
        local,
    )
    barrier = pltpu.get_barrier_semaphore()
    for partner in group + plane + plane_z[4:]:
        pl.semaphore_signal(barrier, inc=1, device_id=partner, device_id_type=BY_ID)
    for k in range(4):
        maker = dp % 8 * 4 + k
        foreign = jnp.logical_or(maker != dp, source_seq != seq)

        @pl.when(foreign)
        def _():
            pl.semaphore_signal(
                barrier,
                inc=1,
                device_id=(maker // 16, maker // 4 % 4, maker % 4, source_seq),
                device_id_type=BY_ID,
            )

    pl.semaphore_wait(barrier, 29 - here.astype(jnp.int32))
    sender = Sender(send, recv)
    circling = [
        sender.start(experts_in.at[pl.ds(1, 2), partner[1]], experts_x.at[k], partner)
        for k, partner in enumerate(along_x)
    ]
    for copy in fetched[:4]:
        copy.wait()
    grad_normed_two = jnp.zeros((TOK, MODEL_WIDTH), F32)
    for e in range(EXPERTS):
        grad_normed_two += jnp.dot(hits[e], rows[e], preferred_element_type=F32)
    gain_first, gain_second = gain_rows[0:1], gain_rows[1:2]
    mid = middle[...]
    factor = lax.rsqrt(jnp.mean(mid * mid, axis=-1, keepdims=True) + EPSILON)
    gain_two = jnp.sum(grad_normed_two * mid * factor, axis=0, keepdims=True)
    scaled = grad_normed_two * gain_second
    mean_term = jnp.mean(scaled * mid, axis=-1, keepdims=True)
    grad_middle[...] = (
        out_tokens[...].astype(F32) + factor * scaled - mid * factor * factor * factor * mean_term
    )
    block[...] = (RESIDUAL * grad_middle[...]).astype(BF16)
    first = [
        sender.start(block, blocks_all.at[yl, core], near),
        sender.start(block, blocks_all.at[yl, core], sibling),
    ]
    blocks_all[yl, core] = block[...]
    arrived(first[:1])
    far = blocks_all.at[1 - yl, core]
    last = sender.start(far, far, sibling)
    row_copies = [
        sender.start(returned.at[partner[2] * 4 + partner[3]], returned_all.at[expert], partner)
        for partner in group
    ]
    for copy in fetched[4:14]:
        copy.wait()
    arrived(first[1:])
    arrived([last])
    branch_all = blocks_all[...].reshape(SEQ_LEN, MODEL_WIDTH)
    output_term[...] = by_rows(attended[...], branch_all).astype(BF16).reshape(8, 2, 16, MODEL_WIDTH)

    def branch_block(place_z):
        left = pl.multiple_of(place_z % 2 * 512, 512)
        return output_term.at[:, place_z // 2, :, pl.ds(left, 512)]

    around = [
        sender.start(branch_block(partner[2]), branch_z.at[k], partner)
        for k, partner in enumerate(along_z)
    ]
    grad_heads = (
        by_columns(branch_all[:, :512], branch_here[0])
        + by_columns(branch_all[:, 512:], branch_here[1])
    ).astype(BF16)
    lane = lax.broadcasted_iota(jnp.int32, (SEQ_LEN, TOK), 1)
    grad_queries, grad_keys, grad_values = [], [], []
    for k in range(2):
        key_head, value_head = key[:, k * 64 : k * 64 + 64], value[:, k * 64 : k * 64 + 64]
        grad_key, grad_value = 0.0, 0.0
        for g in range(2):
            head = k * 2 + g
            query_head = query[:, head * 64 : head * 64 + 64]
            grad_head = grad_heads[:, head * 64 : head * 64 + 64]
            log_sum = jnp.sum(jnp.where(lane == head, sums[...], 0.0), axis=-1, keepdims=True)
            probs = jnp.exp(causal_scores(query_head, key_head) - log_sum)
            grad_probs = by_columns(grad_head, value_head)
            inner = jnp.sum(probs * grad_probs, axis=-1, keepdims=True)
            grad_scores = (probs * (grad_probs - inner)).astype(BF16)
            grad_value += by_rows(probs.astype(BF16), grad_head)
            grad_key += by_rows(grad_scores, query_head)
            grad_queries.append(
                jnp.dot(grad_scores, key_head, preferred_element_type=F32) * (1.0 / HEAD_SIZE)
            )
        grad_keys.append(grad_key * (1.0 / HEAD_SIZE))
        grad_values.append(grad_value)

    def unturn(pair):
        values = jnp.concatenate(pair, axis=1).astype(BF16).astype(F32)
        return (values * cosine[...] - half_turn(values) * sine[...]).astype(BF16)

    projected = jnp.concatenate(
        [
            unturn(grad_queries[:2]),
            unturn(grad_queries[2:]),
            unturn(grad_keys),
            jnp.concatenate(grad_values, axis=1).astype(BF16),
        ],
        axis=1,
    )
    parts[...] = by_columns(projected, heads_w[:, 0:512]).astype(BF16).reshape(2, 2, TOK, MODEL_WIDTH)
    second = [
        sender.start(parts.at[1 - yl, 1 - core], arriving.at[0], sibling),
        sender.start(parts.at[yl, 1 - core], arriving.at[1], sibling),
    ]
    arrived(second[:1])
    outgoing[...] = gather_sums([parts[1 - yl, core], arriving[0]]).astype(BF16)
    third = sender.start(outgoing, incoming, near)
    term = by_rows(normed[...], projected).astype(BF16)
    heads[...] = term.reshape(2, 4, 4, 32, 512)
    upper, lower = pl.ds(0, 16), pl.ds(16, 16)
    heads_first = []
    for k in range(3):
        partner = along_x[k]
        source = heads.at[:, partner[1], :, upper]
        heads_first.append(sender.start(source, upper_in.at[k], partner))
        partner = along_z[k]
        source = heads.at[:, :, partner[2], lower]
        heads_first.append(sender.start(source, lower_in.at[k], partner))
    arrived(around)
    mine = branch_block(z)[...]
    branch_out[...] = gather_sums([mine] + [branch_z[k] for k in range(3)]).astype(BF16)
    across = [
        sender.start(branch_out.at[partner[0] * 4 + partner[1]], branch_plane.at[k], partner)
        for k, partner in enumerate(plane)
    ]
    arrived(second[1:])
    paired[...] = gather_sums([parts[yl, core], arriving[1]])
    arrived([third])
    total = paired[...] + incoming[...].astype(F32)
    fetched[18].wait()
    values = own_tokens[...].astype(F32)
    factor = lax.rsqrt(jnp.mean(values * values, axis=-1, keepdims=True) + EPSILON)
    gain_one = jnp.sum(total * values * factor, axis=0, keepdims=True)
    scaled = total * gain_first
    mean_term = jnp.mean(scaled * values, axis=-1, keepdims=True)
    grad_input[...] = (
        grad_middle[...] + factor * scaled - values * factor * factor * factor * mean_term
    ).astype(BF16)
    gain_terms = jnp.concatenate(
        [gain_one, gain_two, jnp.zeros((TOK - 2, MODEL_WIDTH), F32)], axis=0
    )
    gains[...] = gain_terms.T.astype(BF16).reshape(2, 4, 4, 32, TOK)
    gains_first = [
        sender.start(gains.at[:, partner[1]], gains_in.at[k], partner)
        for k, partner in enumerate(along_x)
    ]
    arrived(heads_first)
    for y in range(2):
        for j in range(4):
            upper_out[y, j] = gather_sums(
                [heads[y, x, j, 0:16]] + [upper_in[k, y, j] for k in range(3)]
            ).astype(BF16)
            lower_out[y, j] = gather_sums(
                [heads[y, j, z, 16:32]] + [lower_in[k, y, j] for k in range(3)]
            ).astype(BF16)
    heads_second = []
    for k in range(7):
        partner = plane_z[k]
        source = upper_out.at[partner[0], partner[2]]
        heads_second.append(sender.start(source, upper_plane.at[k], partner))
        partner = plane[k]
        source = lower_out.at[partner[0], partner[1]]
        heads_second.append(sender.start(source, lower_plane.at[k], partner))
    arrived(gains_first)
    for y in range(2):
        for j in range(4):
            gains_out[y, j] = gather_sums(
                [gains[y, x, j]] + [gains_in[k, y, j] for k in range(3)]
            ).astype(BF16)
    gains_second = [
        sender.start(gains_out.at[partner[0], partner[2]], gains_plane.at[k], partner)
        for k, partner in enumerate(plane_z)
    ]
    arrived(across)
    branch_sum[...] = gather_sums(
        [branch_out[yh * 4 + x]] + [branch_plane[k] for k in range(7)]
    ).astype(BF16)
    place_of = branch_four.at[slot]

    def branch_copy(k):
        return pltpu.make_async_remote_copy(
            src_ref=branch_sum,
            dst_ref=place_of,
            send_sem=branch_sends.at[k],
            recv_sem=branch_recvs.at[slot],
            device_id=(owner // 16, owner // 4 % 4, owner % 4, k),
            device_id_type=BY_ID,
        )

    for k in range(4):
        self_copy = jnp.logical_and(here, seq == k)

        @pl.when(jnp.logical_not(self_copy))
        def _():
            branch_copy(k).start()

        @pl.when(self_copy)
        def _():
            pltpu.make_async_copy(branch_sum, place_of, branch_recvs.at[slot]).start()

    for copy in fetched[15:17]:
        copy.wait()
    arrived(circling)
    for y in range(2):
        for k in range(3):
            if k == 0:
                pieces = [gate_x[j, y] for j in range(3)]
            else:
                pieces = [experts_x[j, k - 1, y] for j in range(3)]
            total = gather_sums([experts_own[k, y]] + pieces).astype(BF16)
            experts[y, :, :, k * 512 : k * 512 + 512] = total.reshape(4, 32, FF)
    experts_second = [
        sender.start(experts.at[partner[0], partner[2]], experts_plane.at[yh, z], partner)
        for partner in plane_z
    ]
    arrived(heads_second)
    heads_sum[0:16, 0:512] = gather_sums(
        [upper_out[yh, z]] + [upper_plane[k] for k in range(7)]
    ).astype(BF16)
    heads_sum[16:32, 0:512] = gather_sums(
        [lower_out[yh, x]] + [lower_plane[k] for k in range(7)]
    ).astype(BF16)
    arrived(gains_second)
    heads_sum[:, 512:640] = gather_sums(
        [gains_out[yh, z]] + [gains_plane[k] for k in range(7)]
    ).astype(BF16)
    heads_shared = [
        sender.start(heads_sum, heads_four.at[yl, core], partner) for partner in (near, sibling)
    ]
    kept = [pltpu.make_async_copy(heads_sum, heads_four.at[yl, core], local.at[19])]
    kept[0].start()
    fetched[14].wait()
    fetched[17].wait()
    arrived(row_copies)
    mixed = middle[...]
    dots = jnp.zeros((TOK, TOK), F32)
    lane = lax.broadcasted_iota(jnp.int32, (TOK, TOK), 1)
    for e in range(EXPERTS):
        mixed += jnp.dot(shares[e], returned_all[e], preferred_element_type=F32)
        found = by_columns(out_tokens[...], returned_all[e]) * hits[e].astype(F32)
        dots = jnp.where(lane == e, jnp.sum(found, axis=-1, keepdims=True), dots)
    layer_out[...] = mixed.astype(BF16)
    pair_dots[...] = dots * RESIDUAL
    arrived(experts_second)
    for j in range(4):

        @pl.when(z == j)
        def _():
            experts_sum[j] = gather_sums([experts[yh, j], experts_plane[1 - yh, j]]).astype(BF16)

        @pl.when(z != j)
        def _():
            experts_sum[j] = gather_sums([experts_plane[0, j], experts_plane[1, j]]).astype(BF16)

    experts_shared = [
        sender.start(experts_sum, experts_four.at[yl, core], partner) for partner in (near, sibling)
    ]
    kept.append(pltpu.make_async_copy(experts_sum, experts_four.at[yl, core], local.at[20]))
    kept[-1].start()
    arrived(heads_shared[:1])
    far = heads_four.at[1 - yl, core]
    ending = [sender.start(far, far, sibling)]
    arrived(experts_shared[:1])
    far = experts_four.at[1 - yl, core]
    ending.append(sender.start(far, far, sibling))
    arrived(heads_shared[1:])
    arrived(experts_shared[1:])
    for copy in kept:
        copy.wait()
    arrived(ending)
    for k in range(4):
        pltpu.make_async_copy(branch_sum, branch_four.at[k], branch_recvs.at[k]).wait()
        self_copy = jnp.logical_and(here, seq == k)

        @pl.when(jnp.logical_not(self_copy))
        def _():
            branch_copy(k).wait_send()

    sender.finish()


def gather_sums(parts):
    total = parts[0].astype(F32)
    for part in parts[1:]:
        total = total + part.astype(F32)
    return total


def unpack_kernel(heads, branch, experts, query, key, value, output, gate, up, down):
    for s in range(4):
        block = heads[s // 2, s % 2].astype(F32)
        query[:, s * 256 : s * 256 + 256] = block[:, :256]
        key[:, s * 128 : s * 128 + 128] = block[:, 256:384]
        value[:, s * 128 : s * 128 + 128] = block[:, 384:512]
        rows, columns = s // 2 * 16, s % 2 * 512
        output[rows : rows + 16, columns : columns + 512] = branch[s].astype(F32)
        for j in range(4):
            block = experts[s // 2, s % 2, j].astype(F32)
            for index, result in enumerate((gate, up, down)):
                result[:, j * 4 + s, :] = block[:, index * 512 : index * 512 + 512]


def expert_kernel(
    rows_all, picks_in, back_in, own_w, weights_all,
    grad_rows, returned_out, expert_grads_out, gate_x,
    picks, back, returned, expert_grads,
    rows_here, weights, outgoing, chosen, active, by_gate, by_up, send, recv, local,
):
    yh, x, z, seq = place()
    expert = z * 4 + seq
    turns = (2, 1, 3, 0)
    offsets = [(turn, k) for turn in turns for k in range(4) if turn + k > 0]
    partners = [(yh, x, (z + turn) % 4, (seq + k) % 4) for turn, k in offsets]
    fetches = local_starts(
        [
            (weights_all.at[:, :, (x + k) % 4], weights.at[:, :, (x + k) % 4])
            for k in (1, 2, 3)
        ]
        + [(own_w, weights.at[:, :, x])]
        + [(rows_all.at[(z + turn) % 4], rows_here.at[turn]) for turn in turns]
        + [(picks_in, picks), (back_in, back)],
        local,
    )
    along_x = [(yh, (x + k) % 4, z, seq) for k in (1, 2, 3)]
    greet(partners + along_x)
    sender = Sender(send, recv)
    for copy in fetches[:4] + fetches[8:]:
        copy.wait()
    gate_w, up_w, down_w = (weights[k].reshape(MODEL_WIDTH, FF) for k in range(3))
    for index, turn in enumerate(turns):
        fetches[4 + index].wait()
        first = (z + turn) % 4 * 4
        rows = jnp.concatenate(
            [
                jnp.dot(picks[first + j], rows_here[turn, j], preferred_element_type=F32)
                for j in range(4)
            ],
            axis=0,
        ).astype(BF16)
        span = pl.ds(index * 288, 288)
        chosen[span, :] = rows
        gate_pre = jnp.dot(rows, gate_w, preferred_element_type=F32)
        up_pre = jnp.dot(rows, up_w, preferred_element_type=F32)
        back_rows = back[pl.ds(pl.multiple_of(first * CAP, 288), 288), :]
        grad_active = jnp.dot(back_rows, down_w, preferred_element_type=F32)
        sigmoid_gate = jax.nn.sigmoid(gate_pre)
        silu = gate_pre * sigmoid_gate
        slope = sigmoid_gate * (1.0 + gate_pre * (1.0 - sigmoid_gate))
        grad_gate = (grad_active * up_pre * slope).astype(BF16)
        grad_up = (grad_active * silu).astype(BF16)
        by_gate[span, :] = grad_gate
        by_up[span, :] = grad_up
        active[span, :] = (silu * up_pre).astype(BF16)
        result = by_columns(grad_gate, gate_w) + by_columns(grad_up, up_w)
        for j in range(4):
            outgoing[first + j] = result[j * CAP : j * CAP + CAP].astype(BF16)
        for partner, offset in zip(partners, offsets):
            if offset[0] == turn:
                block = partner[2] * 4 + partner[3]
                sender.start(outgoing.at[block], grad_rows.at[expert], partner)
    kept = [pltpu.make_async_copy(outgoing.at[expert], grad_rows.at[expert], local.at[10])]
    kept[0].start()
    def grads_of(index, left, right):
        for part in range(2):
            total = by_rows(left[:, part * 512 : part * 512 + 512], right[...])
            expert_grads[index, :, part] = total.astype(BF16).reshape(4, TOK, FF)

    grads_of(0, chosen, by_gate)
    for k, partner in enumerate(along_x):
        sender.start(expert_grads.at[0, partner[1]], gate_x.at[k], partner)
    for index, turn in enumerate(turns):
        first = (z + turn) % 4 * 4
        result = by_columns(active[pl.ds(index * 288, 288), :], down_w)
        for j in range(4):
            returned[first + j] = result[j * CAP : j * CAP + CAP].astype(BF16)
    kept.append(pltpu.make_async_copy(returned, returned_out, local.at[11]))
    kept[-1].start()
    grads_of(1, chosen, by_up)
    for part in range(2):
        total = 0.0
        for index, turn in enumerate(turns):
            start = pl.multiple_of((z + turn) % 4 * 288, 288)
            total += by_rows(
                back[pl.ds(start, 288), pl.ds(part * 512, 512)],
                active[pl.ds(index * 288, 288), :],
            )
        expert_grads[2, :, part] = total.astype(BF16).reshape(4, TOK, FF)
    kept.append(pltpu.make_async_copy(expert_grads, expert_grads_out, local.at[12]))
    kept[-1].start()
    for copy in kept:
        copy.wait()
    arrived(sender.copies)
    sender.finish()


def shards(
    layer_in, norm_one, w_query, key_weight, value_weight, w_output, norm_two,
    w_gate, w_up, w_down, routes, route_gates, cotangent,
):
    key_value_resident = KEY_VALUE_HEADS // 4
    group_width = QUERY_HEADS // KEY_VALUE_HEADS
    head_width = key_value_resident * group_width * HEAD_SIZE
    kv_width = key_value_resident * HEAD_SIZE

    gains = jnp.pad(jnp.stack([norm_one, norm_two], axis=1), ((0, 0), (0, 126)))
    named = (routes[:, :, None] == jnp.arange(EXPERTS, dtype=jnp.int32)).astype(F32)
    gates_sent = jnp.sum(named * route_gates[:, :, None], axis=1).T
    gates_sent = jnp.broadcast_to(gates_sent[:, None, :], (EXPERTS, 8, TOK))

    heads_w, branch_w, tokens_all, weights_here, gates_all = remote_call(
        gather_kernel,
        (
            w_query, key_weight, value_weight, w_output, gains, layer_in,
            w_gate.reshape(512, FF), w_up.reshape(512, FF), w_down.reshape(512, FF), gates_sent,
        ),
        (
            (2, 4, 4, 32, 640),
            (2, 2, 4, 4, 32, 512),
            (2, 2, TOK, MODEL_WIDTH),
            (3, 2, 4, 32, FF),
            jax.ShapeDtypeStruct((EXPERTS, 8, TOK), F32),
        ),
        [
            pltpu.VMEM((32, 640), BF16),
            pltpu.VMEM((3, 512, FF), BF16),
            pltpu.VMEM((4, 3, 32, FF), BF16),
        ],
        37,
        12,
        1,
        "gather_all",
    )
    heads_w = heads_w.reshape(MODEL_WIDTH, 640)
    branch_w = branch_w.reshape(2, MODEL_WIDTH, 512)
    weights_here = weights_here.reshape(3, 2, TOK, FF)

    cosine, sine = jnp.asarray(COSINE), jnp.asarray(SINE)
    hbm, vmem = pl.BlockSpec(memory_space=pltpu.HBM), pl.BlockSpec(memory_space=pltpu.VMEM)
    block = (TOK, MODEL_WIDTH)

    def arrays(*entries):
        return tuple(jax.ShapeDtypeStruct(shape, kind) for shape, kind in entries)

    def buffers(*entries):
        return [pltpu.VMEM(shape, kind) for shape, kind in entries]

    kept_arrays = (
        ((SEQ_LEN, MODEL_WIDTH), BF16),
        ((SEQ_LEN, head_width), BF16),
        ((SEQ_LEN, kv_width), BF16),
        ((SEQ_LEN, kv_width), BF16),
        ((SEQ_LEN, head_width), BF16),
        ((SEQ_LEN, TOK), F32),
        (block, F32),
        ((EXPERTS, CAP, TOK), BF16),
        ((SLOTS, MODEL_WIDTH), BF16),
        ((EXPERTS, TOK, CAP), BF16),
        ((EXPERTS, TOK, CAP), BF16),
    )
    table = ((SEQ_LEN, TOK), F32)
    heads_array = ((MODEL_WIDTH, 640), BF16)
    (
        normed_all, query_all, key_all, value_all, attended, sums, middle, picks, grad_back,
        hits, shares, rows_all, weights_all, gains,
    ) = pl.pallas_call(
        forward_kernel,
        out_shape=arrays(
            *kept_arrays,
            ((4, 2, 2) + block, BF16),
            ((3, 2, 4, TOK, FF), BF16),
            ((8, MODEL_WIDTH), F32),
        ),
        in_specs=[hbm] * 8 + [vmem],
        out_specs=(hbm,) * 13 + (vmem,),
        scratch_shapes=buffers(
            ((4,) + block, BF16),
            heads_array,
            ((2, MODEL_WIDTH, 512), BF16),
            table,
            table,
            ((EXPERTS, 8, TOK), F32),
            ((4, 2, 2) + block, BF16),
            *kept_arrays,
            ((4, TOK, head_width), BF16),
            (block, BF16),
        )
        + [
            pltpu.SemaphoreType.DMA((42,)),
            pltpu.SemaphoreType.DMA((42,)),
            pltpu.SemaphoreType.DMA((7,)),
            pltpu.SemaphoreType.DMA((12,)),
        ],
        compiler_params=pltpu.CompilerParams(
            collective_id=7, has_side_effects=True, vmem_limit_bytes=60 * 2**20
        ),
        name="forward",
    )(
        tokens_all.reshape((4,) + block),
        heads_w,
        branch_w,
        cosine,
        sine,
        gates_all,
        cotangent,
        weights_here,
        gates_sent,
    )
    returned_array = ((EXPERTS, CAP, MODEL_WIDTH), BF16)
    grads_array = ((3, 4, 2, TOK, FF), BF16)
    gate_array = ((3, 2, TOK, FF), BF16)
    grad_rows, returned, expert_grads, gate_x = pl.pallas_call(
        expert_kernel,
        out_shape=arrays(returned_array, returned_array, grads_array, gate_array),
        in_specs=[hbm] * 5,
        out_specs=(hbm,) * 4,
        scratch_shapes=buffers(
            ((EXPERTS, CAP, TOK), BF16), ((SLOTS, MODEL_WIDTH), BF16), returned_array, grads_array
        )
        + [
            pltpu.VMEM((4, 4) + block, BF16),
            pltpu.VMEM((3, 2, 4, TOK, FF), BF16),
            pltpu.VMEM((EXPERTS, CAP, MODEL_WIDTH), BF16),
            pltpu.VMEM((SLOTS, MODEL_WIDTH), BF16),
            pltpu.VMEM((SLOTS, FF), BF16),
            pltpu.VMEM((SLOTS, FF), BF16),
            pltpu.VMEM((SLOTS, FF), BF16),
            pltpu.SemaphoreType.DMA((18,)),
            pltpu.SemaphoreType.DMA((18,)),
            pltpu.SemaphoreType.DMA((13,)),
        ],
        compiler_params=pltpu.CompilerParams(
            collective_id=5, has_side_effects=True, vmem_limit_bytes=60 * 2**20
        ),
        name="experts",
    )(rows_all.reshape((4, 4) + block), picks, grad_back, weights_here, weights_all)
    layer_out, grad_input, pair_dots, heads_four, branch_four, expert_four = pl.pallas_call(
        backward_kernel,
        out_shape=arrays(
            (block, BF16),
            (block, BF16),
            ((TOK, TOK), F32),
            ((2, 2, 32, 640), BF16),
            ((4, 16, 512), BF16),
            ((2, 2, 4, 32, 3 * FF), BF16),
        ),
        in_specs=[hbm] * 19 + [vmem],
        out_specs=(vmem,) * 3 + (hbm,) * 3,
        scratch_shapes=buffers(
            ((SEQ_LEN, head_width), BF16),
            ((SEQ_LEN, head_width), BF16),
            ((SEQ_LEN, kv_width), BF16),
            ((SEQ_LEN, kv_width), BF16),
            table,
            ((SEQ_LEN, MODEL_WIDTH), BF16),
            heads_array,
            table,
            table,
            gate_array,
            returned_array,
            ((EXPERTS, TOK, CAP), BF16),
            ((EXPERTS, TOK, CAP), BF16),
            (block, F32),
            (block, BF16),
            (block, BF16),
            returned_array,
            (block, BF16),
            (block, F32),
            ((3, 2, TOK, FF), BF16),
            ((3, 2, 2, TOK, FF), BF16),
        )
        + [
            pltpu.VMEM((2, 256, 512), BF16),
            pltpu.VMEM((2, 2) + block, BF16),
            pltpu.VMEM((8, 2, 16, MODEL_WIDTH), BF16),
            pltpu.VMEM((2, 2) + block, BF16),
            pltpu.VMEM((2,) + block, BF16),
            pltpu.VMEM(block, F32),
            pltpu.VMEM(block, BF16),
            pltpu.VMEM(block, BF16),
            pltpu.VMEM((3, 8, 16, 512), BF16),
            pltpu.VMEM((8, 16, 512), BF16),
            pltpu.VMEM((7, 16, 512), BF16),
        ]
        + buffers(
            ((2, 4, 4, 32, 512), BF16),
            ((3, 2, 4, 16, 512), BF16),
            ((3, 2, 4, 16, 512), BF16),
            ((2, 4, 16, 512), BF16),
            ((2, 4, 16, 512), BF16),
            ((7, 16, 512), BF16),
            ((7, 16, 512), BF16),
            ((2, 4, 4, 32, TOK), BF16),
            ((3, 2, 4, 32, TOK), BF16),
            ((2, 4, 32, TOK), BF16),
            ((7, 32, TOK), BF16),
            ((2, 4, 32, 3 * FF), BF16),
            ((2, 4, 32, 3 * FF), BF16),
            ((32, 640), BF16),
            ((16, 512), BF16),
            ((4, 32, 3 * FF), BF16),
        )
        + [
            pltpu.SemaphoreType.DMA((77,)),
            pltpu.SemaphoreType.DMA((77,)),
            pltpu.SemaphoreType.DMA((21,)),
            pltpu.SemaphoreType.DMA((4,)),
            pltpu.SemaphoreType.DMA((4,)),
        ],
        compiler_params=pltpu.CompilerParams(
            collective_id=6, has_side_effects=True, vmem_limit_bytes=60 * 2**20
        ),
        name="backward",
    )(
        returned,
        branch_w,
        attended,
        query_all,
        key_all,
        value_all,
        sums,
        normed_all,
        heads_w,
        cosine,
        sine,
        expert_grads,
        gate_x,
        grad_rows,
        hits,
        shares,
        middle,
        cotangent,
        layer_in,
        gains,
    )
    grad_gates = jnp.sum(named * pair_dots[:, None, :EXPERTS], axis=-1)
    gain_sums = jnp.sum(heads_four[:, :, :, 512:514].astype(F32), axis=(0, 1))
    projections = pl.pallas_call(
        unpack_kernel,
        out_shape=tuple(
            jax.ShapeDtypeStruct(shape, F32)
            for shape in ((32, 1024), (32, 512), (32, 512), (32, 1024)) + ((32, EXPERTS, FF),) * 3
        ),
        in_specs=[vmem] * 3,
        out_specs=(vmem,) * 7,
        compiler_params=pltpu.CompilerParams(vmem_limit_bytes=16 * 2**20),
        name="unpack",
    )(heads_four, branch_four, expert_four)
    experts_out = projections[4:]
    return (
        layer_out,
        grad_input,
        gain_sums[:, 0],
        projections[0],
        projections[1],
        projections[2],
        projections[3],
        gain_sums[:, 1],
        experts_out[0],
        experts_out[1],
        experts_out[2],
        grad_gates,
    )


def solution(mesh):
    dp = ("yh", "x", "z")
    cut = Mesh(mesh.devices.reshape(2, 4, 4, 4), AXES)
    tokens, rows, gain, experts = P(AXES, None), P(dp, None), P(dp), P(dp, None, None)
    return jax.shard_map(
        shards,
        mesh=cut,
        in_specs=(
            tokens, gain, rows, rows, rows, rows, gain, experts, experts, experts,
            tokens, tokens, tokens,
        ),
        out_specs=(
            tokens, tokens, gain, rows, rows, rows, rows, gain, experts, experts, experts, tokens,
        ),
        check_vma=False,
    )
```

time: 261 us -> 217 us (0.83)
  Pallas kernels: 218 us -> 205 us
  other arithmetic: 12.2 us -> 2.8 us
  matrix products: 8.09 us -> 0 us
  starting transfers between devices: 7.18 us -> 0 us
  local copies, waits for them, and re-layouts: 13.7 us -> 8.48 us
    pallas_call x1, Pallas kernels: 52.6 us -> 37.8 us  [remote_call(): pl.pallas_call(kernel, out_shape=tuple((shape if isinstance(shape, jax.Sh...]
    dot_general x8 -> x0, matrix products: 8.09 us -> none  [the longest x2 3.72 us: shards(): jnp.einsum('td,jd->tj', cotangent[:, k * 512:k * 512 + 512], half, prefer...]
    ppermute x6 -> x0, starting transfers between devices: 7.18 us -> none  [the longest x3 4.05 us: shards(): lax.ppermute(piece, 'x', [(i, (i + k) % 4) for i in range(4)])]
    convert_element_type x3 -> x0, other arithmetic: 4.92 us -> none  [the longest x1 2.87 us: shards(): expert_grads = (x_parts[0].astype(F32) + x_parts[1].astype(F32) + x_parts...]
    unnamed x59 -> x12, local copies, waits for them, and re-layouts: 1.72 us -> 5.54 us
    pallas_call x1, Pallas kernels: 40.5 us -> 44.3 us  [shards(): pl.pallas_call(forward_kernel, out_shape=arrays(*kept_arrays, ((4, 2, 2)...]
    squeeze x1 -> x0, local copies, waits for them, and re-layouts: 3.36 us -> none  [shards(): lax.dynamic_index_in_dim(expert_grads, (x_place + k) % 4, 0, keepdims=False)]
    concatenate x2 -> x0, other arithmetic: 3.1 us -> none  [the longest x1 2.48 us: shards(): jnp.concatenate([heads_term, gain_terms], axis=1).reshape(32, 32, 640)]
  transfers between devices with their start and end apart: 6 -> 0, of which waited for: 0 -> 0; matrix products, arithmetic and copies ran while one was open for 3% -> 0% of each run, Pallas kernels for 32% -> 0%
where the time goes in v4:
time: 217 us
  Pallas kernels  205 us (94%)
  local copies, waits for them, and re-layouts  8.48 us (4%)
  other arithmetic  2.8 us (1%)
    pallas_call x1, Pallas kernels, shards(): pl.pallas_call(backward_kernel, out_shape=arrays((block, BF16), (block, B...  83.7 us
    pallas_call x1, Pallas kernels, shards(): pl.pallas_call(forward_kernel, out_shape=arrays(*kept_arrays, ((4, 2, 2)...  44.3 us
    pallas_call x1, Pallas kernels, remote_call(): pl.pallas_call(kernel, out_shape=tuple((shape if isinstance(shape, jax.Sh...  37.8 us
    pallas_call x1, Pallas kernels, shards(): pl.pallas_call(expert_kernel, out_shape=arrays(returned_array, returned_a...  36.2 us
    unnamed x12, local copies, waits for them, and re-layouts  5.54 us

profile of v4, /device:TPU:1, one launch (start us, length us, event | category | flops | bytes accessed | tf_op | source)
XLA Modules:
  0.0 216.5 jit_solution(8292908216359857448)
XLA Ops:
  0.6 0.7 pad_maximum_fusion
  1.3 0.1 copy.37
  1.4 0.6 pad.4.gains
  2.0 0.7 select_reduce_fusion.1
  2.8 0.6 broadcast_in_dim.2.gates.own_gates
  3.4 37.8 %gather_all.1 = (bf16[2,4,4,32,640]{4,3,2,1,0:T(8,128)(2,1)}, bf16[2,2,4,4,32,512]{5,4,3,2,1,0:T(8,128)(2,1)}, bf16[2,2,128,1024]{3,2,1,0:T(8,128)(2,1)}, bf16[3...) custom-call(bf16[32,1024]{1,0:T(8,128)(2,1)} %w_query.1, bf16[32,512]{1,0:T(8,128)(2,1)} %key_weight.1, ...), custom_call_target="tpu_custom_call" | custom-call | tf_op jit(solution)/shard_map/gather_all/pallas_call | solution.py:78
  41.2 44.3 %forward.1 = (bf16[512,1024]{1,0:T(8,128)(2,1)}, bf16[512,256]{1,0:T(8,128)(2,1)}, bf16[512,128]{1,0:T(8,128)(2,1)}, bf16[512,128]{1,0:T(8,128)(2,1)}, bf16[512,...) custom-call(bf16[4,128,1024]{2,1,0:T(8,128)(2,1)} %bitcast.19, ...), custom_call_target="tpu_custom_call" | custom-call | tf_op jit(solution)/shard_map/forward/pallas_call | solution.py:928
  85.5 36.2 %experts.1 = (bf16[16,72,1024]{2,1,0:T(8,128)(2,1)}, bf16[16,72,1024]{2,1,0:T(8,128)(2,1)}, bf16[3,4,2,128,512]{4,3,2,1,0:T(8,128)(2,1)}, bf16[3,2,128,512]{3,2,1,0:T(8,128)(2,1)}) custom-call(bf16[4,4,128,1024]{3,2,1,0:T(8,128)(2,1)} %bitcast.16, bf16[16,72,128]{2,1,0:T(8,128)(2,1)} %get-tuple-element.54.picks_in, ...), custom_call_target="tpu_custom_call" | custom-call | tf_op jit(solution)/shard_map/experts/pallas_call | solution.py:974
  121.7 0.0 copy-start.4
  121.7 83.7 %backward.1 = (bf16[128,1024]{1,0:T(8,128)(2,1)}, bf16[128,1024]{1,0:T(8,128)(2,1)}, f32[128,128]{1,0:T(8,128)}, bf16[2,2,32,640]{3,2,1,0:T(8,128)(2,1)}, bf16[4...) custom-call(bf16[16,72,1024]{2,1,0:T(8,128)(2,1)} %get-tuple-element.57.returned, ...), custom_call_target="tpu_custom_call" | custom-call | tf_op jit(solution)/shard_map/backward/pallas_call | solution.py:999
  205.4 0.9 copy.38
  206.3 0.0 copy-done.4
  206.3 0.6 select_reduce_fusion
  207.0 0.8 convert_reduce_fusion
  207.7 0.7 slice_reduce_fusion
  208.4 0.0 copy-start
  208.4 1.4 copy-done
  209.8 0.0 copy-start.1
  209.8 0.9 copy-done.1
  210.8 0.0 copy-start.2
  210.8 0.8 copy-done.2
  211.6 0.0 copy-start.3
  211.6 2.5 %unpack.1 = (f32[32,1024]{1,0:T(8,128)}, f32[32,512]{1,0:T(8,128)}, f32[32,512]{1,0:T(8,128)}, f32[32,1024]{1,0:T(8,128)}, f32[32,16,512]{2,1,0:T(8,128)}, /*ind...) custom-call(bf16[2,2,32,640]{3,2,1,0:T(8,128)(2,1)S(1)} %copy-done.1, bf16[4,16,512]{2,1,0:T(8,128)(2,1)S(1)} %copy-done.2, ...), custom_call_target="tpu_custom_call" | custom-call | tf_op jit(solution)/shard_map/unpack/pallas_call | solution.py:1100
  214.1 1.7 copy.41
  215.8 0.0 copy-done.3
  215.8 0.7 copy.42
Async XLA Ops:
  121.7 84.6 %copy-start.4 = (s32[128,8]{0,1:T(8,128)S(1)}, s32[128,8]{0,1:T(8,128)}, u32[]{:S(2)}) copy-start(s32[128,8]{0,1:T(8,128)} %param.25) | copy-start | bytes 12292
  208.4 1.4 copy-start
  209.8 0.9 copy-start.1
  210.8 0.8 copy-start.2
  211.6 4.2 %copy-start.3 = (bf16[128,1024]{1,0:T(8,128)(2,1)S(1)}, bf16[128,1024]{1,0:T(8,128)(2,1)}, u32[]{:S(2)}) copy-start(bf16[128,1024]{1,0:T(8,128)(2,1)} %get-tuple-element.99) | copy-start | bytes 786436

commit v5 on v4

--- a/solution.py
+++ b/solution.py
@@ -120,23 +120,36 @@
         self.sibling = (yh, x, z, self.yl * 2 + 1 - self.core)
         self.along_z = [(yh, x, (z + k) % 4, seq) for k in (1, 2, 3)]
         own = blocks_all.at[z, self.yl, self.core]
-        self.to_near = sender.start(block, own, self.near)
-        self.to_z = [sender.start(block, own, partner) for partner in self.along_z]
+        first, second = pl.ds(0, 64), pl.ds(64, 64)
+        self.halves = (first, second)
+        self.near_first = sender.start(block.at[first], own.at[first], self.near)
+        self.z_second = [
+            sender.start(block.at[second], own.at[second], partner) for partner in self.along_z
+        ]
+        self.near_second = sender.start(block.at[second], own.at[second], self.near)
+        self.z_first = [
+            sender.start(block.at[first], own.at[first], partner) for partner in self.along_z
+        ]
         self.to_sibling = [sender.start(block, own, self.sibling)]
 
     def again(self, ref, partner):
         return self.sender.start(ref, ref, partner)
 
     def forward(self):
-        arrived([self.to_near])
+        arrived([self.near_first])
         beside = self.blocks.at[self.z, 1 - self.yl, self.core]
-        self.passed = [self.again(beside.at[pl.ds(0, 64)], partner) for partner in self.along_z]
+        self.passed = [
+            self.again(beside.at[self.halves[0]], partner) for partner in self.along_z
+        ]
+        others = [self.blocks.at[(self.z + 3 - k) % 4, self.yl, self.core] for k in range(3)]
+        for k in range(3):
+            arrived([self.z_second[k]])
+            self.passed.append(self.again(others[k].at[self.halves[1]], self.near))
+        arrived([self.near_second])
         self.to_sibling.append(self.again(beside, self.sibling))
-        for k, copy in enumerate(self.to_z):
-            arrived([copy])
-            block = self.blocks.at[(self.z + 3 - k) % 4, self.yl, self.core]
-            self.passed.append(self.again(block.at[pl.ds(64, 64)], self.near))
-            self.to_sibling.append(self.again(block, self.sibling))
+        for k in range(3):
+            arrived([self.z_first[k]])
+            self.to_sibling.append(self.again(others[k], self.sibling))
 
     def finish(self):
         for k in range(3):
@@ -146,162 +159,175 @@
         arrived(self.to_sibling)
 
 
-def gather_kernel(
-    w_query, key_weight, value_weight, w_output, gains, tokens, w_gate, w_up, w_down, gates,
-    heads_all, branch_all, tokens_all, experts_all, gates_all,
-    heads, weights, experts, send, recv, local,
+class Ring:
+    def __init__(self, sender, here, left, right, own, block_at, half_at):
+        self.sender, self.here, self.left, self.right = sender, here, left, right
+        self.half_at = half_at
+        self.from_left = sender.start(own, block_at(here), right)
+        self.from_right = sender.start(own, block_at(here), left)
+
+    def forward(self):
+        arrived([self.from_left])
+        half = self.half_at(0, (self.here + 3) % 4)
+        self.passed = [self.sender.start(half, half, self.right)]
+        arrived([self.from_right])
+        half = self.half_at(1, (self.here + 1) % 4)
+        self.passed.append(self.sender.start(half, half, self.left))
+
+    def finish(self):
+        arrived(self.passed)
+
+
+class Local:
+    def __init__(self, sems):
+        self.sems, self.used = sems, 0
+
+    def start(self, source, target):
+        copy = pltpu.make_async_copy(source, target, self.sems.at[self.used])
+        copy.start()
+        self.used += 1
+        return copy
+
+
+def finished(copies):
+    for copy in copies:
+        copy.wait()
+
+
+def by_rows(left, right):
+    return lax.dot_general(left, right, (((0,), (0,)), ((), ())), preferred_element_type=F32)
+
+
+def by_columns(left, right):
+    return lax.dot_general(left, right, (((1,), (1,)), ((), ())), preferred_element_type=F32)
+
+
+def half_turn(values):
+    lane = lax.broadcasted_iota(jnp.int32, values.shape, 1)
+    return jnp.where(lane % 64 < 32, pltpu.roll(values, 96, 1), pltpu.roll(values, 32, 1))
+
+
+def causal_scores(query, key):
+    row = lax.broadcasted_iota(jnp.int32, (SEQ_LEN, SEQ_LEN), 0)
+    column = lax.broadcasted_iota(jnp.int32, (SEQ_LEN, SEQ_LEN), 1)
+    return jnp.where(row >= column, by_columns(query, key) * (1.0 / HEAD_SIZE), MASK_VALUE)
+
+
+def forward_kernel(
+    w_query, key_weight, value_weight, w_output, gain_columns, tokens, w_gate, w_up, w_down,
+    cosine_in, sine_in, out_in, own_gates,
+    normed_out, query_out, key_out, value_out, attended_out, sums_out, middle_out, picks_out,
+    back_out, hits_out, shares_out, rows_all, weights_plane, weights_all, heads_out, branch_out,
+    gains,
+    heads_piece, weights_raw, experts, heads_all, branch_all, tokens_all, cosine, sine, gates,
+    out_here,
+    normed, query, key, value, attended, sums, middle, picks, back, hits, shares,
+    traded, rows, send, recv, local_sems,
 ):
     yh, x, z, seq = place()
     yl, core = seq // 2, seq % 2
+    expert = z * 4 + seq
     along_y = (1 - yh, x, z, seq)
     along_x = [(yh, (x + k) % 4, z, seq) for k in (1, 2, 3)]
     along_z = [(yh, x, (z + k) % 4, seq) for k in (1, 2, 3)]
+    beside = [(yh, x, z, (seq + k) % 4) for k in (1, 2, 3)]
     near = (yh, x, z, (1 - yl) * 2 + core)
     sibling = (yh, x, z, yl * 2 + 1 - core)
     group = [
         (yh, x, (z + k // 4) % 4, (yl + (k // 2) % 2) % 2 * 2 + (core + k % 2) % 2)
         for k in range(1, 16)
     ]
-    expert = z * 4 + seq
+    local = Local(local_sems)
     wide = pl.ds(pl.multiple_of(seq * 256, 256), 256)
     narrow = pl.ds(pl.multiple_of(seq * 128, 128), 128)
-    branch = w_output.at[:, pl.ds(pl.multiple_of(core * 512, 512), 512)]
-    built = local_starts(
-        [
-            (w_query.at[:, wide], heads.at[:, pl.ds(0, 256)]),
-            (key_weight.at[:, narrow], heads.at[:, pl.ds(256, 128)]),
-            (value_weight.at[:, narrow], heads.at[:, pl.ds(384, 128)]),
-            (gains, heads.at[:, pl.ds(512, 128)]),
-            (w_gate, weights.at[0]),
-            (w_up, weights.at[1]),
-            (w_down, weights.at[2]),
-        ],
-        local,
-    )
+    branch_piece = w_output.at[:, pl.ds(pl.multiple_of(core * 512, 512), 512)]
+    built = [
+        local.start(w_query.at[:, wide], heads_piece.at[:, pl.ds(0, 256)]),
+        local.start(key_weight.at[:, narrow], heads_piece.at[:, pl.ds(256, 128)]),
+        local.start(value_weight.at[:, narrow], heads_piece.at[:, pl.ds(384, 128)]),
+        local.start(gain_columns, heads_piece.at[:, pl.ds(512, 128)]),
+    ]
+    raw = [
+        local.start(source, weights_raw.at[k]) for k, source in enumerate((w_gate, w_up, w_down))
+    ]
     greet([along_y] + along_x + group)
     sender = Sender(send, recv)
-    for copy in built[:4]:
-        copy.wait()
+    finished(built)
     first = [
-        sender.start(heads, heads_all.at[yh, x, z], along_y),
-        sender.start(branch, branch_all.at[core, yh, x, z], along_y),
+        sender.start(heads_piece, heads_all.at[yh, x, z], along_y),
+        sender.start(branch_piece, branch_all.at[core, yh, x, z], along_y),
     ]
     token_copies = [
         sender.start(tokens, tokens_all.at[yl, core], near),
         sender.start(tokens, tokens_all.at[yl, core], sibling),
     ]
-    own = []
-    for source, target in (
-        (heads, heads_all.at[yh, x, z]),
-        (branch, branch_all.at[core, yh, x, z]),
-        (tokens, tokens_all.at[yl, core]),
-        (gates.at[expert], gates_all.at[expert]),
-    ):
-        own.append(pltpu.make_async_copy(source, target, local.at[7 + len(own)]))
-        own[-1].start()
-    for copy in built[4:]:
-        copy.wait()
+    own_pieces = [
+        local.start(heads_piece, heads_all.at[yh, x, z]),
+        local.start(branch_piece, branch_all.at[core, yh, x, z]),
+    ]
+    own_rest = [
+        local.start(tokens, tokens_all.at[yl, core]),
+        local.start(cosine_in, cosine),
+        local.start(sine_in, sine),
+    ]
+    own_late = [
+        local.start(own_gates.at[expert], gates.at[expert]),
+        local.start(out_in, out_here.at[z, yl, core]),
+    ]
+    finished(raw)
     row = lax.broadcasted_iota(jnp.int32, (TOK, 512), 0)
     column = lax.broadcasted_iota(jnp.int32, (TOK, 512), 1)
     same = jnp.logical_and(column // 16 == row % 32, column % 16 == row // 32 * 4 + seq)
     picker = jnp.where(same, 1.0, 0.0).astype(BF16)
     for k in range(3):
-        picked = jnp.dot(picker, weights[k], preferred_element_type=F32).astype(BF16)
+        picked = jnp.dot(picker, weights_raw[k], preferred_element_type=F32).astype(BF16)
         experts[:, k] = picked.reshape(4, 32, FF)
     expert_first = [
-        sender.start(experts.at[partner[2]], experts_all.at[:, yh, z], partner)
+        sender.start(experts.at[partner[2]], weights_plane.at[:, yh, z], partner)
         for partner in along_z
     ]
-    own.append(pltpu.make_async_copy(experts.at[z], experts_all.at[:, yh, z], local.at[11]))
-    own[-1].start()
-    for copy in own[:2]:
-        copy.wait()
+    own_experts = local.start(experts.at[z], weights_plane.at[:, yh, z])
+    finished(own_pieces)
     arrived(first)
-    second = []
+    heads_second, branch_second = [], []
     for k in range(3):
         source = heads_all.at[:, x, z]
-        second.append(sender.start(source, source, along_z[k]))
+        heads_second.append(sender.start(source, source, along_z[k]))
         source = branch_all.at[core, :, x, z]
-        second.append(sender.start(source, source, along_x[k]))
-    own[4].wait()
+        branch_second.append(sender.start(source, source, along_x[k]))
+    own_experts.wait()
     arrived(expert_first)
-    mine = experts_all.at[:, yh]
-    expert_second = [sender.start(mine, mine, along_y)]
-    arrived(second)
-    third = []
-    for k in range(3):
-        source = heads_all.at[:, x]
-        third.append(sender.start(source, source, along_x[k]))
-        source = branch_all.at[core, :, :, z]
-        third.append(sender.start(source, source, along_z[k]))
+    mine = weights_plane.at[:, yh]
+    expert_second = sender.start(mine, mine, along_y)
+    arrived(heads_second)
+    heads_ring = Ring(
+        sender, x, along_x[2], along_x[0], heads_all.at[:, x],
+        lambda i: heads_all.at[:, i], lambda h, i: heads_all.at[h, i],
+    )
+    arrived(branch_second)
+    source = branch_all.at[core, :, :, z]
+    branch_third = [sender.start(source, source, partner) for partner in along_z]
+    out_blocks = Blocks(sender, out_in, out_here)
     gate_copies = [
-        sender.start(gates.at[partner[2] * 4 + partner[3]], gates_all.at[expert], partner)
+        sender.start(own_gates.at[partner[2] * 4 + partner[3]], gates.at[expert], partner)
         for partner in group
     ]
     arrived(token_copies)
     far = tokens_all.at[1 - yl, core]
-    last = [sender.start(far, far, sibling)]
-    for copy in own[2:4]:
-        copy.wait()
-    arrived(third)
-    half = branch_all.at[core]
-    last.append(sender.start(half, half, sibling))
-    arrived(expert_second)
-    arrived(gate_copies)
-    arrived(last)
-    sender.finish()
-
-
-def by_rows(left, right):
-    return lax.dot_general(left, right, (((0,), (0,)), ((), ())), preferred_element_type=F32)
-
-
-def by_columns(left, right):
-    return lax.dot_general(left, right, (((1,), (1,)), ((), ())), preferred_element_type=F32)
-
-
-def half_turn(values):
-    lane = lax.broadcasted_iota(jnp.int32, values.shape, 1)
-    return jnp.where(lane % 64 < 32, pltpu.roll(values, 96, 1), pltpu.roll(values, 32, 1))
-
-
-def causal_scores(query, key):
-    row = lax.broadcasted_iota(jnp.int32, (SEQ_LEN, SEQ_LEN), 0)
-    column = lax.broadcasted_iota(jnp.int32, (SEQ_LEN, SEQ_LEN), 1)
-    return jnp.where(row >= column, by_columns(query, key) * (1.0 / HEAD_SIZE), MASK_VALUE)
-
-
-def forward_kernel(
-    tokens_in, heads_in, branch_in, cosine_in, sine_in, gates_in, out_in, weights_in, own_gates,
-    normed_out, query_out, key_out, value_out, attended_out, sums_out, middle_out, picks_out,
-    back_out, hits_out, shares_out, rows_all, weights_all, gains,
-    tokens, heads_w, branch_here, cosine, sine, gates, out_here,
-    normed, query, key, value, attended, sums, middle, picks, back, hits, shares,
-    traded, rows, send, recv, fetch, keep,
-):
-    yh, x, z, seq = place()
-    yl, core = seq // 2, seq % 2
-    along_z = [(yh, x, (z + k) % 4, seq) for k in (1, 2, 3)]
-    beside = [(yh, x, z, (seq + k) % 4) for k in (1, 2, 3)]
-    fetched = local_starts(
-        [
-            (heads_in, heads_w), (tokens_in, tokens), (cosine_in, cosine), (sine_in, sine),
-            (branch_in, branch_here), (gates_in, gates), (out_in, out_here.at[z, yl, core]),
-        ],
-        fetch,
-    )
-    along_x = [(yh, (x + k) % 4, z, seq) for k in (1, 2, 3)]
-    greet(along_z + beside + along_x)
-    sender = Sender(send, recv)
-    out_blocks = Blocks(sender, out_in, out_here)
-    weights = [
-        sender.start(weights_in, weights_all.at[:, :, x], partner) for partner in along_x
-    ]
-    for copy in fetched[:4]:
-        copy.wait()
+    far_tokens = sender.start(far, far, sibling)
+    heads_ring.forward()
+    arrived([expert_second])
+    weights_ring = Ring(
+        sender, x, along_x[2], along_x[0], weights_plane,
+        lambda i: weights_all.at[:, :, i], lambda h, i: weights_all.at[:, h, i],
+    )
+    finished(own_rest)
+    arrived([far_tokens])
+    sequence = tokens_all[...].reshape(SEQ_LEN, MODEL_WIDTH).astype(F32)
+    factor = lax.rsqrt(jnp.mean(sequence * sequence, axis=-1, keepdims=True) + EPSILON)
+    heads_ring.finish()
+    heads_w = heads_all[...].reshape(MODEL_WIDTH, 640)
     gains[...] = heads_w[:, 512:640].astype(F32).T[0:8]
-    sequence = tokens[...].reshape(SEQ_LEN, MODEL_WIDTH).astype(F32)
-    factor = lax.rsqrt(jnp.mean(sequence * sequence, axis=-1, keepdims=True) + EPSILON)
     normed[...] = (sequence * factor * gains[0:1]).astype(BF16)
     projected = jnp.dot(normed[...], heads_w[:, 0:512], preferred_element_type=F32)
     for k in range(2):
@@ -329,38 +355,46 @@
         attended[:, k * 128 : k * 128 + 128] = jnp.concatenate(results, axis=1).astype(BF16)
     sums[...] = all_sums
 
+    arrived(branch_third)
+    half = branch_all.at[core]
+    branch_half = sender.start(half, half, sibling)
     trades = []
     for partner in beside:
         start = pl.multiple_of(partner[3] * TOK, TOK)
         trades.append(sender.start(attended.at[pl.ds(start, TOK)], traded.at[seq], partner))
     traded[seq] = attended[pl.ds(pl.multiple_of(seq * TOK, TOK), TOK), :]
     out_blocks.forward()
-    kept = local_starts(
-        [
+    kept = [
+        local.start(source, target)
+        for source, target in (
             (normed, normed_out), (query, query_out), (key, key_out), (value, value_out),
-            (attended, attended_out), (sums, sums_out),
-        ],
-        keep,
-    )
-    fetched[4].wait()
+            (attended, attended_out), (sums, sums_out), (heads_all, heads_out),
+        )
+    ]
+    arrived([branch_half])
+    kept.append(local.start(branch_all, branch_out))
     arrived(trades)
     here = jnp.concatenate([traded[k] for k in range(4)], axis=1)
     branch = jnp.concatenate(
-        [jnp.dot(here, branch_here[k], preferred_element_type=F32) for k in range(2)], axis=1
-    )
-    mid = tokens[seq].astype(F32) + RESIDUAL * branch
+        [
+            jnp.dot(
+                here, branch_all[k].reshape(MODEL_WIDTH, 512), preferred_element_type=F32
+            )
+            for k in range(2)
+        ],
+        axis=1,
+    )
+    mid = tokens_all[yl, core].astype(F32) + RESIDUAL * branch
     middle[...] = mid
     factor = lax.rsqrt(jnp.mean(mid * mid, axis=-1, keepdims=True) + EPSILON)
     rows[...] = (mid * factor * gains[1:2]).astype(BF16)
 
     blocks = Blocks(sender, rows, rows_all)
-    for index, (source, target) in enumerate(
-        ((rows, rows_all.at[z, yl, core]), (middle, middle_out))
-    ):
-        kept.append(pltpu.make_async_copy(source, target, keep.at[6 + index]))
-        kept[-1].start()
-    for copy in fetched[5:]:
-        copy.wait()
+    weights_ring.forward()
+    kept.append(local.start(rows, rows_all.at[z, yl, core]))
+    kept.append(local.start(middle, middle_out))
+    finished(own_late)
+    arrived(gate_copies)
     out_blocks.finish()
     row = lax.broadcasted_iota(jnp.int32, (TOK, TOK), 0)
     column = lax.broadcasted_iota(jnp.int32, (TOK, TOK), 1)
@@ -399,15 +433,14 @@
         hit = jnp.where(lane == places[:, e : e + 1], 1.0, 0.0)
         hits[e] = hit.astype(BF16)
         shares[e] = (hit * gate_columns[:, e : e + 1]).astype(BF16)
-    for index, (source, target) in enumerate(
-        ((picks, picks_out), (back, back_out), (hits, hits_out), (shares, shares_out))
+    for source, target in (
+        (picks, picks_out), (back, back_out), (hits, hits_out), (shares, shares_out)
     ):
-        kept.append(pltpu.make_async_copy(source, target, keep.at[8 + index]))
-        kept[-1].start()
+        kept.append(local.start(source, target))
     blocks.finish()
     for copy in kept:
         copy.wait()
-    arrived(weights)
+    weights_ring.finish()
     sender.finish()
 
 
@@ -479,6 +512,11 @@
         sender.start(experts_in.at[pl.ds(1, 2), partner[1]], experts_x.at[k], partner)
         for k, partner in enumerate(along_x)
     ]
+    def send_rows(partner):
+        block_index = partner[2] * 4 + partner[3]
+        return sender.start(returned.at[block_index], returned_all.at[expert], partner)
+
+    row_copies = [send_rows(group[k - 1]) for k in range(1, 16) if (k // 2) % 2 == 0]
     for copy in fetched[:4]:
         copy.wait()
     grad_normed_two = jnp.zeros((TOK, MODEL_WIDTH), F32)
@@ -498,14 +536,11 @@
         sender.start(block, blocks_all.at[yl, core], near),
         sender.start(block, blocks_all.at[yl, core], sibling),
     ]
+    row_copies += [send_rows(group[k - 1]) for k in range(1, 16) if (k // 2) % 2 == 1]
     blocks_all[yl, core] = block[...]
     arrived(first[:1])
     far = blocks_all.at[1 - yl, core]
     last = sender.start(far, far, sibling)
-    row_copies = [
-        sender.start(returned.at[partner[2] * 4 + partner[3]], returned_all.at[expert], partner)
-        for partner in group
-    ]
     for copy in fetched[4:14]:
         copy.wait()
     arrived(first[1:])
@@ -579,6 +614,21 @@
         partner = along_z[k]
         source = heads.at[:, :, partner[2], lower]
         heads_first.append(sender.start(source, lower_in.at[k], partner))
+    for copy in fetched[15:17]:
+        copy.wait()
+    arrived(circling)
+    for y in range(2):
+        for k in range(3):
+            if k == 0:
+                pieces = [gate_x[j, y] for j in range(3)]
+            else:
+                pieces = [experts_x[j, k - 1, y] for j in range(3)]
+            total = gather_sums([experts_own[k, y]] + pieces).astype(BF16)
+            experts[y, :, :, k * 512 : k * 512 + 512] = total.reshape(4, 32, FF)
+    experts_second = [
+        sender.start(experts.at[partner[0], partner[2]], experts_plane.at[yh, z], partner)
+        for partner in plane_z
+    ]
     arrived(around)
     mine = branch_block(z)[...]
     branch_out[...] = gather_sums([mine] + [branch_z[k] for k in range(3)]).astype(BF16)
@@ -661,21 +711,22 @@
         def _():
             pltpu.make_async_copy(branch_sum, place_of, branch_recvs.at[slot]).start()
 
-    for copy in fetched[15:17]:
-        copy.wait()
-    arrived(circling)
-    for y in range(2):
-        for k in range(3):
-            if k == 0:
-                pieces = [gate_x[j, y] for j in range(3)]
-            else:
-                pieces = [experts_x[j, k - 1, y] for j in range(3)]
-            total = gather_sums([experts_own[k, y]] + pieces).astype(BF16)
-            experts[y, :, :, k * 512 : k * 512 + 512] = total.reshape(4, 32, FF)
-    experts_second = [
-        sender.start(experts.at[partner[0], partner[2]], experts_plane.at[yh, z], partner)
-        for partner in plane_z
-    ]
+    arrived(experts_second)
+    for j in range(4):
+
+        @pl.when(z == j)
+        def _():
+            experts_sum[j] = gather_sums([experts[yh, j], experts_plane[1 - yh, j]]).astype(BF16)
+
+        @pl.when(z != j)
+        def _():
+            experts_sum[j] = gather_sums([experts_plane[0, j], experts_plane[1, j]]).astype(BF16)
+
+    experts_shared = [
+        sender.start(experts_sum, experts_four.at[yl, core], partner) for partner in (near, sibling)
+    ]
+    kept = [pltpu.make_async_copy(experts_sum, experts_four.at[yl, core], local.at[20])]
+    kept[0].start()
     arrived(heads_second)
     heads_sum[0:16, 0:512] = gather_sums(
         [upper_out[yh, z]] + [upper_plane[k] for k in range(7)]
@@ -690,8 +741,8 @@
     heads_shared = [
         sender.start(heads_sum, heads_four.at[yl, core], partner) for partner in (near, sibling)
     ]
-    kept = [pltpu.make_async_copy(heads_sum, heads_four.at[yl, core], local.at[19])]
-    kept[0].start()
+    kept.append(pltpu.make_async_copy(heads_sum, heads_four.at[yl, core], local.at[19]))
+    kept[-1].start()
     fetched[14].wait()
     fetched[17].wait()
     arrived(row_copies)
@@ -704,22 +755,6 @@
         dots = jnp.where(lane == e, jnp.sum(found, axis=-1, keepdims=True), dots)
     layer_out[...] = mixed.astype(BF16)
     pair_dots[...] = dots * RESIDUAL
-    arrived(experts_second)
-    for j in range(4):
-
-        @pl.when(z == j)
-        def _():
-            experts_sum[j] = gather_sums([experts[yh, j], experts_plane[1 - yh, j]]).astype(BF16)
-
-        @pl.when(z != j)
-        def _():
-            experts_sum[j] = gather_sums([experts_plane[0, j], experts_plane[1, j]]).astype(BF16)
-
-    experts_shared = [
-        sender.start(experts_sum, experts_four.at[yl, core], partner) for partner in (near, sibling)
-    ]
-    kept.append(pltpu.make_async_copy(experts_sum, experts_four.at[yl, core], local.at[20]))
-    kept[-1].start()
     arrived(heads_shared[:1])
     far = heads_four.at[1 - yl, core]
     ending = [sender.start(far, far, sibling)]
@@ -749,18 +784,46 @@
     return total
 
 
-def unpack_kernel(heads, branch, experts, query, key, value, output, gate, up, down):
+def unpack_kernel(
+    heads_in, branch_in, experts_in, layer_in, grad_in, dots_in, routes,
+    query, key, value, output, gate, up, down, layer_out, grad_input, gates, gain_one, gain_two,
+    heads, branch, experts, dots, local,
+):
+    copies = local_starts(
+        [
+            (heads_in, heads), (branch_in, branch), (dots_in, dots),
+            (layer_in, layer_out), (grad_in, grad_input),
+        ]
+        + [(experts_in.at[s // 2, s % 2], experts.at[s]) for s in range(4)],
+        local,
+    )
+    for copy in copies[:3]:
+        copy.wait()
+    gains = jnp.zeros((32, TOK), F32)
     for s in range(4):
         block = heads[s // 2, s % 2].astype(F32)
         query[:, s * 256 : s * 256 + 256] = block[:, :256]
         key[:, s * 128 : s * 128 + 128] = block[:, 256:384]
         value[:, s * 128 : s * 128 + 128] = block[:, 384:512]
+        gains += block[:, 512:640]
         rows, columns = s // 2 * 16, s % 2 * 512
         output[rows : rows + 16, columns : columns + 512] = branch[s].astype(F32)
+    gains = gains.T
+    gain_one[...] = gains[0:1]
+    gain_two[...] = gains[1:2]
+    by_expert = dots[...].T[0:EXPERTS]
+    index = lax.broadcasted_iota(jnp.int32, (EXPERTS, TOK), 0)
+    for k in range(TOP):
+        picked = jnp.where(index == routes[k : k + 1, :], by_expert, 0.0)
+        gates[k : k + 1, :] = jnp.sum(picked, axis=0, keepdims=True)
+    for s in range(4):
+        copies[5 + s].wait()
         for j in range(4):
-            block = experts[s // 2, s % 2, j].astype(F32)
+            block = experts[s, j].astype(F32)
             for index, result in enumerate((gate, up, down)):
                 result[:, j * 4 + s, :] = block[:, index * 512 : index * 512 + 512]
+    for copy in copies[3:5]:
+        copy.wait()
 
 
 def expert_kernel(
@@ -870,33 +933,6 @@
     gates_sent = jnp.sum(named * route_gates[:, :, None], axis=1).T
     gates_sent = jnp.broadcast_to(gates_sent[:, None, :], (EXPERTS, 8, TOK))
 
-    heads_w, branch_w, tokens_all, weights_here, gates_all = remote_call(
-        gather_kernel,
-        (
-            w_query, key_weight, value_weight, w_output, gains, layer_in,
-            w_gate.reshape(512, FF), w_up.reshape(512, FF), w_down.reshape(512, FF), gates_sent,
-        ),
-        (
-            (2, 4, 4, 32, 640),
-            (2, 2, 4, 4, 32, 512),
-            (2, 2, TOK, MODEL_WIDTH),
-            (3, 2, 4, 32, FF),
-            jax.ShapeDtypeStruct((EXPERTS, 8, TOK), F32),
-        ),
-        [
-            pltpu.VMEM((32, 640), BF16),
-            pltpu.VMEM((3, 512, FF), BF16),
-            pltpu.VMEM((4, 3, 32, FF), BF16),
-        ],
-        37,
-        12,
-        1,
-        "gather_all",
-    )
-    heads_w = heads_w.reshape(MODEL_WIDTH, 640)
-    branch_w = branch_w.reshape(2, MODEL_WIDTH, 512)
-    weights_here = weights_here.reshape(3, 2, TOK, FF)
-
     cosine, sine = jnp.asarray(COSINE), jnp.asarray(SINE)
     hbm, vmem = pl.BlockSpec(memory_space=pltpu.HBM), pl.BlockSpec(memory_space=pltpu.VMEM)
     block = (TOK, MODEL_WIDTH)
@@ -924,21 +960,27 @@
     heads_array = ((MODEL_WIDTH, 640), BF16)
     (
         normed_all, query_all, key_all, value_all, attended, sums, middle, picks, grad_back,
-        hits, shares, rows_all, weights_all, gains,
+        hits, shares, rows_all, weights_here, weights_all, heads_w, branch_w, gains,
     ) = pl.pallas_call(
         forward_kernel,
         out_shape=arrays(
             *kept_arrays,
             ((4, 2, 2) + block, BF16),
-            ((3, 2, 4, TOK, FF), BF16),
+            ((3, 2, 4, 32, FF), BF16),
+            ((3, 2, 4, 4, 32, FF), BF16),
+            ((2, 4, 4, 32, 640), BF16),
+            ((2, 2, 4, 4, 32, 512), BF16),
             ((8, MODEL_WIDTH), F32),
         ),
-        in_specs=[hbm] * 8 + [vmem],
-        out_specs=(hbm,) * 13 + (vmem,),
+        in_specs=[hbm] * 12 + [vmem],
+        out_specs=(hbm,) * 16 + (vmem,),
         scratch_shapes=buffers(
-            ((4,) + block, BF16),
-            heads_array,
-            ((2, MODEL_WIDTH, 512), BF16),
+            ((32, 640), BF16),
+            ((3, 512, FF), BF16),
+            ((4, 3, 32, FF), BF16),
+            ((2, 4, 4, 32, 640), BF16),
+            ((2, 2, 4, 4, 32, 512), BF16),
+            ((2, 2) + block, BF16),
             table,
             table,
             ((EXPERTS, 8, TOK), F32),
@@ -948,26 +990,34 @@
             (block, BF16),
         )
         + [
-            pltpu.SemaphoreType.DMA((42,)),
-            pltpu.SemaphoreType.DMA((42,)),
-            pltpu.SemaphoreType.DMA((7,)),
-            pltpu.SemaphoreType.DMA((12,)),
+            pltpu.SemaphoreType.DMA((89,)),
+            pltpu.SemaphoreType.DMA((89,)),
+            pltpu.SemaphoreType.DMA((29,)),
         ],
         compiler_params=pltpu.CompilerParams(
             collective_id=7, has_side_effects=True, vmem_limit_bytes=60 * 2**20
         ),
         name="forward",
     )(
-        tokens_all.reshape((4,) + block),
-        heads_w,
-        branch_w,
+        w_query,
+        key_weight,
+        value_weight,
+        w_output,
+        gains,
+        layer_in,
+        w_gate.reshape(512, FF),
+        w_up.reshape(512, FF),
+        w_down.reshape(512, FF),
         cosine,
         sine,
-        gates_all,
         cotangent,
-        weights_here,
         gates_sent,
     )
+    heads_w = heads_w.reshape(MODEL_WIDTH, 640)
+    branch_w = branch_w.reshape(2, MODEL_WIDTH, 512)
+    weights_here = weights_here.reshape(3, 2, TOK, FF)
+    weights_all = weights_all.reshape(3, 2, 4, TOK, FF)
+
     returned_array = ((EXPERTS, CAP, MODEL_WIDTH), BF16)
     grads_array = ((3, 4, 2, TOK, FF), BF16)
     gate_array = ((3, 2, TOK, FF), BF16)
@@ -1095,33 +1145,51 @@
         layer_in,
         gains,
     )
-    grad_gates = jnp.sum(named * pair_dots[:, None, :EXPERTS], axis=-1)
-    gain_sums = jnp.sum(heads_four[:, :, :, 512:514].astype(F32), axis=(0, 1))
-    projections = pl.pallas_call(
+    (
+        grad_query_proj, grad_key_proj, grad_value_proj, grad_output_proj,
+        grad_gate_proj, grad_up_proj, grad_down_proj, layer_out, grad_input,
+        grad_gates, grad_norm_one, grad_norm_two,
+    ) = pl.pallas_call(
         unpack_kernel,
-        out_shape=tuple(
-            jax.ShapeDtypeStruct(shape, F32)
-            for shape in ((32, 1024), (32, 512), (32, 512), (32, 1024)) + ((32, EXPERTS, FF),) * 3
+        out_shape=arrays(
+            ((32, 1024), F32),
+            ((32, 512), F32),
+            ((32, 512), F32),
+            ((32, 1024), F32),
+            ((32, EXPERTS, FF), F32),
+            ((32, EXPERTS, FF), F32),
+            ((32, EXPERTS, FF), F32),
+            (block, BF16),
+            (block, BF16),
+            ((TOP, TOK), F32),
+            ((1, 32), F32),
+            ((1, 32), F32),
         ),
-        in_specs=[vmem] * 3,
-        out_specs=(vmem,) * 7,
-        compiler_params=pltpu.CompilerParams(vmem_limit_bytes=16 * 2**20),
+        in_specs=[hbm] * 6 + [vmem],
+        out_specs=(vmem,) * 12,
+        scratch_shapes=buffers(
+            ((2, 2, 32, 640), BF16),
+            ((4, 16, 512), BF16),
+            ((4, 4, 32, 3 * FF), BF16),
+            ((TOK, TOK), F32),
+        )
+        + [pltpu.SemaphoreType.DMA((9,))],
+        compiler_params=pltpu.CompilerParams(vmem_limit_bytes=60 * 2**20),
         name="unpack",
-    )(heads_four, branch_four, expert_four)
-    experts_out = projections[4:]
+    )(heads_four, branch_four, expert_four, layer_out, grad_input, pair_dots, routes.T)
     return (
         layer_out,
         grad_input,
-        gain_sums[:, 0],
-        projections[0],
-        projections[1],
-        projections[2],
-        projections[3],
-        gain_sums[:, 1],
-        experts_out[0],
-        experts_out[1],
-        experts_out[2],
-        grad_gates,
+        grad_norm_one.reshape(32),
+        grad_query_proj,
+        grad_key_proj,
+        grad_value_proj,
+        grad_output_proj,
+        grad_norm_two.reshape(32),
+        grad_gate_proj,
+        grad_up_proj,
+        grad_down_proj,
+        grad_gates.T,
     )
 
 

time: 217 us -> 191 us (0.88)
  Pallas kernels: 205 us -> 187 us
  local copies, waits for them, and re-layouts: 8.48 us -> 1.35 us
    pallas_call x2 -> x1, Pallas kernels: 40.4 us -> 4.99 us  [shards(): pl.pallas_call(unpack_kernel, out_shape=arrays(((32, 1024), F32), ((32, 5...]
    pallas_call x1, Pallas kernels: 44.3 us -> 70.3 us  [shards(): pl.pallas_call(forward_kernel, out_shape=arrays(*kept_arrays, ((4, 2, 2)...]
    pallas_call x1, Pallas kernels: 83.7 us -> 76.5 us  [shards(): pl.pallas_call(backward_kernel, out_shape=arrays((block, BF16), (block, B...]
    unnamed x12 -> x0, local copies, waits for them, and re-layouts: 5.54 us -> none
where the time goes in v5:
time: 191 us; the launch traced here: 190 us
  Pallas kernels  187 us (98%)
    pallas_call x1, Pallas kernels, shards(): pl.pallas_call(backward_kernel, out_shape=arrays((block, BF16), (block, B...  76.5 us
    pallas_call x1, Pallas kernels, shards(): pl.pallas_call(forward_kernel, out_shape=arrays(*kept_arrays, ((4, 2, 2)...  70.3 us
    pallas_call x1, Pallas kernels, shards(): pl.pallas_call(expert_kernel, out_shape=arrays(returned_array, returned_a...  35 us
    pallas_call x1, Pallas kernels, shards(): pl.pallas_call(unpack_kernel, out_shape=arrays(((32, 1024), F32), ((32, 5...  4.99 us

profile of v5, /device:TPU:1, one launch (start us, length us, event | category | flops | bytes accessed | tf_op | source)
XLA Modules:
  0.0 190.4 jit_solution(1937342287423031683)
XLA Ops:
  0.6 0.7 pad_maximum_fusion
  1.3 0.1 copy.34
  1.4 0.6 pad.4.gain_columns
  2.0 0.7 select_reduce_fusion
  2.8 0.6 broadcast_in_dim.2.own_gates
  3.4 70.3 %forward.1 = (bf16[512,1024]{1,0:T(8,128)(2,1)}, bf16[512,256]{1,0:T(8,128)(2,1)}, bf16[512,128]{1,0:T(8,128)(2,1)}, bf16[512,128]{1,0:T(8,128)(2,1)}, bf16[512,...) custom-call(bf16[32,1024]{1,0:T(8,128)(2,1)} %w_query.1, ...), custom_call_target="tpu_custom_call" | custom-call | tf_op jit(solution)/shard_map/forward/pallas_call | solution.py:964
  73.7 35.0 %experts.1 = (bf16[16,72,1024]{2,1,0:T(8,128)(2,1)}, bf16[16,72,1024]{2,1,0:T(8,128)(2,1)}, bf16[3,4,2,128,512]{4,3,2,1,0:T(8,128)(2,1)}, bf16[3,2,128,512]{3,2,1,0:T(8,128)(2,1)}) custom-call(bf16[4,4,128,1024]{3,2,1,0:T(8,128)(2,1)} %bitcast.15, bf16[16,72,128]{2,1,0:T(8,128)(2,1)} %get-tuple-element.52.picks_in, ...), custom_call_target="tpu_custom_call" | custom-call | tf_op jit(solution)/shard_map/experts/pallas_call | solution.py:1024
  108.7 76.5 %backward.1 = (bf16[128,1024]{1,0:T(8,128)(2,1)}, bf16[128,1024]{1,0:T(8,128)(2,1)}, f32[128,128]{1,0:T(8,128)}, bf16[2,2,32,640]{3,2,1,0:T(8,128)(2,1)}, bf16[4...) custom-call(bf16[16,72,1024]{2,1,0:T(8,128)(2,1)} %get-tuple-element.56.returned, ...), custom_call_target="tpu_custom_call" | custom-call | tf_op jit(solution)/shard_map/backward/pallas_call | solution.py:1049
  185.2 5.0 %unpack.1 = (f32[32,1024]{1,0:T(8,128)}, f32[32,512]{1,0:T(8,128)}, f32[32,512]{1,0:T(8,128)}, f32[32,1024]{1,0:T(8,128)}, f32[32,16,512]{2,1,0:T(8,128)}, /*ind...) custom-call(bf16[2,2,32,640]{3,2,1,0:T(8,128)(2,1)} %get-tuple-eleme, ...), custom_call_target="tpu_custom_call" | custom-call | tf_op jit(solution)/shard_map/unpack/pallas_call | solution.py:1152

commit v6 on v5

--- a/solution.py
+++ b/solution.py
@@ -207,19 +207,20 @@
     return jnp.where(lane % 64 < 32, pltpu.roll(values, 96, 1), pltpu.roll(values, 32, 1))
 
 
-def causal_scores(query, key):
-    row = lax.broadcasted_iota(jnp.int32, (SEQ_LEN, SEQ_LEN), 0)
-    column = lax.broadcasted_iota(jnp.int32, (SEQ_LEN, SEQ_LEN), 1)
+def causal_scores(query, key, first):
+    shape = (query.shape[0], key.shape[0])
+    row = lax.broadcasted_iota(jnp.int32, shape, 0) + first
+    column = lax.broadcasted_iota(jnp.int32, shape, 1)
     return jnp.where(row >= column, by_columns(query, key) * (1.0 / HEAD_SIZE), MASK_VALUE)
 
 
 def forward_kernel(
-    w_query, key_weight, value_weight, w_output, gain_columns, tokens, w_gate, w_up, w_down,
-    cosine_in, sine_in, out_in, own_gates,
+    w_query, key_weight, value_weight, w_output, tokens, w_gate, w_up, w_down,
+    cosine_in, sine_in, out_in, norm_one, norm_two, routes, route_gates,
     normed_out, query_out, key_out, value_out, attended_out, sums_out, middle_out, picks_out,
     back_out, hits_out, shares_out, rows_all, weights_plane, weights_all, heads_out, branch_out,
     gains,
-    heads_piece, weights_raw, experts, heads_all, branch_all, tokens_all, cosine, sine, gates,
+    own_gates, heads_piece, weights_raw, experts, heads_all, branch_all, tokens_all, cosine, sine, gates,
     out_here,
     normed, query, key, value, attended, sums, middle, picks, back, hits, shares,
     traded, rows, send, recv, local_sems,
@@ -245,11 +246,22 @@
         local.start(w_query.at[:, wide], heads_piece.at[:, pl.ds(0, 256)]),
         local.start(key_weight.at[:, narrow], heads_piece.at[:, pl.ds(256, 128)]),
         local.start(value_weight.at[:, narrow], heads_piece.at[:, pl.ds(384, 128)]),
-        local.start(gain_columns, heads_piece.at[:, pl.ds(512, 128)]),
     ]
     raw = [
         local.start(source, weights_raw.at[k]) for k, source in enumerate((w_gate, w_up, w_down))
     ]
+    gain_rows = jnp.concatenate(
+        [
+            norm_one[...].astype(F32),
+            norm_two[...].astype(F32),
+            jnp.zeros((TOK - 2, 32), F32),
+        ],
+        axis=0,
+    )
+    heads_piece[:, 512:640] = gain_rows.T.astype(BF16)
+    for e in range(EXPERTS):
+        gate = jnp.where(routes[...] == e, route_gates[...], 0.0)
+        own_gates[e] = jnp.broadcast_to(jnp.sum(gate, axis=0, keepdims=True), (8, TOK))
     greet([along_y] + along_x + group)
     sender = Sender(send, recv)
     finished(built)
@@ -345,13 +357,21 @@
         key_head, value_head = key[:, k * 64 : k * 64 + 64], value[:, k * 64 : k * 64 + 64]
         for g in range(2):
             head = k * 2 + g
-            scores = causal_scores(query[:, head * 64 : head * 64 + 64], key_head)
-            top = jnp.max(scores, axis=-1, keepdims=True)
-            exponent = jnp.exp(scores - top)
-            total = jnp.sum(exponent, axis=-1, keepdims=True)
-            probs = (exponent / total).astype(BF16)
-            all_sums = jnp.where(lane == head, top + jnp.log(total), all_sums)
-            results.append(jnp.dot(probs, value_head, preferred_element_type=F32))
+            columns = slice(head * 64, head * 64 + 64)
+            halves, half_sums = [], []
+            for part in range(2):
+                start, keys = part * 256, part * 256 + 256
+                scores = causal_scores(
+                    query[start : start + 256, columns], key_head[:keys], start
+                )
+                top = jnp.max(scores, axis=-1, keepdims=True)
+                exponent = jnp.exp(scores - top)
+                total = jnp.sum(exponent, axis=-1, keepdims=True)
+                probs = (exponent / total).astype(BF16)
+                half_sums.append(top + jnp.log(total))
+                halves.append(jnp.dot(probs, value_head[:keys], preferred_element_type=F32))
+            all_sums = jnp.where(lane == head, jnp.concatenate(half_sums, axis=0), all_sums)
+            results.append(jnp.concatenate(halves, axis=0))
         attended[:, k * 128 : k * 128 + 128] = jnp.concatenate(results, axis=1).astype(BF16)
     sums[...] = all_sums
 
@@ -564,21 +584,38 @@
     grad_queries, grad_keys, grad_values = [], [], []
     for k in range(2):
         key_head, value_head = key[:, k * 64 : k * 64 + 64], value[:, k * 64 : k * 64 + 64]
-        grad_key, grad_value = 0.0, 0.0
+        key_terms, value_terms = ([], []), ([], [])
         for g in range(2):
             head = k * 2 + g
             query_head = query[:, head * 64 : head * 64 + 64]
             grad_head = grad_heads[:, head * 64 : head * 64 + 64]
             log_sum = jnp.sum(jnp.where(lane == head, sums[...], 0.0), axis=-1, keepdims=True)
-            probs = jnp.exp(causal_scores(query_head, key_head) - log_sum)
-            grad_probs = by_columns(grad_head, value_head)
-            inner = jnp.sum(probs * grad_probs, axis=-1, keepdims=True)
-            grad_scores = (probs * (grad_probs - inner)).astype(BF16)
-            grad_value += by_rows(probs.astype(BF16), grad_head)
-            grad_key += by_rows(grad_scores, query_head)
-            grad_queries.append(
-                jnp.dot(grad_scores, key_head, preferred_element_type=F32) * (1.0 / HEAD_SIZE)
+            halves = []
+            for part in range(2):
+                start, keys = part * 256, part * 256 + 256
+                query_part = query_head[start : start + 256]
+                grad_part = grad_head[start : start + 256]
+                scores = causal_scores(query_part, key_head[:keys], start)
+                probs = jnp.exp(scores - log_sum[start : start + 256])
+                grad_probs = by_columns(grad_part, value_head[:keys])
+                inner = jnp.sum(probs * grad_probs, axis=-1, keepdims=True)
+                grad_scores = (probs * (grad_probs - inner)).astype(BF16)
+                value_terms[part].append(by_rows(probs.astype(BF16), grad_part))
+                key_terms[part].append(by_rows(grad_scores, query_part))
+                halves.append(
+                    jnp.dot(grad_scores, key_head[:keys], preferred_element_type=F32)
+                )
+            grad_queries.append(jnp.concatenate(halves, axis=0) * (1.0 / HEAD_SIZE))
+        grad_key, grad_value = (
+            jnp.concatenate(
+                [
+                    terms[0][0] + terms[0][1] + terms[1][0][:256] + terms[1][1][:256],
+                    terms[1][0][256:] + terms[1][1][256:],
+                ],
+                axis=0,
             )
+            for terms in (key_terms, value_terms)
+        )
         grad_keys.append(grad_key * (1.0 / HEAD_SIZE))
         grad_values.append(grad_value)
 
@@ -928,11 +965,6 @@
     head_width = key_value_resident * group_width * HEAD_SIZE
     kv_width = key_value_resident * HEAD_SIZE
 
-    gains = jnp.pad(jnp.stack([norm_one, norm_two], axis=1), ((0, 0), (0, 126)))
-    named = (routes[:, :, None] == jnp.arange(EXPERTS, dtype=jnp.int32)).astype(F32)
-    gates_sent = jnp.sum(named * route_gates[:, :, None], axis=1).T
-    gates_sent = jnp.broadcast_to(gates_sent[:, None, :], (EXPERTS, 8, TOK))
-
     cosine, sine = jnp.asarray(COSINE), jnp.asarray(SINE)
     hbm, vmem = pl.BlockSpec(memory_space=pltpu.HBM), pl.BlockSpec(memory_space=pltpu.VMEM)
     block = (TOK, MODEL_WIDTH)
@@ -972,9 +1004,10 @@
             ((2, 2, 4, 4, 32, 512), BF16),
             ((8, MODEL_WIDTH), F32),
         ),
-        in_specs=[hbm] * 12 + [vmem],
+        in_specs=[hbm] * 11 + [vmem] * 4,
         out_specs=(hbm,) * 16 + (vmem,),
         scratch_shapes=buffers(
+            ((EXPERTS, 8, TOK), F32),
             ((32, 640), BF16),
             ((3, 512, FF), BF16),
             ((4, 3, 32, FF), BF16),
@@ -992,7 +1025,7 @@
         + [
             pltpu.SemaphoreType.DMA((89,)),
             pltpu.SemaphoreType.DMA((89,)),
-            pltpu.SemaphoreType.DMA((29,)),
+            pltpu.SemaphoreType.DMA((28,)),
         ],
         compiler_params=pltpu.CompilerParams(
             collective_id=7, has_side_effects=True, vmem_limit_bytes=60 * 2**20
@@ -1003,7 +1036,6 @@
         key_weight,
         value_weight,
         w_output,
-        gains,
         layer_in,
         w_gate.reshape(512, FF),
         w_up.reshape(512, FF),
@@ -1011,7 +1043,10 @@
         cosine,
         sine,
         cotangent,
-        gates_sent,
+        norm_one.reshape(1, 32),
+        norm_two.reshape(1, 32),
+        routes.T,
+        route_gates.T,
     )
     heads_w = heads_w.reshape(MODEL_WIDTH, 640)
     branch_w = branch_w.reshape(2, MODEL_WIDTH, 512)

time: 191 us -> 188 us (0.984)
  no operation moved by 1% of the time
where the time goes in v6:
time: 188 us
  Pallas kernels  187 us (99%)
    pallas_call x1, Pallas kernels, shards(): pl.pallas_call(backward_kernel, out_shape=arrays((block, BF16), (block, B...  76.8 us
    pallas_call x1, Pallas kernels, shards(): pl.pallas_call(forward_kernel, out_shape=arrays(*kept_arrays, ((4, 2, 2)...  70.5 us
    pallas_call x1, Pallas kernels, shards(): pl.pallas_call(expert_kernel, out_shape=arrays(returned_array, returned_a...  34.8 us
    pallas_call x1, Pallas kernels, shards(): pl.pallas_call(unpack_kernel, out_shape=arrays(((32, 1024), F32), ((32, 5...  4.99 us

profile of v6, /device:TPU:1, one launch (start us, length us, event | category | flops | bytes accessed | tf_op | source)
XLA Modules:
  0.0 187.9 jit_solution(9507231402455742594)
XLA Ops:
  0.6 70.5 %forward.1 = (bf16[512,1024]{1,0:T(8,128)(2,1)}, bf16[512,256]{1,0:T(8,128)(2,1)}, bf16[512,128]{1,0:T(8,128)(2,1)}, bf16[512,128]{1,0:T(8,128)(2,1)}, bf16[512,...) custom-call(bf16[32,1024]{1,0:T(8,128)(2,1)} %w_query.1, ...), custom_call_target="tpu_custom_call" | custom-call | tf_op jit(solution)/shard_map/forward/pallas_call | solution.py:996
  71.1 34.8 %experts.1 = (bf16[16,72,1024]{2,1,0:T(8,128)(2,1)}, bf16[16,72,1024]{2,1,0:T(8,128)(2,1)}, bf16[3,4,2,128,512]{4,3,2,1,0:T(8,128)(2,1)}, bf16[3,2,128,512]{3,2,1,0:T(8,128)(2,1)}) custom-call(bf16[4,4,128,1024]{3,2,1,0:T(8,128)(2,1)} %bitcast.15, bf16[16,72,128]{2,1,0:T(8,128)(2,1)} %get-tuple-element.52.picks_in, ...), custom_call_target="tpu_custom_call" | custom-call | tf_op jit(solution)/shard_map/experts/pallas_call | solution.py:1059
  105.9 76.8 %backward.1 = (bf16[128,1024]{1,0:T(8,128)(2,1)}, bf16[128,1024]{1,0:T(8,128)(2,1)}, f32[128,128]{1,0:T(8,128)}, bf16[2,2,32,640]{3,2,1,0:T(8,128)(2,1)}, bf16[4...) custom-call(bf16[16,72,1024]{2,1,0:T(8,128)(2,1)} %get-tuple-element.56.returned, ...), custom_call_target="tpu_custom_call" | custom-call | tf_op jit(solution)/shard_map/backward/pallas_call | solution.py:1084
  182.7 5.0 %unpack.1 = (f32[32,1024]{1,0:T(8,128)}, f32[32,512]{1,0:T(8,128)}, f32[32,512]{1,0:T(8,128)}, f32[32,1024]{1,0:T(8,128)}, f32[32,16,512]{2,1,0:T(8,128)}, /*ind...) custom-call(bf16[2,2,32,640]{3,2,1,0:T(8,128)(2,1)} %get-tuple-eleme, ...), custom_call_target="tpu_custom_call" | custom-call | tf_op jit(solution)/shard_map/unpack/pallas_call | solution.py:1187
